TPU v7x, 32 devices: a whole 2x2x4 slice. The times are simulated.
32 devices in a mesh: fsdp: 16 (over z, y, x), seq: 2 (over core).
Axes of the slice: x: 2, y: 2, z: 4, core: 2. Of those that a mesh axis runs over, the one named last changes fastest.
Arguments:
- latent: bfloat16 [32, 256, 1408], P('fsdp', 'seq'), may hold values from -6 to 6
- skip_input: bfloat16 [32, 256, 1408], P('fsdp', 'seq'), may hold values from -6 to 6
- condition: bfloat16 [32, 1408], P('fsdp'), may hold values from -6 to 6
- text_encoder_states: bfloat16 [32, 256, 1024], P('fsdp'), may hold values from -6 to 6
- text_lengths: int32 [32], P('fsdp'), may hold values from 64 to 256, as said below
- out_grad: bfloat16 [32, 256, 1408], P('fsdp', 'seq'), may hold values from -6 to 6
- skip_gain: bfloat16 [2816], P('fsdp'), may hold values from 0.099609375 to 1.8984375
- norm_gains: bfloat16 [3, 1408], P(None, 'fsdp'), may hold values from 0.099609375 to 1.8984375
- skip_linear: bfloat16 [2816, 1408], P('fsdp'), may hold values from -0.109375 to 0.109375
- shift_linear: bfloat16 [1408, 1408], P('fsdp'), may hold values from -0.15625 to 0.15625
- self_qkv: bfloat16 [1408, 4224], P('fsdp'), may hold values from -0.15625 to 0.15625
- self_out: bfloat16 [1408, 1408], P('fsdp'), may hold values from -1.25 to 1.25
- cross_query: bfloat16 [1408, 1408], P('fsdp'), may hold values from -0.15625 to 0.15625
- cross_keyval: bfloat16 [1024, 2816], P('fsdp'), may hold values from -0.1875 to 0.1875
- cross_out: bfloat16 [1408, 1408], P('fsdp'), may hold values from -1.25 to 1.25
- mlp_up: bfloat16 [1408, 6144], P('fsdp'), may hold values from -0.15625 to 0.15625
- mlp_down: bfloat16 [6144, 1408], P('fsdp'), may hold values from -0.078125 to 0.078125
- thresholds: float32 [2, 16], replicated, may hold values from 1 to 3
Outputs:
- block_out: bfloat16 [32, 256, 1408], P('fsdp', 'seq')
- grad_latent: float32 [32, 256, 1408], P('fsdp', 'seq')
- grad_skip: float32 [32, 256, 1408], P('fsdp', 'seq')
- grad_condition: float32 [32, 1408], P('fsdp')
- grad_text: float32 [32, 256, 1024], P('fsdp', 'seq')
- grad_skip_gain: float32 [2816], P('fsdp')
- grad_norm_gains: float32 [3, 1408], P(None, 'fsdp')
- grad_skip_linear: float32 [2816, 1408], P('fsdp')
- grad_shift_linear: float32 [1408, 1408], P('fsdp')
- grad_self_qkv: float32 [1408, 4224], P('fsdp')
- grad_self_out: float32 [1408, 1408], P('fsdp')
- grad_cross_query: float32 [1408, 1408], P('fsdp')
- grad_cross_keyval: float32 [1024, 2816], P('fsdp')
- grad_cross_out: float32 [1408, 1408], P('fsdp')
- grad_mlp_up: float32 [1408, 6144], P('fsdp')
- grad_mlp_down: float32 [6144, 1408], P('fsdp')
- clipped_qkv: bfloat16 [1408, 4224], P('fsdp')
- clipped_query: bfloat16 [1408, 1408], P('fsdp')
- clipped_keyval: bfloat16 [1024, 2816], P('fsdp')
- logit_peaks: float32 [2, 16], replicated
Inputs may be any that keep to these rules, and one draw needn't show every extreme that they name: `text_lengths`: number of real text tokens of each sample, the rest padding; some sample has all 256.
All inputs are finite; a program needn't handle non-finite values.
Results may differ from a plain program's by a relative error of at most 0.019.
Values may be sent and summed in bfloat16 or wider, within the bound.
A program may use at most 384 MiB of HBM per device.

v0:
```python
import jax
import jax.numpy as jnp
from jax import lax
from jax.sharding import PartitionSpec as P

HEADS = 16
HD = 88
GRID_W = 32

norm_eps = 1e-06
masked_value = -1e30
bf16 = jnp.bfloat16
f32 = jnp.float32


def layer_norm(values):
    center = values - jnp.mean(values, axis=-1, keepdims=True)
    spread = jnp.mean(center * center, axis=-1, keepdims=True)
    return center * lax.rsqrt(spread + norm_eps)


def rotary_tables(row_pos, col_pos, head_dim):
    quarter = head_dim // 4
    freqs = 10000.0 ** (-jnp.arange(quarter, dtype=f32) / quarter)
    row_angle = row_pos.astype(f32)[:, None] * freqs[None, :]
    col_angle = col_pos.astype(f32)[:, None] * freqs[None, :]
    angles = jnp.stack([row_angle, col_angle], axis=1)
    return (jnp.cos(angles), jnp.sin(angles))


def rotate(values, cosine_table, sine_table):
    rows, tokens, heads, head_dim = values.shape
    quarter = head_dim // 4
    pieces = values.reshape(rows, tokens, heads, 2, 2, quarter)
    former = pieces[..., 0, :]
    latter = pieces[..., 1, :]
    cos_wide = cosine_table[None, :, None, :, :]
    sin_wide = sine_table[None, :, None, :, :]
    turned = jnp.stack(
        [former * cos_wide - latter * sin_wide, latter * cos_wide + former * sin_wide], axis=4
    )
    return turned.reshape(rows, tokens, heads, head_dim)


def gained_norm(values, gain):
    return layer_norm(values) * gain


def gelu_tanh(values):
    return jax.nn.gelu(values, approximate=True)


def dot_plain(left, right):
    return jnp.dot(left, right, preferred_element_type=f32)


def dot_left_t(left, right):
    return lax.dot_general(
        left, right, (((0,), (0,)), ((), ())), preferred_element_type=f32
    )


def dot_right_t(left, right):
    return lax.dot_general(
        left, right, (((1,), (1,)), ((), ())), preferred_element_type=f32
    )


def softmax_back(probs, prob_grad):
    return probs * (prob_grad - jnp.sum(prob_grad * probs, axis=-1, keepdims=True))


class Links:
    def __init__(self, fsdp_count):
        self.count = fsdp_count
        self.inner = fsdp_count // 4
        self.bits = self.inner.bit_length() - 1
        self.low_count = self.inner
        self.me = lax.axis_index("fsdp")
        self.core = lax.axis_index("seq")

    def swap(self, value, mask_first, mask_second):
        pairs = []
        for index in range(self.count):
            pairs.append((2 * index, 2 * (index ^ mask_first)))
            pairs.append((2 * index + 1, 2 * (index ^ mask_second) + 1))
        return lax.ppermute(value, ("fsdp", "seq"), pairs)

    def sibling(self, value):
        return lax.ppermute(value, "seq", [(0, 1), (1, 0)])

    def pick(self, first, second):
        return jnp.where(self.core == 0, first, second)

    def reverse(self, index):
        out = 0
        for bit in range(self.bits):
            out |= ((index >> bit) & 1) << (self.bits - 1 - bit)
        return out

    def masks(self, step):
        return 1 << step, 1 << (self.bits - 1 - step)

    def offset(self, block):
        return (block % 4) * self.inner + block // 4

    def place(self, offset):
        return (offset % self.inner) * 4 + offset // self.inner

    def gather(self, shard):
        half = shard.shape[1] // 2
        mine = self.pick(shard[:, :half], shard[:, half:])
        stack = [mine]
        for k in range(1, 4):
            stack.append(self.swap(mine, k * self.inner, k * self.inner))
        blocks = [jnp.concatenate(stack, axis=0)]
        for step in range(self.bits):
            got = [self.swap(block, *self.masks(step)) for block in blocks]
            blocks = blocks + got
        ordered = []
        for index in range(self.low_count):
            back = self.reverse(index)
            ordered.append(
                blocks[index] if back == index else self.pick(blocks[index], blocks[back])
            )
        own = jnp.concatenate(ordered, axis=0)
        return own, self.sibling(own)

    def scatter(self, own, other):
        rows = own.shape[0]
        whole = (own.astype(f32) + self.sibling(other).astype(f32)).astype(bf16)
        size = rows // self.low_count
        cuts = [whole[index * size : (index + 1) * size] for index in range(self.low_count)]
        blocks = []
        for index in range(self.low_count):
            back = self.reverse(index)
            blocks.append(cuts[index] if back == index else self.pick(cuts[index], cuts[back]))
        for step in reversed(range(self.bits)):
            keep = blocks[: 1 << step]
            send = jnp.concatenate(blocks[1 << step :], axis=0)
            got = self.swap(send, *self.masks(step))
            blocks = [
                (block.astype(f32) + got[at * size : (at + 1) * size].astype(f32)).astype(bf16)
                for at, block in enumerate(keep)
            ]
        last = blocks[0]
        part = size // 4
        total = last[:part].astype(f32)
        for k in range(1, 4):
            got = self.swap(last[k * part : (k + 1) * part], k * self.inner, k * self.inner)
            total = total + got.astype(f32)
        return self.columns(total, self.sibling(total))

    def columns(self, own, other):
        return self.pick(
            jnp.concatenate([own, other], axis=-1), jnp.concatenate([other, own], axis=-1)
        )

    def halves(self, value):
        half = value.shape[-1] // 2
        first, second = value[..., :half], value[..., half:]
        return self.pick(first, second), self.pick(second, first)

    def order_matrix(self, size):
        block = size // self.count
        at = lax.broadcasted_iota(jnp.int32, (size, size), 0)
        to = lax.broadcasted_iota(jnp.int32, (size, size), 1)
        place = to // block
        source = jnp.bitwise_xor(self.me, (place % 4) * self.inner + place // 4)
        return (at == source * block + to % block).astype(bf16)

    def order_blocks(self, value):
        size = value.shape[1] // self.count
        parts = []
        for block in range(self.count):
            source = jnp.bitwise_xor(self.me, self.offset(block))
            parts.append(lax.dynamic_slice_in_dim(value, source * size, size, 1))
        return jnp.concatenate(parts, axis=1)

    def restore_blocks(self, value):
        size = value.shape[1] // self.count
        parts = []
        for shard in range(self.count):
            source = self.place(jnp.bitwise_xor(self.me, shard))
            parts.append(lax.dynamic_slice_in_dim(value, source * size, size, 1))
        return jnp.concatenate(parts, axis=1)

    def small_gather(self, value):
        for bit in range(self.count.bit_length() - 1):
            got = self.swap(value, 1 << bit, 1 << bit)
            upper = (self.me >> bit) & 1
            value = jnp.where(
                upper == 1,
                jnp.concatenate([got, value], axis=0),
                jnp.concatenate([value, got], axis=0),
            )
        return value

    def small_scatter(self, value):
        for bit in reversed(range(self.count.bit_length() - 1)):
            size = value.shape[0] // 2
            upper = (self.me >> bit) & 1
            keep = jnp.where(upper == 1, value[size:], value[:size])
            send = jnp.where(upper == 1, value[:size], value[size:])
            value = keep + self.swap(send, 1 << bit, 1 << bit)
        return value

    def largest(self, value):
        value = jnp.maximum(value, self.sibling(value))
        for bit in range(self.count.bit_length() - 1):
            value = jnp.maximum(value, self.swap(value, 1 << bit, 1 << bit))
        return value


def exact_restore(matrix, value):
    high = value.astype(bf16)
    low = (value - high.astype(f32)).astype(bf16)
    return dot_right_t(high, matrix) + dot_right_t(low, matrix)


def attend(queries, keys, scaling):
    return jnp.einsum("bqhd,bkhd->bhqk", queries, keys, preferred_element_type=f32) * scaling


def mix(probs, values):
    return jnp.einsum("bhqk,bkhd->bqhd", probs, values, preferred_element_type=f32)


def mix_back(probs, grads):
    return jnp.einsum("bhqk,bqhd->bkhd", probs, grads, preferred_element_type=f32)


def local(
    latent,
    skip_input,
    condition,
    text_encoder_states,
    text_lengths,
    out_grad,
    skip_gain,
    norm_gains,
    skip_linear,
    shift_linear,
    self_qkv,
    self_out,
    cross_query,
    cross_keyval,
    cross_out,
    mlp_up,
    mlp_down,
    thresholds,
):
    batch, tokens, width = latent.shape
    rows = batch * tokens
    text_rows = text_encoder_states.shape[1]
    text_width = text_encoder_states.shape[2]
    scaling = HD ** (-0.5)
    links = Links(lax.axis_size("fsdp"))
    me, core = links.me, links.core
    count = links.count

    positions = core * tokens + jnp.arange(tokens)
    cosine_table, sine_table = rotary_tables(positions // GRID_W, positions % GRID_W, HD)

    gain_rows = skip_gain.shape[0]
    third = norm_gains.shape[1]
    packed = links.small_gather(
        jnp.concatenate([skip_gain, norm_gains.reshape(-1)])[None, :]
    )
    skip_gain_all = packed[:, :gain_rows].reshape(-1).astype(f32)
    gains = (
        packed[:, gain_rows:].reshape(count, 3, third).transpose(1, 0, 2).reshape(3, width)
    ).astype(f32)
    cond_act = jax.nn.silu(condition.astype(f32)).astype(bf16)
    cond_all = links.small_gather(cond_act)
    shift_rows = shift_linear.shape[0]
    cond_cut = lax.dynamic_slice_in_dim(cond_all, me * shift_rows, shift_rows, 1)
    shift = links.small_scatter(dot_plain(cond_cut, shift_linear))

    w_skip = links.gather(skip_linear)
    w_qkv = links.gather(self_qkv)
    w_self_out = links.gather(self_out)
    w_query = links.gather(cross_query)
    w_keyval = links.gather(cross_keyval)
    w_cross_out = links.gather(cross_out)
    w_up = links.gather(mlp_up)
    w_down = links.gather(mlp_down)

    order = links.order_matrix(width)
    order_wide = links.order_matrix(2 * width)
    order_text = links.order_matrix(text_width)

    def product(value, weight):
        return links.columns(dot_plain(value, weight[0]), dot_plain(value, weight[1]))

    def product_back(grad_halves, weight):
        return dot_right_t(grad_halves[0], weight[0]) + dot_right_t(grad_halves[1], weight[1])

    def weight_grad(value, grad_halves):
        return links.scatter(
            dot_left_t(value, grad_halves[0]).astype(bf16),
            dot_left_t(value, grad_halves[1]).astype(bf16),
        )

    def reorder(value):
        return dot_plain(value, order).astype(bf16)

    def restore(value):
        return dot_right_t(value.astype(bf16), order).astype(bf16)

    def heads_of(value):
        return value.reshape(batch, -1, HEADS, HD)

    joined = jnp.concatenate(
        [latent.reshape(rows, width), skip_input.reshape(rows, width)], axis=1
    ).astype(f32)
    normed = gained_norm(joined, skip_gain_all).astype(bf16)
    normed = dot_plain(normed, order_wide).astype(bf16)
    hidden = product(normed, w_skip)

    def shifted(values, gain, moved):
        wide = jnp.broadcast_to(moved[:, None, :], (batch, tokens, width)).reshape(rows, width)
        return layer_norm(values) * gain + wide

    attn_in = reorder(shifted(hidden, gains[0], shift).astype(bf16))
    qkv_proj = product(attn_in, w_qkv)
    query_proj = heads_of(qkv_proj[:, :width])
    key_proj = heads_of(qkv_proj[:, width : 2 * width])

    def norm_rotate(values):
        return rotate(layer_norm(values), cosine_table, sine_table)

    queries = norm_rotate(query_proj).astype(bf16)
    keys_here = norm_rotate(key_proj).astype(bf16)
    values_here = heads_of(qkv_proj[:, 2 * width :].astype(bf16))
    keyval_here = jnp.concatenate(
        [keys_here.reshape(rows, width), values_here.reshape(rows, width)], axis=1
    )
    keyval_there = links.sibling(keyval_here)
    keys_all = jnp.concatenate([keys_here, heads_of(keyval_there[:, :width])], axis=1)
    values_all = jnp.concatenate([values_here, heads_of(keyval_there[:, width:])], axis=1)
    scores = attend(queries, keys_all, scaling)
    self_peak = jnp.max(scores, axis=(0, 2, 3))
    probs = jax.nn.softmax(scores, axis=-1)
    mixed = mix(probs.astype(bf16), values_all)
    attn_cat = reorder(mixed.reshape(rows, width).astype(bf16))
    after_self = hidden + product(attn_cat, w_self_out)
    cross_in = reorder(gained_norm(after_self, gains[1]).astype(bf16))
    cq_proj = heads_of(product(cross_in, w_query))
    cross_queries = layer_norm(cq_proj).astype(bf16)

    text = text_encoder_states.reshape(batch * text_rows, text_width)
    text_ordered = dot_plain(text, order_text).astype(bf16)
    ckv_proj = product(text_ordered, w_keyval)
    ckey_proj = heads_of(ckv_proj[:, :width])
    cross_keys = layer_norm(ckey_proj).astype(bf16)
    cross_values = heads_of(ckv_proj[:, width:].astype(bf16))
    text_valid = jnp.arange(text_rows)[None, :] < text_lengths[:, None]
    cross_scores = jnp.where(
        text_valid[:, None, None, :], attend(cross_queries, cross_keys, scaling), masked_value
    )
    cross_peak = jnp.max(cross_scores, axis=(0, 2, 3))
    cross_probs = jax.nn.softmax(cross_scores, axis=-1)
    cross_mixed = mix(cross_probs.astype(bf16), cross_values)
    cross_cat = reorder(cross_mixed.reshape(rows, width).astype(bf16))
    after_cross = after_self + product(cross_cat, w_cross_out)
    mlp_in = reorder(gained_norm(after_cross, gains[2]).astype(bf16))
    upper = product(mlp_in, w_up)
    activated = links.order_blocks(gelu_tanh(upper).astype(bf16))

    down_in = out_grad.reshape(rows, width)
    result_grad = down_in.astype(f32)
    down_halves = links.halves(down_in)
    grad_down = weight_grad(activated, down_halves)
    block_out = (after_cross + product(activated, w_down)).astype(bf16)
    act_grad = links.restore_blocks(product_back(down_halves, w_down))
    upper_grad = jax.vjp(gelu_tanh, upper)[1](act_grad)[0].astype(bf16)
    upper_halves = links.halves(upper_grad)
    grad_up = weight_grad(mlp_in, upper_halves)
    mlp_in_grad = exact_restore(order, product_back(upper_halves, w_up))
    cross_part, gain_third = jax.vjp(gained_norm, after_cross, gains[2])[1](mlp_in_grad)
    cross_grad = result_grad + cross_part
    cross_halves = links.halves(cross_grad.astype(bf16))
    grad_cross_out = weight_grad(cross_cat, cross_halves)
    cmix_grad = heads_of(restore(product_back(cross_halves, w_cross_out)))
    cval_grad = mix_back(cross_probs.astype(bf16), cmix_grad)
    cprob_grad = jnp.einsum("bqhd,bkhd->bhqk", cmix_grad, cross_values, preferred_element_type=f32)
    cscore_grad = softmax_back(cross_probs, cprob_grad).astype(bf16)
    cquery_grad = mix(cscore_grad, cross_keys) * scaling
    ckey_grad = mix_back(cscore_grad, cross_queries) * scaling
    cq_grad = jax.vjp(layer_norm, cq_proj)[1](cquery_grad)[0].reshape(rows, width).astype(bf16)
    cq_halves = links.halves(cq_grad)
    grad_cross_query = weight_grad(cross_in, cq_halves)
    cross_in_grad = exact_restore(order, product_back(cq_halves, w_query))
    self_part, gain_second = jax.vjp(gained_norm, after_self, gains[1])[1](cross_in_grad)
    self_grad = cross_grad + self_part

    text_half = text_rows // 2
    ckeyval = jnp.concatenate(
        [
            ckey_grad.reshape(batch, text_rows, width),
            cval_grad.reshape(batch, text_rows, width),
        ],
        axis=2,
    ).astype(bf16)
    ckeyval_mine = lax.dynamic_slice_in_dim(ckeyval, core * text_half, text_half, 1)
    ckeyval_theirs = lax.dynamic_slice_in_dim(ckeyval, (1 - core) * text_half, text_half, 1)
    ckeyval_sum = ckeyval_mine.astype(f32) + links.sibling(ckeyval_theirs).astype(f32)
    ckey_mine = lax.dynamic_slice_in_dim(ckey_proj, core * text_half, text_half, 1)
    ckey_pre = jax.vjp(layer_norm, ckey_mine)[1](heads_of(ckeyval_sum[..., :width]))[0]
    keyval_grad = jnp.concatenate(
        [ckey_pre.reshape(batch * text_half, width), ckeyval_sum[..., width:].reshape(-1, width)],
        axis=1,
    ).astype(bf16)
    text_mine = lax.dynamic_slice_in_dim(
        text_ordered.reshape(batch, text_rows, text_width), core * text_half, text_half, 1
    ).reshape(-1, text_width)
    keyval_halves = links.halves(keyval_grad)
    grad_keyval = weight_grad(text_mine, keyval_halves)
    grad_text = exact_restore(order_text, product_back(keyval_halves, w_keyval))
    grad_text = grad_text.reshape(batch, text_half, text_width)

    self_halves = links.halves(self_grad.astype(bf16))
    grad_self_out = weight_grad(attn_cat, self_halves)
    mix_grad = heads_of(restore(product_back(self_halves, w_self_out)))
    value_grad = mix_back(probs.astype(bf16), mix_grad)
    prob_grad = jnp.einsum("bqhd,bkhd->bhqk", mix_grad, values_all, preferred_element_type=f32)
    score_grad = softmax_back(probs, prob_grad).astype(bf16)
    query_grad = mix(score_grad, keys_all) * scaling
    key_grad = mix_back(score_grad, queries) * scaling
    there = jnp.concatenate(
        [key_grad[:, tokens:].reshape(rows, width), value_grad[:, tokens:].reshape(rows, width)],
        axis=1,
    ).astype(bf16)
    from_there = links.sibling(there).astype(f32)
    key_here = key_grad[:, :tokens] + heads_of(from_there[:, :width])
    value_here = value_grad[:, :tokens].reshape(rows, width) + from_there[:, width:]
    query_pre = jax.vjp(norm_rotate, query_proj)[1](query_grad)[0]
    key_pre = jax.vjp(norm_rotate, key_proj)[1](key_here)[0]
    qkv_grad = jnp.concatenate(
        [query_pre.reshape(rows, width), key_pre.reshape(rows, width), value_here], axis=1
    ).astype(bf16)
    qkv_halves = links.halves(qkv_grad)
    grad_qkv = weight_grad(attn_in, qkv_halves)
    attn_in_grad = exact_restore(order, product_back(qkv_halves, w_qkv))
    hidden_part, gain_first, shift_grad = jax.vjp(shifted, hidden, gains[0], shift)[1](
        attn_in_grad
    )
    hidden_grad = self_grad + hidden_part
    hidden_halves = links.halves(hidden_grad.astype(bf16))
    grad_skip_linear = weight_grad(normed, hidden_halves)
    normed_grad = exact_restore(order_wide, product_back(hidden_halves, w_skip))
    joined_grad, skip_gain_grad = jax.vjp(gained_norm, joined, skip_gain_all)[1](normed_grad)

    shift_sum = shift_grad + links.sibling(shift_grad)
    shift_all = links.small_gather(shift_sum.astype(bf16))
    grad_shift = dot_left_t(cond_cut, shift_all)
    cond_back = links.small_gather(dot_right_t(shift_all, shift_linear)[None])
    cond_mine = lax.dynamic_slice_in_dim(cond_back, me * batch, batch, 1)
    cond_mine = cond_mine.transpose(1, 0, 2).reshape(batch, width)
    grad_cond = jax.vjp(jax.nn.silu, condition.astype(f32))[1](cond_mine)[0]

    gains_grad = jnp.stack([gain_first, gain_second, gain_third])
    gains_grad = gains_grad.reshape(3, count, third).transpose(1, 0, 2).reshape(count, 3 * third)
    packed_grad = jnp.concatenate([skip_gain_grad.reshape(count, gain_rows), gains_grad], axis=1)
    packed_grad = links.small_scatter(packed_grad)
    packed_grad = (packed_grad + links.sibling(packed_grad))[0]
    grad_skip_gain = packed_grad[:gain_rows]
    grad_gains = packed_grad[gain_rows:].reshape(3, third)

    peaks = links.largest(jnp.stack([self_peak, cross_peak]))
    roots = jnp.sqrt(thresholds / jnp.maximum(peaks, thresholds))
    self_cols = jnp.repeat(roots[0], HD)
    cross_cols = jnp.repeat(roots[1], HD)
    unit_cols = jnp.ones((width,), f32)
    clipped_qkv = (
        self_qkv.astype(f32) * jnp.concatenate([self_cols, self_cols, unit_cols])[None, :]
    ).astype(bf16)
    clipped_query = (cross_query.astype(f32) * cross_cols[None, :]).astype(bf16)
    clipped_keyval = (
        cross_keyval.astype(f32) * jnp.concatenate([cross_cols, unit_cols])[None, :]
    ).astype(bf16)
    return (
        block_out.reshape(batch, tokens, width),
        joined_grad[:, :width].reshape(batch, tokens, width),
        joined_grad[:, width:].reshape(batch, tokens, width),
        grad_cond,
        grad_text,
        grad_skip_gain,
        grad_gains,
        grad_skip_linear,
        grad_shift,
        grad_qkv,
        grad_self_out,
        grad_cross_query,
        grad_keyval,
        grad_cross_out,
        grad_up,
        grad_down,
        clipped_qkv,
        clipped_query,
        clipped_keyval,
        peaks,
    )


def solution(mesh):
    rows = P("fsdp", None)
    tokens = P("fsdp", "seq", None)
    in_specs = (
        tokens,
        tokens,
        rows,
        P("fsdp", None, None),
        P("fsdp"),
        tokens,
        P("fsdp"),
        P(None, "fsdp"),
        *([rows] * 9),
        P(),
    )
    out_specs = (
        *([tokens] * 3),
        rows,
        tokens,
        P("fsdp"),
        P(None, "fsdp"),
        *([rows] * 12),
        P(),
    )
    return jax.shard_map(local, mesh=mesh, in_specs=in_specs, out_specs=out_specs, check_vma=False)
```

profile of v0, /device:TPU:0, one launch (start us, length us, event | category | flops | bytes accessed | tf_op | source)
XLA Modules:
  0.0 1562.1 jit_solution(4821807080840859541)
XLA Ops:
  135.5 8.6 collective-permute-done.16
  148.0 12.2 collective-permute-done.35
  164.1 8.7 collective-permute-start.20
  178.7 21.4 %collective-permute-start.63 = (bf16[384,704]{0,1:T(8,128)(2,1)S(1)}, bf16[384,704]{0,1:T(8,128)(2,1)S(1)}, u32[]{:S(2)}, u32[]{:S(2)}) collective-permute-start(bf16[384,704]{0,1:T(8,128)(2,1)S(1)} %copy-done.126), channel_id=1, source_target_pairs={{0,16},{1,17},{2,18},{3,19},{4,20},{5,21},{6,22},{7,23},{8,24},{9,... | collective-permute-start | bytes 1622024 | tf_op jit(solution)/shard_map/ppermute | solution.py:87
  214.8 10.6 collective-permute-done.55
  227.2 50.8 %collective-permute-done.56 = bf16[88,3072]{1,0:T(8,128)(2,1)S(1)} collective-permute-done((bf16[88,3072]{1,0:T(8,128)(2,1)S(1)}, bf16[88,3072]{1,0:T(8,128)(2,1)S(1)}, u32[]{:S(2)}, u32[]{:S(2)}) %collective-permute-start.56) | collective-permute-done | bytes 540704 | tf_op jit(solution)/shard_map/ppermute | solution.py:87
  296.1 8.6 collective-permute-done.45
  307.1 9.2 collective-permute-done.52
  316.8 15.6 collective-permute-done.51
  339.8 11.1 collective-permute-done.46
  353.7 28.5 %collective-permute-done.53 = bf16[352,704]{0,1:T(8,128)(2,1)} collective-permute-done((bf16[352,704]{0,1:T(8,128)(2,1)S(1)}, bf16[352,704]{0,1:T(8,128)(2,1)}, u32[]{:S(2)}, u32[]{:S(2)}) %collective-permute-start.53) | collective-permute-done | bytes 495648 | tf_op jit(solution)/shard_map/ppermute | solution.py:87
  406.7 15.3 collective-permute-done.39
  442.0 68.6 %collective-permute-done.9 = bf16[704,704]{0,1:T(8,128)(2,1)} collective-permute-done((bf16[704,704]{0,1:T(8,128)(2,1)}, bf16[704,704]{0,1:T(8,128)(2,1)}, u32[]{:S(2)}, u32[]{:S(2)}) %collective-permute-start.9) | collective-permute-done | bytes 991264 | tf_op jit(solution)/shard_map/ppermute | solution.py:87
  547.4 9.1 copy.618
  662.7 11.3 fusion.79
  720.1 8.5 collective-permute-start.144
  844.9 12.6 convolution_bitcast_fusion
  884.5 9.1 copy_dynamic-update-slice_fusion.1
  893.7 9.2 copy_dynamic-update-slice_fusion
  1103.1 10.7 collective-permute-done.107
  1115.3 15.9 %collective-permute-done.121 = bf16[704,704]{0,1:T(8,128)(2,1)S(1)} collective-permute-done((bf16[704,704]{0,1:T(8,128)(2,1)S(1)}, bf16[704,704]{0,1:T(8,128)(2,1)S(1)}, u32[]{:S(2)}, u32[]{:S(2)}) %collective-permute-start.121) | collective-permute-done | bytes 991264 | tf_op jit(solution)/shard_map/ppermute | solution.py:87
  1148.4 10.0 collective-permute-done.103
  1230.3 19.0 %collective-permute-done.86 = bf16[1408,704]{0,1:T(8,128)(2,1)} collective-permute-done((bf16[1408,704]{0,1:T(8,128)(2,1)}, bf16[1408,704]{0,1:T(8,128)(2,1)}, u32[]{:S(2)}, u32[]{:S(2)}) %collective-permute-start.86) | collective-permute-done | bytes 1982496 | tf_op jit(solution)/shard_map/ppermute | solution.py:87
  1254.9 9.3 copy.711
  1286.1 9.3 add_convert_fusion
  1321.1 12.3 collective-permute-start.116
  1352.3 12.2 collective-permute-start.88
  1399.5 10.4 collective-permute-done.128
  1423.4 16.2 %collective-permute-done.136 = bf16[1536,704]{0,1:T(8,128)(2,1)S(1)} collective-permute-done((bf16[1536,704]{0,1:T(8,128)(2,1)S(1)}, bf16[1536,704]{0,1:T(8,128)(2,1)S(1)}, u32[]{:S(2)}, u32[]{:S(2)}) %collective-permute-start.136) | collective-permute-done | bytes 2162720 | tf_op jit(solution)/shard_map/ppermute | solution.py:87
  1444.0 18.7 %collective-permute-done.129 = bf16[352,3072]{1,0:T(8,128)(2,1)S(1)} collective-permute-done((bf16[352,3072]{1,0:T(8,128)(2,1)S(1)}, bf16[352,3072]{1,0:T(8,128)(2,1)S(1)}, u32[]{:S(2)}, u32[]{:S(2)}) %collective-permute-start.129) | collective-permute-done | bytes 2162720 | tf_op jit(solution)/shard_map/ppermute | solution.py:87
  1470.8 27.6 %collective-permute-start.137 = (bf16[384,704]{0,1:T(8,128)(2,1)S(1)}, bf16[384,704]{0,1:T(8,128)(2,1)S(1)}, u32[]{:S(2)}, u32[]{:S(2)}) collective-permute-start(bf16[384,704]{0,1:T(8,128)(2,1)S(1)} %get-tuple-element.189), channel_id=1, source_target_pairs={{0,8},{1,9},{2,10},{3,11},{4,12},{5,13},{6,14},{7,15},{8,0},{9,1},... | collective-permute-start | bytes 1622024 | tf_op jit(solution)/shard_map/ppermute | solution.py:87
  1499.4 44.7 %collective-permute-done.138 = bf16[384,704]{0,1:T(8,128)(2,1)S(1)} collective-permute-done((bf16[384,704]{0,1:T(8,128)(2,1)S(1)}, bf16[384,704]{0,1:T(8,128)(2,1)S(1)}, u32[]{:S(2)}, u32[]{:S(2)}) %collective-permute-start.138) | collective-permute-done | bytes 540704 | tf_op jit(solution)/shard_map/ppermute | solution.py:87
  (1352 shorter events, 1010.3 us)
Async XLA Ops:
  3.2 169.7 %collective-permute-start.4 = (bf16[176,704]{0,1:T(8,128)(2,1)S(1)}, bf16[176,704]{0,1:T(8,128)(2,1)}, u32[]{:S(2)}, u32[]{:S(2)}) collective-permute-start(bf16[176,704]{0,1:T(8,128)(2,1)S(1)} %broadcast_select_fusion.34), channel_id=1, source_target_pairs={{0,8},{1,9},{2,10},{3,11},{4,12},{5,13},{6,14},{7,15},{8,0},{9,1},... | collective-permute-start | bytes 743432 | tf_op jit(solution)/shard_map/ppermute | solution.py:87
  6.3 168.5 %collective-permute-start.5 = (bf16[176,704]{0,1:T(8,128)(2,1)S(1)}, bf16[176,704]{0,1:T(8,128)(2,1)}, u32[]{:S(2)}, u32[]{:S(2)}) collective-permute-start(bf16[176,704]{0,1:T(8,128)(2,1)S(1)} %broadcast_select_fusion.34), channel_id=1, source_target_pairs={{0,16},{1,17},{2,18},{3,19},{4,20},{5,21},{6,22},{7,23},{8,24},{9,... | collective-permute-start | bytes 743432 | tf_op jit(solution)/shard_map/ppermute | solution.py:87
  12.6 77.7 %collective-permute-start.27 = (bf16[88,704]{0,1:T(8,128)(2,1)S(1)}, bf16[88,704]{0,1:T(8,128)(2,1)}, u32[]{:S(2)}, u32[]{:S(2)}) collective-permute-start(bf16[88,704]{0,1:T(8,128)(2,1)S(1)} %broadcast_select_fusion.41), channel_id=1, source_target_pairs={{0,8},{1,9},{2,10},{3,11},{4,12},{5,13},{6,14},{7,15},{8,0},{9,1},... | collective-permute-start | bytes 371720 | tf_op jit(solution)/shard_map/ppermute | solution.py:87
  13.1 77.3 %collective-permute-start.28 = (bf16[88,704]{0,1:T(8,128)(2,1)S(1)}, bf16[88,704]{0,1:T(8,128)(2,1)}, u32[]{:S(2)}, u32[]{:S(2)}) collective-permute-start(bf16[88,704]{0,1:T(8,128)(2,1)S(1)} %broadcast_select_fusion.41), channel_id=1, source_target_pairs={{0,16},{1,17},{2,18},{3,19},{4,20},{5,21},{6,22},{7,23},{8,24},{9,... | collective-permute-start | bytes 371720 | tf_op jit(solution)/shard_map/ppermute | solution.py:87
  174.8 107.4 %collective-permute-start.62 = (bf16[384,704]{0,1:T(8,128)(2,1)S(1)}, bf16[384,704]{0,1:T(8,128)(2,1)S(1)}, u32[]{:S(2)}, u32[]{:S(2)}) collective-permute-start(bf16[384,704]{0,1:T(8,128)(2,1)S(1)} %copy-done.126), channel_id=1, source_target_pairs={{0,8},{1,9},{2,10},{3,11},{4,12},{5,13},{6,14},{7,15},{8,0},{9,1},... | collective-permute-start | bytes 1622024 | tf_op jit(solution)/shard_map/ppermute | solution.py:87
  178.7 106.8 %collective-permute-start.63 = (bf16[384,704]{0,1:T(8,128)(2,1)S(1)}, bf16[384,704]{0,1:T(8,128)(2,1)S(1)}, u32[]{:S(2)}, u32[]{:S(2)}) collective-permute-start(bf16[384,704]{0,1:T(8,128)(2,1)S(1)} %copy-done.126), channel_id=1, source_target_pairs={{0,16},{1,17},{2,18},{3,19},{4,20},{5,21},{6,22},{7,23},{8,24},{9,... | collective-permute-start | bytes 1622024 | tf_op jit(solution)/shard_map/ppermute | solution.py:87
  339.3 94.9 %collective-permute-start.22 = (bf16[352,2112]{1,0:T(8,128)(2,1)}, bf16[352,2112]{1,0:T(8,128)(2,1)}, u32[]{:S(2)}, u32[]{:S(2)}) collective-permute-start(bf16[352,2112]{1,0:T(8,128)(2,1)} %pad_maximum_fusion.6), channel_id=1, source_target_pairs={{0,2},{1,5},{2,0},{3,7},{4,6},{5,1},{6,4},{7,3},{8,10},{9,13},{10,... | collective-permute-start | bytes 4460552 | tf_op jit(solution)/shard_map/ppermute | solution.py:87
  351.7 84.3 %collective-permute-start.23 = (bf16[352,2112]{1,0:T(8,128)(2,1)}, bf16[352,2112]{1,0:T(8,128)(2,1)}, u32[]{:S(2)}, u32[]{:S(2)}) collective-permute-start(bf16[352,2112]{1,0:T(8,128)(2,1)} %pad_maximum_fusion.6), channel_id=1, source_target_pairs={{0,4},{1,3},{2,6},{3,1},{4,0},{5,7},{6,2},{7,5},{8,12},{9,11},{10,... | collective-permute-start | bytes 4460552 | tf_op jit(solution)/shard_map/ppermute | solution.py:87
  402.0 122.0 %collective-permute-start.65 = (bf16[1536,704]{0,1:T(8,128)(2,1)}, bf16[1536,704]{0,1:T(8,128)(2,1)}, u32[]{:S(2)}, u32[]{:S(2)}) collective-permute-start(bf16[1536,704]{0,1:T(8,128)(2,1)} %pad_maximum_fusion.4), channel_id=1, source_target_pairs={{0,2},{1,5},{2,0},{3,7},{4,6},{5,1},{6,4},{7,3},{8,10},{9,13},{10,... | collective-permute-start | bytes 6488072 | tf_op jit(solution)/shard_map/ppermute | solution.py:87
  402.5 121.9 %collective-permute-start.66 = (bf16[1536,704]{0,1:T(8,128)(2,1)}, bf16[1536,704]{0,1:T(8,128)(2,1)S(1)}, u32[]{:S(2)}, u32[]{:S(2)}) collective-permute-start(bf16[1536,704]{0,1:T(8,128)(2,1)} %pad_maximum_fusion.4), channel_id=1, source_target_pairs={{0,4},{1,3},{2,6},{3,1},{4,0},{5,7},{6,2},{7,5},{8,12},{9,11},{10,... | collective-permute-start | bytes 6488072 | tf_op jit(solution)/shard_map/ppermute | solution.py:87
  421.9 107.4 %collective-permute-start.58 = (bf16[352,3072]{1,0:T(8,128)(2,1)}, bf16[352,3072]{1,0:T(8,128)(2,1)}, u32[]{:S(2)}, u32[]{:S(2)}) collective-permute-start(bf16[352,3072]{1,0:T(8,128)(2,1)} %pad_maximum_fusion.3), channel_id=1, source_target_pairs={{0,2},{1,5},{2,0},{3,7},{4,6},{5,1},{6,4},{7,3},{8,10},{9,13},{10,... | collective-permute-start | bytes 6488072 | tf_op jit(solution)/shard_map/ppermute | solution.py:87
  434.1 95.2 %collective-permute-start.59 = (bf16[352,3072]{1,0:T(8,128)(2,1)}, bf16[352,3072]{1,0:T(8,128)(2,1)}, u32[]{:S(2)}, u32[]{:S(2)}) collective-permute-start(bf16[352,3072]{1,0:T(8,128)(2,1)} %pad_maximum_fusion.3), channel_id=1, source_target_pairs={{0,4},{1,3},{2,6},{3,1},{4,0},{5,7},{6,2},{7,5},{8,12},{9,11},{10,... | collective-permute-start | bytes 6488072 | tf_op jit(solution)/shard_map/ppermute | solution.py:87
  510.6 168.5 %collective-permute-start.33 = (bf16[1408,704]{0,1:T(8,128)(2,1)}, bf16[1408,704]{0,1:T(8,128)(2,1)}, u32[]{:S(2)}, u32[]{:S(2)}) collective-permute-start(bf16[1408,704]{0,1:T(8,128)(2,1)} %concatenate.399), channel_id=1, source_target_pairs={{0,1},{1,0},{2,3},{3,2},{4,5},{5,4},{6,7},{7,6},{8,9},{9,8},{10,11... | collective-permute-start | bytes 5947400 | tf_op jit(solution)/shard_map/ppermute | solution.py:90
  584.5 103.7 %collective-permute-start.47 = (bf16[1408,704]{0,1:T(8,128)(2,1)}, bf16[1408,704]{0,1:T(8,128)(2,1)}, u32[]{:S(2)}, u32[]{:S(2)}) collective-permute-start(bf16[1408,704]{0,1:T(8,128)(2,1)} %concatenate.411), channel_id=1, source_target_pairs={{0,1},{1,0},{2,3},{3,2},{4,5},{5,4},{6,7},{7,6},{8,9},{9,8},{10,11... | collective-permute-start | bytes 5947400 | tf_op jit(solution)/shard_map/ppermute | solution.py:90
  591.1 115.6 %collective-permute-start.54 = (bf16[1408,704]{0,1:T(8,128)(2,1)}, bf16[1408,704]{0,1:T(8,128)(2,1)}, u32[]{:S(2)}, u32[]{:S(2)}) collective-permute-start(bf16[1408,704]{0,1:T(8,128)(2,1)} %concatenate.415), channel_id=1, source_target_pairs={{0,1},{1,0},{2,3},{3,2},{4,5},{5,4},{6,7},{7,6},{8,9},{9,8},{10,11... | collective-permute-start | bytes 5947400 | tf_op jit(solution)/shard_map/ppermute | solution.py:90
  594.2 149.2 %collective-permute-start.68 = (bf16[6144,704]{0,1:T(8,128)(2,1)}, bf16[6144,704]{0,1:T(8,128)(2,1)}, u32[]{:S(2)}, u32[]{:S(2)}) collective-permute-start(bf16[6144,704]{0,1:T(8,128)(2,1)} %constant_dynamic-update-slice_fusion.10), channel_id=1, source_target_pairs={{0,1},{1,0},{2,3},{3,2},{4,5},{5,4},{6,7},{7,6},{8,9},{9,8},{10,11... | collective-permute-start | bytes 25952264 | tf_op jit(solution)/shard_map/ppermute | solution.py:90
  645.4 109.3 %collective-permute-start.61 = (bf16[1408,3072]{1,0:T(8,128)(2,1)}, bf16[1408,3072]{1,0:T(8,128)(2,1)}, u32[]{:S(2)}, u32[]{:S(2)}) collective-permute-start(bf16[1408,3072]{1,0:T(8,128)(2,1)} %constant_dynamic-update-slice_fusion.5), channel_id=1, source_target_pairs={{0,1},{1,0},{2,3},{3,2},{4,5},{5,4},{6,7},{7,6},{8,9},{9,8},{10,11... | collective-permute-start | bytes 25952264 | tf_op jit(solution)/shard_map/ppermute | solution.py:90
  908.8 174.7 %collective-permute-start.99 = (bf16[1408,704]{0,1:T(8,128)(2,1)}, bf16[1408,704]{0,1:T(8,128)(2,1)}, u32[]{:S(2)}, u32[]{:S(2)}) collective-permute-start(bf16[1408,704]{0,1:T(8,128)(2,1)} %convolution_convert_fusion.15), channel_id=1, source_target_pairs={{0,1},{1,0},{2,3},{3,2},{4,5},{5,4},{6,7},{7,6},{8,9},{9,8},{10,11... | collective-permute-start | bytes 5947400 | tf_op jit(solution)/shard_map/ppermute | solution.py:90
  908.9 178.0 %collective-permute-start.106 = (bf16[1408,704]{0,1:T(8,128)(2,1)}, bf16[1408,704]{0,1:T(8,128)(2,1)}, u32[]{:S(2)}, u32[]{:S(2)}) collective-permute-start(bf16[1408,704]{0,1:T(8,128)(2,1)} %convolution_convert_fusion.13), channel_id=1, source_target_pairs={{0,1},{1,0},{2,3},{3,2},{4,5},{5,4},{6,7},{7,6},{8,9},{9,8},{10,11... | collective-permute-start | bytes 5947400 | tf_op jit(solution)/shard_map/ppermute | solution.py:90
  909.4 181.3 %collective-permute-start.120 = (bf16[1408,704]{0,1:T(8,128)(2,1)}, bf16[1408,704]{0,1:T(8,128)(2,1)}, u32[]{:S(2)}, u32[]{:S(2)}) collective-permute-start(bf16[1408,704]{0,1:T(8,128)(2,1)} %convolution_convert_fusion.11), channel_id=1, source_target_pairs={{0,1},{1,0},{2,3},{3,2},{4,5},{5,4},{6,7},{7,6},{8,9},{9,8},{10,11... | collective-permute-start | bytes 5947400 | tf_op jit(solution)/shard_map/ppermute | solution.py:90
  1045.8 133.2 %collective-permute-start.85 = (bf16[2816,704]{0,1:T(8,128)(2,1)S(1)}, bf16[2816,704]{0,1:T(8,128)(2,1)S(1)}, u32[]{:S(2)}, u32[]{:S(2)}) collective-permute-start(bf16[2816,704]{0,1:T(8,128)(2,1)S(1)} %copy-done.59), channel_id=1, source_target_pairs={{0,1},{1,0},{2,3},{3,2},{4,5},{5,4},{6,7},{7,6},{8,9},{9,8},{10,11... | collective-permute-start | bytes 11894792 | tf_op jit(solution)/shard_map/ppermute | solution.py:90
  1102.2 151.3 %collective-permute-start.92 = (bf16[1408,2112]{0,1:T(8,128)(2,1)}, bf16[1408,2112]{0,1:T(8,128)(2,1)}, u32[]{:S(2)}, u32[]{:S(2)}) collective-permute-start(bf16[1408,2112]{0,1:T(8,128)(2,1)} %convolution_convert_fusion), channel_id=1, source_target_pairs={{0,1},{1,0},{2,3},{3,2},{4,5},{5,4},{6,7},{7,6},{8,9},{9,8},{10,11... | collective-permute-start | bytes 17842184 | tf_op jit(solution)/shard_map/ppermute | solution.py:90
  1148.3 124.1 %collective-permute-start.127 = (bf16[1408,3072]{1,0:T(8,128)(2,1)}, bf16[1408,3072]{1,0:T(8,128)(2,1)}, u32[]{:S(2)}, u32[]{:S(2)}) collective-permute-start(bf16[1408,3072]{1,0:T(8,128)(2,1)} %convolution_convert_fusion.1), channel_id=1, source_target_pairs={{0,1},{1,0},{2,3},{3,2},{4,5},{5,4},{6,7},{7,6},{8,9},{9,8},{10,11... | collective-permute-start | bytes 25952264 | tf_op jit(solution)/shard_map/ppermute | solution.py:90
  1175.6 105.9 %collective-permute-start.134 = (bf16[6144,704]{0,1:T(8,128)(2,1)}, bf16[6144,704]{0,1:T(8,128)(2,1)}, u32[]{:S(2)}, u32[]{:S(2)}) collective-permute-start(bf16[6144,704]{0,1:T(8,128)(2,1)} %convolution_convert_fusion.4), channel_id=1, source_target_pairs={{0,1},{1,0},{2,3},{3,2},{4,5},{5,4},{6,7},{7,6},{8,9},{9,8},{10,11... | collective-permute-start | bytes 25952264 | tf_op jit(solution)/shard_map/ppermute | solution.py:90
  1228.1 82.8 %collective-permute-start.112 = (f32[88,704]{0,1:T(8,128)}, f32[88,704]{0,1:T(8,128)}, u32[]{:S(2)}, u32[]{:S(2)}) collective-permute-start(f32[88,704]{0,1:T(8,128)} %convert_add_fusion.7), channel_id=1, source_target_pairs={{0,1},{1,0},{2,3},{3,2},{4,5},{5,4},{6,7},{7,6},{8,9},{9,8},{10,11... | collective-permute-start | bytes 743432 | tf_op jit(solution)/shard_map/ppermute | solution.py:90
  1273.7 116.9 %collective-permute-start.93 = (bf16[704,2112]{1,0:T(8,128)(2,1)}, bf16[704,2112]{1,0:T(8,128)(2,1)}, u32[]{:S(2)}, u32[]{:S(2)}) collective-permute-start(bf16[704,2112]{1,0:T(8,128)(2,1)} %pad_maximum_fusion.2), channel_id=1, source_target_pairs={{0,4},{1,3},{2,6},{3,1},{4,0},{5,7},{6,2},{7,5},{8,12},{9,11},{10,... | collective-permute-start | bytes 8921096 | tf_op jit(solution)/shard_map/ppermute | solution.py:87
  1301.4 93.6 %collective-permute-start.135 = (bf16[3072,704]{0,1:T(8,128)(2,1)}, bf16[3072,704]{0,1:T(8,128)(2,1)}, u32[]{:S(2)}, u32[]{:S(2)}) collective-permute-start(bf16[3072,704]{0,1:T(8,128)(2,1)} %pad_maximum_fusion.1), channel_id=1, source_target_pairs={{0,4},{1,3},{2,6},{3,1},{4,0},{5,7},{6,2},{7,5},{8,12},{9,11},{10,... | collective-permute-start | bytes 12976136 | tf_op jit(solution)/shard_map/ppermute | solution.py:87
  1305.2 104.7 %collective-permute-start.128 = (bf16[704,3072]{1,0:T(8,128)(2,1)}, bf16[704,3072]{1,0:T(8,128)(2,1)}, u32[]{:S(2)}, u32[]{:S(2)}) collective-permute-start(bf16[704,3072]{1,0:T(8,128)(2,1)} %pad_maximum_fusion), channel_id=1, source_target_pairs={{0,4},{1,3},{2,6},{3,1},{4,0},{5,7},{6,2},{7,5},{8,12},{9,11},{10,... | collective-permute-start | bytes 12976136 | tf_op jit(solution)/shard_map/ppermute | solution.py:87
  1466.2 81.0 %collective-permute-start.132 = (bf16[88,3072]{1,0:T(8,128)(2,1)S(1)}, bf16[88,3072]{1,0:T(8,128)(2,1)S(1)}, u32[]{:S(2)}, u32[]{:S(2)}) collective-permute-start(bf16[88,3072]{1,0:T(8,128)(2,1)S(1)} %get-tuple-element.193), channel_id=1, source_target_pairs={{0,24},{1,25},{2,26},{3,27},{4,28},{5,29},{6,30},{7,31},{8,16},{9,... | collective-permute-start | bytes 1622024 | tf_op jit(solution)/shard_map/ppermute | solution.py:87
  1467.4 79.9 %collective-permute-start.131 = (bf16[88,3072]{1,0:T(8,128)(2,1)S(1)}, bf16[88,3072]{1,0:T(8,128)(2,1)S(1)}, u32[]{:S(2)}, u32[]{:S(2)}) collective-permute-start(bf16[88,3072]{1,0:T(8,128)(2,1)S(1)} %get-tuple-element.194), channel_id=1, source_target_pairs={{0,16},{1,17},{2,18},{3,19},{4,20},{5,21},{6,22},{7,23},{8,24},{9,... | collective-permute-start | bytes 1622024 | tf_op jit(solution)/shard_map/ppermute | solution.py:87
  1467.4 79.9 %collective-permute-start.130 = (bf16[88,3072]{1,0:T(8,128)(2,1)S(1)}, bf16[88,3072]{1,0:T(8,128)(2,1)S(1)}, u32[]{:S(2)}, u32[]{:S(2)}) collective-permute-start(bf16[88,3072]{1,0:T(8,128)(2,1)S(1)} %get-tuple-element.192), channel_id=1, source_target_pairs={{0,8},{1,9},{2,10},{3,11},{4,12},{5,13},{6,14},{7,15},{8,0},{9,1},... | collective-permute-start | bytes 1622024 | tf_op jit(solution)/shard_map/ppermute | solution.py:87
  1470.8 76.1 %collective-permute-start.137 = (bf16[384,704]{0,1:T(8,128)(2,1)S(1)}, bf16[384,704]{0,1:T(8,128)(2,1)S(1)}, u32[]{:S(2)}, u32[]{:S(2)}) collective-permute-start(bf16[384,704]{0,1:T(8,128)(2,1)S(1)} %get-tuple-element.189), channel_id=1, source_target_pairs={{0,8},{1,9},{2,10},{3,11},{4,12},{5,13},{6,14},{7,15},{8,0},{9,1},... | collective-permute-start | bytes 1622024 | tf_op jit(solution)/shard_map/ppermute | solution.py:87
  (407 other events, 6694.0 us)
where the time goes:
time: 1570 us; the launch traced here: 1560 us
  waiting for transfers between devices  550 us (35%)
  matrix products  290 us (18%)
  local copies, waits for them, and re-layouts  266 us (17%)
  starting transfers between devices  234 us (15%)
  other arithmetic  215 us (14%)
    ppermute x116, waiting for transfers between devices, swap(): return lax.ppermute(value, ('fsdp', 'seq'), pairs)  550 us
    ppermute x116, starting transfers between devices, swap(): return lax.ppermute(value, ('fsdp', 'seq'), pairs)  226 us
    dot_general x27, matrix products, dot_right_t(): lax.dot_general(left, right, (((1,), (1,)), ((), ())), preferred_element_...  97.3 us
    dot_general x22, matrix products, dot_plain(): return jnp.dot(left, right, preferred_element_type=f32)  72.4 us
    unnamed x648, local copies, waits for them, and re-layouts  69.9 us
    dot_general x17, matrix products, dot_left_t(): lax.dot_general(left, right, (((0,), (0,)), ((), ())), preferred_element_...  59.4 us
    concatenate x9, local copies, waits for them, and re-layouts, gather(): own = jnp.concatenate(ordered, axis=0)  47.1 us
    reshape x15, local copies, waits for them, and re-layouts, heads_of(): return value.reshape(batch, -1, HEADS, HD)  44.6 us
  transfers between devices with their start and end apart: 146, of which 64 were waited for; matrix products, arithmetic and copies ran while one was open for 40% of the time, Pallas kernels for 0%

commit v1 on v0

v1 whole, which is shorter than its diff:
```python
import functools

import jax
import jax.numpy as jnp
from jax import lax
from jax.experimental import pallas as pl
from jax.experimental.pallas import tpu as pltpu
from jax.sharding import PartitionSpec as P

HEADS = 16
HD = 88
GRID_W = 32

norm_eps = 1e-06
masked_value = -1e30
bf16 = jnp.bfloat16
f32 = jnp.float32
MESH = pl.DeviceIdType.MESH
ANYWHERE = pl.BlockSpec(memory_space=pl.ANY)
IN_VMEM = pl.BlockSpec(memory_space=pltpu.VMEM)


def layer_norm(values):
    center = values - jnp.mean(values, axis=-1, keepdims=True)
    spread = jnp.mean(center * center, axis=-1, keepdims=True)
    return center * lax.rsqrt(spread + norm_eps)


def rotary_tables(row_pos, col_pos, head_dim):
    quarter = head_dim // 4
    freqs = 10000.0 ** (-jnp.arange(quarter, dtype=f32) / quarter)
    row_angle = row_pos.astype(f32)[:, None] * freqs[None, :]
    col_angle = col_pos.astype(f32)[:, None] * freqs[None, :]
    angles = jnp.stack([row_angle, col_angle], axis=1)
    return (jnp.cos(angles), jnp.sin(angles))


def rotate(values, cosine_table, sine_table):
    rows, tokens, heads, head_dim = values.shape
    quarter = head_dim // 4
    pieces = values.reshape(rows, tokens, heads, 2, 2, quarter)
    former = pieces[..., 0, :]
    latter = pieces[..., 1, :]
    cos_wide = cosine_table[None, :, None, :, :]
    sin_wide = sine_table[None, :, None, :, :]
    turned = jnp.stack(
        [former * cos_wide - latter * sin_wide, latter * cos_wide + former * sin_wide], axis=4
    )
    return turned.reshape(rows, tokens, heads, head_dim)


def gained_norm(values, gain):
    return layer_norm(values) * gain


def gelu_tanh(values):
    return jax.nn.gelu(values, approximate=True)


def dot_plain(left, right):
    return jnp.dot(left, right, preferred_element_type=f32)


def dot_left_t(left, right):
    return lax.dot_general(
        left, right, (((0,), (0,)), ((), ())), preferred_element_type=f32
    )


def dot_right_t(left, right):
    return lax.dot_general(
        left, right, (((1,), (1,)), ((), ())), preferred_element_type=f32
    )


def softmax_back(probs, prob_grad):
    return probs * (prob_grad - jnp.sum(prob_grad * probs, axis=-1, keepdims=True))


def greet(peers):
    barrier = pltpu.get_barrier_semaphore()
    for peer in peers:
        pl.semaphore_signal(barrier, inc=1, device_id=peer, device_id_type=MESH)
    pl.semaphore_wait(barrier, len(peers))


def trade_body(count, same, source, out, send, recv, local):
    me = lax.axis_index("fsdp")
    core = lax.axis_index("seq")
    greet([(jnp.bitwise_xor(me, j), core) for j in range(1, count)])

    def part(index):
        return source if same else source.at[index]

    def copy(j):
        peer = jnp.bitwise_xor(me, j)
        return pltpu.make_async_remote_copy(
            src_ref=part(peer),
            dst_ref=out.at[me],
            send_sem=send.at[j],
            recv_sem=recv.at[j],
            device_id=(peer, core),
            device_id_type=MESH,
        )

    for j in range(1, count):
        copy(j).start()
    here = pltpu.make_async_copy(part(me), out.at[me], local.at[0])
    here.start()
    here.wait()
    for j in range(1, count):
        copy(j).wait_send()
        copy(j).wait_recv()


def trade(value, count, same, identity):
    shape = value.shape if same else value.shape[1:]
    return pl.pallas_call(
        functools.partial(trade_body, count, same),
        out_shape=jax.ShapeDtypeStruct((count, *shape), value.dtype),
        in_specs=[IN_VMEM],
        out_specs=IN_VMEM,
        scratch_shapes=[
            pltpu.SemaphoreType.DMA((count,)),
            pltpu.SemaphoreType.DMA((count,)),
            pltpu.SemaphoreType.DMA((1,)),
        ],
        compiler_params=pltpu.CompilerParams(collective_id=identity, has_side_effects=True),
    )(value)


def neighbours(quad):
    me = lax.axis_index("fsdp")
    core = lax.axis_index("seq")
    first, second = 1 + core, 2 - core

    def at(mask):
        return (jnp.bitwise_xor(me, mask), core)

    return core, first, second, at, (me, 1 - core)


def gather_body(count, quad, *refs):
    mine, out = refs[:count], refs[count : 2 * count]
    send, recv, local = refs[2 * count :]
    core, first_mask, second_mask, at, sibling = neighbours(quad)
    far_peers = [at(k * quad) for k in range(1, 4)]
    greet([*far_peers, at(first_mask), at(second_mask), sibling])

    def copy(w, slot, source, target, peer):
        return pltpu.make_async_remote_copy(
            src_ref=source,
            dst_ref=target,
            send_sem=send.at[w, slot],
            recv_sem=recv.at[w, slot],
            device_id=peer,
            device_id_type=MESH,
        )

    def block(w, q):
        return out[w].at[core, pl.ds(4 * q, 4)]

    def far(w, k):
        return copy(w, k - 1, mine[w], out[w].at[core, k], far_peers[k - 1])

    def keep(w):
        return pltpu.make_async_copy(mine[w], out[w].at[core, 0], local.at[w])

    def first(w):
        return copy(w, 3, block(w, 0), block(w, first_mask), at(first_mask))

    def second(w):
        return copy(w, 4, block(w, 0), block(w, second_mask), at(second_mask))

    def both(w):
        return copy(w, 5, block(w, first_mask), block(w, 3), at(second_mask))

    def twin(w, n):
        q = (0, first_mask, second_mask, 3)[n]
        return copy(w, 6 + n, block(w, q), block(w, q), sibling)

    for w in range(count):
        keep(w).start()
        for k in range(1, 4):
            far(w, k).start()
    for step in range(count + 2):
        w = step
        if w < count:
            keep(w).wait()
            for k in range(1, 4):
                far(w, k).wait_recv()
            first(w).start()
            second(w).start()
            twin(w, 0).start()
        w = step - 1
        if 0 <= w < count:
            first(w).wait_recv()
            both(w).start()
            twin(w, 1).start()
            second(w).wait_recv()
            twin(w, 2).start()
        w = step - 2
        if 0 <= w < count:
            both(w).wait_recv()
            twin(w, 3).start()
    for w in range(count):
        for k in range(1, 4):
            far(w, k).wait_send()
        first(w).wait_send()
        second(w).wait_send()
        both(w).wait_send()
        for n in range(4):
            twin(w, n).wait_send()
            twin(w, n).wait_recv()


def gather(shards, quad, identity):
    count = len(shards)
    return pl.pallas_call(
        functools.partial(gather_body, count, quad),
        out_shape=[jax.ShapeDtypeStruct((2, 16, *s.shape), bf16) for s in shards],
        in_specs=[ANYWHERE] * count,
        out_specs=[ANYWHERE] * count,
        scratch_shapes=[
            pltpu.SemaphoreType.DMA((count, 10)),
            pltpu.SemaphoreType.DMA((count, 10)),
            pltpu.SemaphoreType.DMA((count,)),
        ],
        compiler_params=pltpu.CompilerParams(collective_id=identity, has_side_effects=True),
    )(*shards)


def scatter_body(count, quad, *refs):
    source, out = refs[:count], refs[count : 2 * count]
    kept, half, quarter, last, total = (
        refs[(2 + n) * count : (3 + n) * count] for n in range(5)
    )
    send, recv, local = refs[7 * count :]
    core, first_mask, second_mask, at, sibling = neighbours(quad)
    far_peers = [at(k * quad) for k in range(1, 4)]
    greet([*far_peers, at(first_mask), at(second_mask), sibling])

    def copy(w, slot, origin, target, peer):
        return pltpu.make_async_remote_copy(
            src_ref=origin,
            dst_ref=target,
            send_sem=send.at[w, slot],
            recv_sem=recv.at[w, slot],
            device_id=peer,
            device_id_type=MESH,
        )

    def block(w, q):
        return source[w].at[pl.ds(4 * q, 4)]

    def give(w, n):
        q = 3 if n == 0 else second_mask
        return copy(w, n, block(w, q), half[w].at[n], at(second_mask))

    def load(w, n):
        q = first_mask if n == 0 else 0
        return pltpu.make_async_copy(block(w, q), kept[w].at[n], local.at[w, n])

    def pass_on(w):
        return copy(w, 2, half[w].at[0], quarter[w], at(first_mask))

    def far(w, k):
        return copy(w, 2 + k, half[w].at[1, k], last[w].at[k - 1], far_peers[k - 1])

    def twin(w):
        return copy(w, 6, total[w], out[w].at[core], sibling)

    def store(w):
        return pltpu.make_async_copy(total[w], out[w].at[core], local.at[w, 2])

    def lanes(w, body):
        width = total[w].shape[1]
        step = 256 if width % 256 == 0 else 128 if width % 128 == 0 else width
        if step == width:
            body(slice(None))
        else:

            @pl.loop(0, width // step)
            def _(i):
                body(pl.ds(pl.multiple_of(i * step, step), step))

    for w in range(count):
        for n in range(2):
            give(w, n).start()
            load(w, n).start()
    for step in range(count + 2):
        w = step
        if w < count:
            give(w, 0).wait_recv()
            load(w, 0).wait()

            def body(c):
                for k in range(4):
                    half[w][0, k, :, c] = (
                        half[w][0, k, :, c].astype(f32) + kept[w][0, k, :, c].astype(f32)
                    ).astype(bf16)

            lanes(w, body)
            pass_on(w).start()
        w = step - 1
        if 0 <= w < count:
            give(w, 1).wait_recv()
            load(w, 1).wait()
            pass_on(w).wait_recv()

            def body(c):
                for k in range(4):
                    value = half[w][1, k, :, c].astype(f32) + kept[w][1, k, :, c].astype(f32)
                    value = value + quarter[w][k, :, c].astype(f32)
                    if k == 0:
                        total[w][:, c] = value
                    else:
                        half[w][1, k, :, c] = value.astype(bf16)

            lanes(w, body)
            for k in range(1, 4):
                far(w, k).start()
        w = step - 2
        if 0 <= w < count:
            for k in range(1, 4):
                far(w, k).wait_recv()

            def body(c):
                value = total[w][:, c]
                for k in range(3):
                    value = value + last[w][k, :, c].astype(f32)
                total[w][:, c] = value

            lanes(w, body)
            twin(w).start()
            store(w).start()
    for w in range(count):
        give(w, 0).wait_send()
        give(w, 1).wait_send()
        pass_on(w).wait_send()
        for k in range(1, 4):
            far(w, k).wait_send()
        twin(w).wait_send()
        twin(w).wait_recv()
        store(w).wait()


def scatter(sums, quad, identity):
    count = len(sums)
    shapes = [s.shape[1:] for s in sums]

    def buffers(*lead):
        return [pltpu.VMEM((*lead, *s), bf16) for s in shapes]

    return pl.pallas_call(
        functools.partial(scatter_body, count, quad),
        out_shape=[jax.ShapeDtypeStruct((2, *s), f32) for s in shapes],
        in_specs=[ANYWHERE] * count,
        out_specs=[ANYWHERE] * count,
        scratch_shapes=[
            *buffers(2, 4),
            *buffers(2, 4),
            *buffers(4),
            *buffers(3),
            *[pltpu.VMEM(s, f32) for s in shapes],
            pltpu.SemaphoreType.DMA((count, 7)),
            pltpu.SemaphoreType.DMA((count, 7)),
            pltpu.SemaphoreType.DMA((count, 3)),
        ],
        compiler_params=pltpu.CompilerParams(
            collective_id=identity, has_side_effects=True, vmem_limit_bytes=56 * 2**20
        ),
    )(*sums)


class Links:
    def __init__(self, fsdp_count):
        self.count = fsdp_count
        self.me = lax.axis_index("fsdp")
        self.core = lax.axis_index("seq")
        self.high_bits = fsdp_count.bit_length() - 3
        self.quad = 4 << (self.high_bits - 2)
        offsets = [0]
        for bit in range(self.high_bits - 2):
            offsets = offsets + [offset | (4 << bit) for offset in offsets]
        self.high_offsets = [k * self.quad | offset for k in range(4) for offset in offsets]

    def swap(self, value, mask_first, mask_second):
        pairs = []
        for index in range(self.count):
            pairs.append((2 * index, 2 * (index ^ mask_first)))
            pairs.append((2 * index + 1, 2 * (index ^ mask_second) + 1))
        return lax.ppermute(value, ("fsdp", "seq"), pairs)

    def sibling(self, value):
        return lax.ppermute(value, "seq", [(0, 1), (1, 0)])

    def pick(self, first, second):
        return jnp.where(self.core == 0, first, second)

    def offset(self, block):
        return self.high_offsets[block % (self.count // 4)] | (block // (self.count // 4))

    def place(self, offset):
        table = [0] * self.count
        for block in range(self.count):
            table[self.offset(block)] = block
        return jnp.array(table, jnp.int32)[offset]

    def columns(self, own, other):
        return self.pick(
            jnp.concatenate([own, other], axis=-1), jnp.concatenate([other, own], axis=-1)
        )

    def halves(self, value):
        half = value.shape[-1] // 2
        first, second = value[..., :half], value[..., half:]
        return self.pick(first, second), self.pick(second, first)

    def order_matrix(self, size):
        block = size // self.count
        at = lax.broadcasted_iota(jnp.int32, (size, size), 0)
        table = jnp.array([self.offset(b) for b in range(self.count)], jnp.int32)
        starts = jnp.bitwise_xor(self.me, table) * block
        wanted = (starts[:, None] + jnp.arange(block, dtype=jnp.int32)[None, :]).reshape(1, size)
        return (at == wanted).astype(bf16)

    def order_skip(self, width):
        block = width // self.count
        offsets = [
            offset & (self.count // 2 - 1) for offset in self.high_offsets[: self.count // 2 // 4 * 1]
        ]
        offsets = [offset | q for q in range(4) for offset in offsets]
        lower = jnp.bitwise_and(self.me, self.count // 2 - 1)
        starts = jnp.bitwise_xor(lower, jnp.array(offsets, jnp.int32)) * (2 * block)
        starts = jnp.stack([starts, starts + block])
        wanted = (starts[:, :, None] + jnp.arange(block, dtype=jnp.int32)).reshape(1, width)
        return (lax.broadcasted_iota(jnp.int32, (width, width), 0) == wanted).astype(bf16)

    def order_blocks(self, value):
        size = value.shape[1] // self.count
        parts = []
        for block in range(self.count):
            source = jnp.bitwise_xor(self.me, self.offset(block))
            parts.append(lax.dynamic_slice_in_dim(value, source * size, size, 1))
        return jnp.concatenate(parts, axis=1)

    def restore_blocks(self, value):
        size = value.shape[1] // self.count
        parts = []
        for shard in range(self.count):
            source = self.place(jnp.bitwise_xor(self.me, shard))
            parts.append(lax.dynamic_slice_in_dim(value, source * size, size, 1))
        return jnp.concatenate(parts, axis=1)

    def extra_gather(self, mine):
        blocks = mine
        for bit in range(self.high_bits - 2):
            blocks = jnp.concatenate([blocks, self.swap(blocks, 4 << bit, 4 << bit)], axis=0)
        return blocks

    def extra_scatter(self, value):
        for bit in reversed(range(self.high_bits - 2)):
            size = value.shape[-2] // 2
            value = value[..., :size, :] + self.swap(value[..., size:, :], 4 << bit, 4 << bit)
        return value


class Gather:
    def __init__(self, links, shards):
        self.links = links
        half = shards[0].shape[1] // 2
        self.rows = shards[0].shape[0]
        self.weights = len(shards)
        self.shards = jnp.concatenate(
            [links.pick(shard[:, :half], shard[:, half:]) for shard in shards], axis=0
        )
        self.pending = [self.shards]
        self.stage = 0

    def advance(self):
        links = self.links
        self.stage += 1
        if self.stage == 1:
            blocks = [self.pending[0]]
            for bit in range(links.high_bits - 2):
                got = links.swap(jnp.concatenate(blocks, axis=0), 4 << bit, 4 << bit)
                size = self.rows * self.weights
                blocks = blocks + [got[at * size : (at + 1) * size] for at in range(len(blocks))]
            self.low_blocks = len(blocks)
            mine = jnp.concatenate(blocks, axis=0) if len(blocks) > 1 else blocks[0]
            self.pending = [mine] + [
                links.swap(mine, k * links.quad, k * links.quad) for k in range(1, 4)
            ]
        elif self.stage == 2:
            size = self.rows * self.weights
            cuts = [
                got[at * size + w * self.rows : at * size + (w + 1) * self.rows]
                for w in range(self.weights)
                for got in self.pending
                for at in range(self.low_blocks)
            ]
            base = jnp.concatenate(cuts, axis=0)
            self.pending = [
                base, links.swap(base, 1, 2), links.swap(base, 2, 1), links.sibling(base)
            ]
        elif self.stage == 3:
            base, first, second, base_there = self.pending
            self.kept = [base, second, base_there]
            self.pending = [
                links.swap(first, 2, 1), links.sibling(first), links.sibling(second), *self.pending
            ]
        elif self.stage == 4:
            self.pending[0:1] = [links.sibling(self.pending[0]), self.pending[0]]
        elif self.stage == 5:
            both_there, both, first_there, second_there, base, first, second, base_there = self.pending
            size = base.shape[0] // self.weights
            self.result = []
            for w in range(self.weights):
                cut = slice(w * size, (w + 1) * size)
                pick = links.pick
                own = jnp.concatenate(
                    [base[cut], pick(first[cut], second[cut]), pick(second[cut], first[cut]), both[cut]],
                    axis=0,
                )
                other = jnp.concatenate(
                    [
                        base_there[cut],
                        pick(second_there[cut], first_there[cut]),
                        pick(first_there[cut], second_there[cut]),
                        both_there[cut],
                    ],
                    axis=0,
                )
                self.result.append((own, other))
            self.pending = []

    def finish(self):
        while self.stage < 5:
            self.advance()
        return self.result


class Scatter:
    def __init__(self, links, pairs):
        self.links = links
        self.pairs = pairs
        self.pending = [other for _, other in pairs]
        self.stage = 0

    def advance(self):
        links = self.links
        pick = links.pick
        self.stage += 1
        if self.stage == 1:
            self.pending = [own for own, _ in self.pairs] + [
                links.sibling(other) for other in self.pending
            ]
        elif self.stage == 2:
            count = len(self.pairs)
            send, keep = [[], []], [[], []]
            for own, got in zip(self.pending[:count], self.pending[count:]):
                size = own.shape[0] // 4
                cuts = [
                    own[q * size : (q + 1) * size].astype(f32) + got[q * size : (q + 1) * size].astype(f32)
                    for q in range(4)
                ]
                send[0].append(pick(cuts[2], cuts[1]).astype(bf16))
                send[1].append(cuts[3].astype(bf16))
                keep[0].append(cuts[0])
                keep[1].append(pick(cuts[1], cuts[2]))
            self.sizes = [part.shape[0] for part in keep[0]]
            self.keep = [jnp.concatenate(part, axis=0) for part in keep]
            self.pending = [links.swap(jnp.concatenate(send[0] + send[1], axis=0), 2, 1)]
        elif self.stage == 3:
            total = sum(self.sizes)
            got = self.pending[0].astype(f32)
            self.keep, send = self.keep[0] + got[:total], (self.keep[1] + got[total:]).astype(bf16)
            self.pending = [links.swap(send, 1, 2)]
        elif self.stage == 4:
            summed = self.keep + self.pending[0].astype(f32)
            keep, send = [], [[], [], []]
            start = 0
            for size in self.sizes:
                part = size // 4
                keep.append(summed[start : start + part])
                for k in range(1, 4):
                    send[k - 1].append(summed[start + k * part : start + (k + 1) * part].astype(bf16))
                start += size
            self.keep = jnp.concatenate(keep, axis=0)
            self.pending = [
                links.swap(jnp.concatenate(send[k - 1], axis=0), k * links.quad, k * links.quad)
                for k in range(1, 4)
            ]
        elif self.stage == 5:
            total = self.keep
            for got in self.pending:
                total = total + got.astype(f32)
            rows = [size // 4 for size in self.sizes]
            for bit in reversed(range(links.high_bits - 2)):
                keep, send, start = [], [], 0
                for at, size in enumerate(rows):
                    keep.append(total[start : start + size // 2])
                    send.append(total[start + size // 2 : start + size])
                    start += size
                    rows[at] = size // 2
                got = links.swap(jnp.concatenate(send, axis=0), 4 << bit, 4 << bit)
                total = jnp.concatenate(keep, axis=0) + got
            self.rows = rows
            self.pending = [total, links.sibling(total)]
        elif self.stage == 6:
            whole = links.columns(*self.pending)
            self.result, start = [], 0
            for size in self.rows:
                self.result.append(whole[start : start + size])
                start += size
            self.pending = []

    def finish(self):
        while self.stage < 6:
            self.advance()
        return self.result


def tie(value, *jobs):
    leaves, tree = jax.tree.flatten(value)
    flat = list(leaves)
    for job in jobs:
        flat.extend(job.pending)
    flat = list(lax.optimization_barrier(tuple(flat)))
    at = len(leaves)
    value = jax.tree.unflatten(tree, flat[:at])
    for job in jobs:
        job.pending = flat[at : at + len(job.pending)]
        at += len(job.pending)
        job.advance()
    return value


def lanes_of(value, multiple):
    size = 128 * multiple
    spare = -value.shape[-1] % size
    value = jnp.pad(value, [(0, 0)] * (value.ndim - 1) + [(0, spare)])
    return value.reshape(*value.shape[:-1], -1, 128)


def exact_restore(matrix, value):
    high = value.astype(bf16)
    low = (value - high.astype(f32)).astype(bf16)
    return dot_right_t(high, matrix) + dot_right_t(low, matrix)


def attend(queries, keys, scaling):
    return jnp.einsum("bqhd,bkhd->bhqk", queries, keys, preferred_element_type=f32) * scaling


def mix(probs, values):
    return jnp.einsum("bhqk,bkhd->bqhd", probs, values, preferred_element_type=f32)


def mix_back(probs, grads):
    return jnp.einsum("bhqk,bqhd->bkhd", probs, grads, preferred_element_type=f32)


def local(
    latent,
    skip_input,
    condition,
    text_encoder_states,
    text_lengths,
    out_grad,
    skip_gain,
    norm_gains,
    skip_linear,
    shift_linear,
    self_qkv,
    self_out,
    cross_query,
    cross_keyval,
    cross_out,
    mlp_up,
    mlp_down,
    thresholds,
):
    batch, tokens, width = latent.shape
    rows = batch * tokens
    text_rows = text_encoder_states.shape[1]
    text_width = text_encoder_states.shape[2]
    scaling = HD ** (-0.5)
    links = Links(lax.axis_size("fsdp"))
    me, core = links.me, links.core
    count = links.count

    positions = core * tokens + jnp.arange(tokens)
    cosine_table, sine_table = rotary_tables(positions // GRID_W, positions % GRID_W, HD)

    gain_rows = skip_gain.shape[0]
    third = norm_gains.shape[1]
    cond_act = jax.nn.silu(condition.astype(f32)).astype(bf16)
    small = jnp.concatenate([skip_gain, norm_gains.reshape(-1), cond_act.reshape(-1)])
    small = trade(lanes_of(small, 16), count, True, 1).reshape(count, -1)
    skip_gain_all = small[:, :gain_rows].reshape(-1).astype(f32)
    cond_start = gain_rows + 3 * third
    gains = small[:, gain_rows:cond_start].reshape(count, 3, third)
    gains = gains.transpose(1, 0, 2).reshape(3, width).astype(f32)
    cond_all = small[:, cond_start : cond_start + batch * width].reshape(count * batch, width)
    shift_rows = shift_linear.shape[0]
    cond_cut = lax.dynamic_slice_in_dim(cond_all, me * shift_rows, shift_rows, 1)
    shift_parts = dot_plain(cond_cut, shift_linear).reshape(count, batch * width)
    shift_parts = trade(lanes_of(shift_parts, 8), count, False, 2)
    shift = jnp.sum(shift_parts.reshape(count, -1), axis=0)[: batch * width].reshape(batch, width)

    def columns_mine(weight):
        half = weight.shape[1] // 2
        return links.pick(weight[:, :half], weight[:, half:])

    skip_half = skip_linear.shape[0] // 2
    shards = [
        links.pick(skip_linear[:skip_half], skip_linear[skip_half:]),
        columns_mine(self_qkv),
        links.pick(self_out, cross_out),
        columns_mine(cross_query),
        columns_mine(cross_keyval),
    ]
    shards = [links.extra_gather(shard) for shard in shards]
    shards = lax.optimization_barrier((shift, *shards))
    shift = shards[0]
    gathered = gather(shards[1:], links.quad, 3)
    w_skip, w_qkv, w_pair, w_query, w_keyval = (
        g.reshape(2, 16 * g.shape[2], g.shape[3]) for g in gathered
    )
    w_self_out, w_cross_out = w_pair[0], w_pair[1]
    get_up = Gather(links, [mlp_up])
    get_down = Gather(links, [mlp_down])
    w_skip = tie(w_skip, get_up, get_down)

    order = links.order_matrix(width)
    order_skip = links.order_skip(width)
    order_text = links.order_matrix(text_width)

    def product(value, weight):
        return jnp.concatenate([dot_plain(value, weight[0]), dot_plain(value, weight[1])], axis=1)

    def product_back(grad, weight):
        half = grad.shape[1] // 2
        return dot_right_t(grad[:, :half], weight[0]) + dot_right_t(grad[:, half:], weight[1])

    def sum_twins(own, other):
        there = links.sibling(dot_left_t(*other).astype(bf16))
        return own, there

    def finish_twins(own, there):
        value = (dot_left_t(*own) + there.astype(f32)).astype(bf16)
        return value.reshape(16, value.shape[0] // 16, value.shape[1])

    def column_grad(value, grad):
        own, other = links.halves(grad)
        return sum_twins((value, own), (value, other))

    def weight_grad(value, grad_halves):
        return (
            dot_left_t(value, grad_halves[0]).astype(bf16),
            dot_left_t(value, grad_halves[1]).astype(bf16),
        )

    def relative_product(value, weight):
        return links.columns(dot_plain(value, weight[0]), dot_plain(value, weight[1]))

    def relative_back(grad_halves, weight):
        return dot_right_t(grad_halves[0], weight[0]) + dot_right_t(grad_halves[1], weight[1])

    def reorder(value):
        return dot_plain(value, order).astype(bf16)

    def restore(value):
        return dot_right_t(value.astype(bf16), order).astype(bf16)

    def heads_of(value):
        return value.reshape(batch, -1, HEADS, HD)

    joined = jnp.concatenate(
        [latent.reshape(rows, width), skip_input.reshape(rows, width)], axis=1
    ).astype(f32)
    normed = gained_norm(joined, skip_gain_all).astype(bf16)
    upper_half = (me >= count // 2).astype(jnp.int32)
    near = jnp.where(upper_half == 0, normed[:, :width], normed[:, width:])
    away = jnp.where(upper_half == 0, normed[:, width:], normed[:, :width])
    near = dot_plain(near, order_skip).astype(bf16).reshape(rows, 2, 4, 1, -1)
    away = dot_plain(away, order_skip).astype(bf16).reshape(rows, 2, 4, 1, -1)
    normed = jnp.concatenate([near, away], axis=3).reshape(rows, 2, width)
    normed = (normed[:, 0], normed[:, 1])
    hidden = dot_plain(normed[0], w_skip[0]) + dot_plain(normed[1], w_skip[1])

    def shifted(values, gain, moved):
        wide = jnp.broadcast_to(moved[:, None, :], (batch, tokens, width)).reshape(rows, width)
        return layer_norm(values) * gain + wide

    attn_in = reorder(shifted(hidden, gains[0], shift).astype(bf16))
    qkv_proj = product(attn_in, w_qkv)
    query_proj = heads_of(qkv_proj[:, :width])
    key_proj = heads_of(qkv_proj[:, width : 2 * width])

    def norm_rotate(values):
        return rotate(layer_norm(values), cosine_table, sine_table)

    queries = norm_rotate(query_proj).astype(bf16)
    keys_here = norm_rotate(key_proj).astype(bf16)
    values_here = heads_of(qkv_proj[:, 2 * width :].astype(bf16))
    keyval_here = jnp.concatenate(
        [keys_here.reshape(rows, width), values_here.reshape(rows, width)], axis=1
    )
    keyval_there = links.sibling(keyval_here)
    keys_all = jnp.concatenate([keys_here, heads_of(keyval_there[:, :width])], axis=1)
    values_all = jnp.concatenate([values_here, heads_of(keyval_there[:, width:])], axis=1)
    queries = tie(queries, get_up)
    scores = attend(queries, keys_all, scaling)
    self_peak = jnp.max(scores, axis=(0, 2, 3))
    probs = jax.nn.softmax(scores, axis=-1)
    mixed = mix(probs.astype(bf16), values_all)
    attn_cat = reorder(mixed.reshape(rows, width).astype(bf16))
    attn_cat = tie(attn_cat, get_down)
    after_self = hidden + dot_plain(attn_cat, w_self_out)
    cross_in = reorder(gained_norm(after_self, gains[1]).astype(bf16))
    cq_proj = heads_of(product(cross_in, w_query))
    cross_queries = layer_norm(cq_proj).astype(bf16)

    text = text_encoder_states.reshape(batch * text_rows, text_width)
    text_ordered = dot_plain(text, order_text).astype(bf16)
    ckv_proj = product(text_ordered, w_keyval)
    ckey_proj = heads_of(ckv_proj[:, :width])
    cross_keys = layer_norm(ckey_proj).astype(bf16)
    cross_values = heads_of(ckv_proj[:, width:].astype(bf16))
    text_valid = jnp.arange(text_rows)[None, :] < text_lengths[:, None]
    cross_queries = tie(cross_queries, get_up)
    cross_scores = jnp.where(
        text_valid[:, None, None, :], attend(cross_queries, cross_keys, scaling), masked_value
    )
    cross_peak = jnp.max(cross_scores, axis=(0, 2, 3))
    cross_probs = jax.nn.softmax(cross_scores, axis=-1)
    cross_mixed = mix(cross_probs.astype(bf16), cross_values)
    cross_cat = reorder(cross_mixed.reshape(rows, width).astype(bf16))
    after_cross = after_self + dot_plain(cross_cat, w_cross_out)
    mlp_in = reorder(gained_norm(after_cross, gains[2]).astype(bf16))
    mlp_in = tie(mlp_in, get_up, get_down)
    (w_up,) = get_up.finish()
    upper = relative_product(mlp_in, w_up)
    activated = links.order_blocks(gelu_tanh(upper).astype(bf16))

    down_in = out_grad.reshape(rows, width)
    result_grad = down_in.astype(f32)
    down_halves = links.halves(down_in)
    put_down = Scatter(links, [weight_grad(activated, down_halves)])
    put_down.advance()
    activated = tie(activated, put_down)
    (w_down,) = get_down.finish()
    block_out = (after_cross + relative_product(activated, w_down)).astype(bf16)
    act_grad = links.restore_blocks(relative_back(down_halves, w_down))
    upper_grad = jax.vjp(gelu_tanh, upper)[1](act_grad)[0].astype(bf16)
    upper_halves = links.halves(upper_grad)
    put_up = Scatter(links, [weight_grad(mlp_in, upper_halves)])
    put_up.advance()
    mlp_in_grad = exact_restore(order, relative_back(upper_halves, w_up))
    cross_part, gain_third = jax.vjp(gained_norm, after_cross, gains[2])[1](mlp_in_grad)
    cross_grad = result_grad + cross_part
    cross_bf = tie(cross_grad.astype(bf16), put_up)
    cmix_grad = heads_of(restore(dot_right_t(cross_bf, w_cross_out)))
    cval_grad = mix_back(cross_probs.astype(bf16), cmix_grad)
    cmix_grad = tie(cmix_grad, put_down)
    cprob_grad = jnp.einsum("bqhd,bkhd->bhqk", cmix_grad, cross_values, preferred_element_type=f32)
    cscore_grad = softmax_back(cross_probs, cprob_grad).astype(bf16)
    cquery_grad = mix(cscore_grad, cross_keys) * scaling
    ckey_grad = mix_back(cscore_grad, cross_queries) * scaling
    cq_grad = jax.vjp(layer_norm, cq_proj)[1](cquery_grad)[0].reshape(rows, width).astype(bf16)
    put_query = column_grad(cross_in, cq_grad)
    cq_grad = tie(cq_grad, put_up, put_down)
    cross_in_grad = exact_restore(order, product_back(cq_grad, w_query))
    self_part, gain_second = jax.vjp(gained_norm, after_self, gains[1])[1](cross_in_grad)
    self_grad = cross_grad + self_part

    text_half = text_rows // 2
    ckeyval = jnp.concatenate(
        [
            ckey_grad.reshape(batch, text_rows, width),
            cval_grad.reshape(batch, text_rows, width),
        ],
        axis=2,
    ).astype(bf16)
    ckeyval_mine = lax.dynamic_slice_in_dim(ckeyval, core * text_half, text_half, 1)
    ckeyval_theirs = lax.dynamic_slice_in_dim(ckeyval, (1 - core) * text_half, text_half, 1)
    ckeyval_sum = ckeyval_mine.astype(f32) + links.sibling(ckeyval_theirs).astype(f32)
    ckey_mine = lax.dynamic_slice_in_dim(ckey_proj, core * text_half, text_half, 1)
    ckey_pre = jax.vjp(layer_norm, ckey_mine)[1](heads_of(ckeyval_sum[..., :width]))[0]
    keyval_grad = jnp.concatenate(
        [ckey_pre.reshape(batch * text_half, width), ckeyval_sum[..., width:].reshape(-1, width)],
        axis=1,
    ).astype(bf16)
    text_mine = lax.dynamic_slice_in_dim(
        text_ordered.reshape(batch, text_rows, text_width), core * text_half, text_half, 1
    ).reshape(-1, text_width)
    put_keyval = column_grad(text_mine, keyval_grad)
    grad_text = exact_restore(order_text, product_back(keyval_grad, w_keyval))
    grad_text = grad_text.reshape(batch, text_half, text_width)

    self_bf = self_grad.astype(bf16)
    put_pair = sum_twins(
        (links.pick(attn_cat, cross_cat), links.pick(self_bf, cross_bf)),
        (links.pick(cross_cat, attn_cat), links.pick(cross_bf, self_bf)),
    )
    self_bf = tie(self_bf, put_down)
    mix_grad = heads_of(restore(dot_right_t(self_bf, w_self_out)))
    mix_grad = tie(mix_grad, put_up)
    value_grad = mix_back(probs.astype(bf16), mix_grad)
    prob_grad = jnp.einsum("bqhd,bkhd->bhqk", mix_grad, values_all, preferred_element_type=f32)
    score_grad = softmax_back(probs, prob_grad).astype(bf16)
    score_grad = tie(score_grad, put_up)
    query_grad = mix(score_grad, keys_all) * scaling
    key_grad = mix_back(score_grad, queries) * scaling
    there = jnp.concatenate(
        [key_grad[:, tokens:].reshape(rows, width), value_grad[:, tokens:].reshape(rows, width)],
        axis=1,
    ).astype(bf16)
    from_there = links.sibling(there).astype(f32)
    key_here = key_grad[:, :tokens] + heads_of(from_there[:, :width])
    value_here = value_grad[:, :tokens].reshape(rows, width) + from_there[:, width:]
    query_pre = jax.vjp(norm_rotate, query_proj)[1](query_grad)[0]
    key_pre = jax.vjp(norm_rotate, key_proj)[1](key_here)[0]
    qkv_grad = jnp.concatenate(
        [query_pre.reshape(rows, width), key_pre.reshape(rows, width), value_here], axis=1
    ).astype(bf16)
    put_qkv = column_grad(attn_in, qkv_grad)
    attn_in_grad = exact_restore(order, product_back(qkv_grad, w_qkv))
    hidden_part, gain_first, shift_grad = jax.vjp(shifted, hidden, gains[0], shift)[1](
        attn_in_grad
    )
    hidden_grad = self_grad + hidden_part
    hidden_bf = hidden_grad.astype(bf16)
    put_skip = sum_twins(
        (links.pick(*normed), hidden_bf), (links.pick(normed[1], normed[0]), hidden_bf)
    )
    normed_grad = jnp.concatenate(
        [dot_right_t(hidden_bf, w_skip[0]), dot_right_t(hidden_bf, w_skip[1])], axis=1
    ).reshape(rows, 2, 4, 2, -1)
    near_grad = exact_restore(order_skip, normed_grad[:, :, :, 0].reshape(rows, width))
    away_grad = exact_restore(order_skip, normed_grad[:, :, :, 1].reshape(rows, width))
    normed_grad = jnp.concatenate(
        [
            jnp.where(upper_half == 0, near_grad, away_grad),
            jnp.where(upper_half == 0, away_grad, near_grad),
        ],
        axis=1,
    )
    joined_grad, skip_gain_grad = jax.vjp(gained_norm, joined, skip_gain_all)[1](normed_grad)

    sums = [
        finish_twins(*put) for put in (put_pair, put_query, put_keyval, put_qkv, put_skip)
    ]
    (grad_down,) = put_down.finish()
    (grad_up,) = put_up.finish()
    scattered = [links.extra_scatter(part) for part in scatter(sums, links.quad, 4)]
    grad_self_out, grad_cross_out = scattered[0][0], scattered[0][1]
    grad_cross_query, grad_keyval, grad_qkv = (
        jnp.concatenate([part[0], part[1]], axis=1) for part in scattered[1:4]
    )
    grad_skip_linear = scattered[4].reshape(skip_linear.shape)

    gains_grad = jnp.stack([gain_first, gain_second, gain_third])
    gains_grad = gains_grad.reshape(3, count, third).transpose(1, 0, 2).reshape(count, 3 * third)
    gains_grad = jnp.concatenate([skip_gain_grad.reshape(count, gain_rows), gains_grad], axis=1)
    peaks = jnp.stack([self_peak, cross_peak])
    cores = jnp.concatenate([shift_grad.reshape(-1), gains_grad.reshape(-1), peaks.reshape(-1)])
    there = links.sibling(cores)
    peaks = jnp.maximum(cores, there)[-2 * HEADS :]
    cores = cores + there
    ends = (batch * width, batch * width + count * cond_start)
    gains_grad = cores[ends[0] : ends[1]].reshape(count, cond_start)
    shift_bf = cores[: ends[0]].astype(bf16).astype(f32)
    shared = trade(lanes_of(jnp.concatenate([shift_bf, peaks]), 8), count, True, 5)
    shared = shared.reshape(count, -1)
    shift_all = shared[:, : ends[0]].reshape(count * batch, width).astype(bf16)
    peaks = jnp.max(shared[:, ends[0] : ends[0] + 2 * HEADS], axis=0).reshape(2, HEADS)
    grad_shift = dot_left_t(cond_cut, shift_all)
    cond_back = dot_right_t(shift_all, shift_linear).reshape(count, batch * shift_rows)
    owned = trade(lanes_of(jnp.concatenate([cond_back, gains_grad], axis=1), 8), count, False, 6)
    owned = owned.reshape(count, -1)
    cond_mine = owned[:, : batch * shift_rows].reshape(count, batch, shift_rows)
    cond_mine = cond_mine.transpose(1, 0, 2).reshape(batch, width)
    grad_cond = jax.vjp(jax.nn.silu, condition.astype(f32))[1](cond_mine)[0]
    own_gains = jnp.sum(owned[:, batch * shift_rows : batch * shift_rows + cond_start], axis=0)
    grad_skip_gain = own_gains[:gain_rows]
    grad_gains = own_gains[gain_rows:].reshape(3, third)

    roots = jnp.sqrt(thresholds / jnp.maximum(peaks, thresholds))
    self_cols = jnp.repeat(roots[0], HD)
    cross_cols = jnp.repeat(roots[1], HD)
    unit_cols = jnp.ones((width,), f32)
    clipped_qkv = (
        self_qkv.astype(f32) * jnp.concatenate([self_cols, self_cols, unit_cols])[None, :]
    ).astype(bf16)
    clipped_query = (cross_query.astype(f32) * cross_cols[None, :]).astype(bf16)
    clipped_keyval = (
        cross_keyval.astype(f32) * jnp.concatenate([cross_cols, unit_cols])[None, :]
    ).astype(bf16)
    return (
        block_out.reshape(batch, tokens, width),
        joined_grad[:, :width].reshape(batch, tokens, width),
        joined_grad[:, width:].reshape(batch, tokens, width),
        grad_cond,
        grad_text,
        grad_skip_gain,
        grad_gains,
        grad_skip_linear,
        grad_shift,
        grad_qkv,
        grad_self_out,
        grad_cross_query,
        grad_keyval,
        grad_cross_out,
        grad_up,
        grad_down,
        clipped_qkv,
        clipped_query,
        clipped_keyval,
        peaks,
    )


def solution(mesh):
    rows = P("fsdp", None)
    tokens = P("fsdp", "seq", None)
    in_specs = (
        tokens,
        tokens,
        rows,
        P("fsdp", None, None),
        P("fsdp"),
        tokens,
        P("fsdp"),
        P(None, "fsdp"),
        *([rows] * 9),
        P(),
    )
    out_specs = (
        *([tokens] * 3),
        rows,
        tokens,
        P("fsdp"),
        P(None, "fsdp"),
        *([rows] * 12),
        P(),
    )
    return jax.shard_map(local, mesh=mesh, in_specs=in_specs, out_specs=out_specs, check_vma=False)
```

time: 1570 us -> 1270 us (0.81)
  waiting for transfers between devices: 550 us -> 80.6 us
  Pallas kernels: 0 us -> 421 us
  starting transfers between devices: 234 us -> 75.6 us
  local copies, waits for them, and re-layouts: 266 us -> 219 us
  other arithmetic: 215 us -> 183 us
  matrix products: 290 us -> 261 us
    ppermute x116 -> x22, waiting for transfers between devices: 550 us -> 80.6 us  [swap(): return lax.ppermute(value, ('fsdp', 'seq'), pairs)]
    pallas_call x0 -> x6, Pallas kernels: none -> 421 us  [the longest x1 192 us: scatter(): pl.pallas_call(functools.partial(scatter_body, count, quad), out_shape=[j...]
    ppermute x116 -> x22, starting transfers between devices: 226 us -> 72.4 us  [swap(): return lax.ppermute(value, ('fsdp', 'seq'), pairs)]
    concatenate x16 -> x6, local copies, waits for them, and re-layouts: 64.4 us -> 8.44 us  [the longest x2 3.83 us: advance(): base = jnp.concatenate(cuts, axis=0)]
    unnamed x11 -> x9, other arithmetic: 24.4 us -> 0.79 us
    sub x0 -> x1, other arithmetic: none -> 23.4 us  [softmax_back(): prob_grad - jnp.sum(prob_grad * probs, axis=-1, keepdims=True)]
    convert_element_type x2 -> x9, local copies, waits for them, and re-layouts: 0.16 us -> 20.2 us  [the longest x2 13.4 us: finish_twins(): value = (dot_left_t(*own) + there.astype(f32)).astype(bf16)]
    dot_general x27, matrix products: 97.3 us -> 80.4 us  [dot_right_t(): lax.dot_general(left, right, (((1,), (1,)), ((), ())), preferred_element_...]
  transfers between devices with their start and end apart: 146 -> 43, of which waited for: 64 -> 7; matrix products, arithmetic and copies ran while one was open for 40% -> 41% of each run, Pallas kernels for 0% -> 2%
where the time goes in v1:
time: 1270 us; the launch traced here: 1260 us
  Pallas kernels  421 us (33%)
  matrix products  261 us (21%)
  local copies, waits for them, and re-layouts  219 us (17%)
  other arithmetic  183 us (14%)
  waiting for transfers between devices  80.6 us (6%)
  starting transfers between devices  75.6 us (6%)
  between operations  15.9 us (1%)
    pallas_call x1, Pallas kernels, scatter(): pl.pallas_call(functools.partial(scatter_body, count, quad), out_shape=[j...  192 us
    pallas_call x1, Pallas kernels, gather(): pl.pallas_call(functools.partial(gather_body, count, quad), out_shape=[ja...  185 us
    ppermute x22, waiting for transfers between devices, swap(): return lax.ppermute(value, ('fsdp', 'seq'), pairs)  80.6 us
    dot_general x27, matrix products, dot_right_t(): lax.dot_general(left, right, (((1,), (1,)), ((), ())), preferred_element_...  80.4 us
    dot_general x15, matrix products, dot_left_t(): lax.dot_general(left, right, (((0,), (0,)), ((), ())), preferred_element_...  73 us
    ppermute x22, starting transfers between devices, swap(): return lax.ppermute(value, ('fsdp', 'seq'), pairs)  72.4 us
    dot_general x23, matrix products, dot_plain(): return jnp.dot(left, right, preferred_element_type=f32)  66.2 us
    unnamed x537, local copies, waits for them, and re-layouts  64.2 us
  transfers between devices with their start and end apart: 43, of which 7 were waited for; matrix products, arithmetic and copies ran while one was open for 41% of the time, Pallas kernels for 2%

profile of v1, /device:TPU:0, one launch (start us, length us, event | category | flops | bytes accessed | tf_op | source)
XLA Modules:
  0.0 1256.3 jit_solution(755861554285632572)
XLA Ops:
  3.7 12.0 shard_map.500
  20.2 10.9 shard_map.501
  40.4 185.1 %shard_map.502 = (bf16[2,16,88,1408]{3,2,1,0:T(8,128)(2,1)}, bf16[2,16,88,2112]{3,2,1,0:T(8,128)(2,1)}, bf16[2,16,88,1408]{3,2,1,0:T(8,128)(2,1)}, bf16[2,16,88,...) custom-call(bf16[88,1408]{1,0:T(8,128)(2,1)} %get-tuple-element.87.refs_0_, bf16[88,2112]{1,0:T(8,128)(2,1)} %slice_select_fusion.1.refs_1_, ...), custom_call_target="tpu_custom_call" | custom-call | tf_op jit(solution)/shard_map/pallas_call | solution.py:219
  225.6 25.2 %collective-permute-start.1 = (bf16[88,3072]{1,0:T(8,128)(2,1)}, bf16[88,3072]{1,0:T(8,128)(2,1)}, u32[]{:S(2)}, u32[]{:S(2)}) collective-permute-start(bf16[88,3072]{1,0:T(8,128)(2,1)} %slice_select_fusion), channel_id=1, source_target_pairs={{0,8},{1,9},{2,10},{3,11},{4,12},{5,13},{6,14},{7,15},{8,0},{9,1},... | collective-permute-start | bytes 1622024 | tf_op jit(solution)/shard_map/ppermute | solution.py:393
  269.5 9.9 fusion.282
  300.7 11.2 collective-permute-start.4
  406.7 12.1 fusion.135
  452.4 30.9 %collective-permute-done.13 = bf16[1536,704]{0,1:T(8,128)(2,1)} collective-permute-done((bf16[1536,704]{0,1:T(8,128)(2,1)}, bf16[1536,704]{0,1:T(8,128)(2,1)}, u32[]{:S(2)}, u32[]{:S(2)}) %collective-permute-start.13) | collective-permute-done | bytes 2162720 | tf_op jit(solution)/shard_map/ppermute | solution.py:393
  491.6 13.5 %collective-permute-done.10 = bf16[352,3072]{1,0:T(8,128)(2,1)S(1)} collective-permute-done((bf16[352,3072]{1,0:T(8,128)(2,1)}, bf16[352,3072]{1,0:T(8,128)(2,1)S(1)}, u32[]{:S(2)}, u32[]{:S(2)}) %collective-permute-start.10) | collective-permute-done | bytes 2162720 | tf_op jit(solution)/shard_map/ppermute | solution.py:393
  521.7 10.5 collective-permute-done.18
  533.9 6.4 fusion.115
  540.3 9.8 fusion.112
  550.1 9.2 convolution_add_fusion.1
  560.1 11.0 fusion.29
  588.4 8.2 convolution_convert_fusion.1
  613.4 8.1 convolution_convert_fusion.2
  624.2 7.1 select_convert_fusion.1
  635.4 7.1 fusion.113
  642.5 7.7 fusion.111
  693.7 6.8 convert_element_type.516
  705.6 7.1 fusion.33
  771.1 7.5 fusion.31
  787.8 15.1 %collective-permute-done.27 = bf16[384,704]{0,1:T(8,128)(2,1)S(1)} collective-permute-done((bf16[384,704]{0,1:T(8,128)(2,1)S(1)}, bf16[384,704]{0,1:T(8,128)(2,1)S(1)}, u32[]{:S(2)}, u32[]{:S(2)}) %collective-permute-start.27) | collective-permute-done | bytes 540704 | tf_op jit(solution)/shard_map/ppermute | solution.py:393
  835.5 7.7 fusion.276
  844.4 11.1 collective-permute-start.30
  858.7 23.4 %multiply_convert_fusion.1 = bf16[2,16,128,256]{3,2,1,0:T(8,128)(2,1)} fusion(f32[2,16,128,256]{3,2,1,0:T(8,128)S(1)} %fusion.197, f32[2,16,128,256]{3,2,1,0:T(8,128)S(1)} %copy-done.85, f32[2,16,128]{2,1,0:T(8,128)S(1)} %copy-done.187), kind=kOutput, calls=%fused_computation.71 | output fusion | flops 6295807 | bytes 10502144 | tf_op jit(solution)/shard_map/sub | solution.py:77
  882.1 12.5 convolution_bitcast_fusion
  991.1 11.4 shard_map.503
  1013.2 9.5 shard_map.504
  1039.7 8.2 add_convert_fusion
  1047.9 9.0 copy.388
  1056.8 191.9 %shard_map.505 = (f32[2,88,1408]{2,1,0:T(8,128)}, f32[2,88,704]{2,1,0:T(8,128)}, f32[2,64,1408]{2,1,0:T(8,128)}, f32[2,88,2112]{2,1,0:T(8,128)}, f32[2,88,1408]{2,1,0:T(8,128)}) custom-call(bf16[16,88,1408]{2,1,0:T(8,128)(2,1)} %bitcast.439, bf16[16,88,704]{2,1,0:T(8,128)(2,1)} %bitcast.458, bf16[16,64,1408]{2,1,0:T(8,128)(2,1)} %bitcast.449, ...), custom_call_target="tpu_custom_call" | custom-call | tf_op jit(solution)/shard_map/pallas_call | solution.py:355
  (967 shorter events, 523.3 us)
Async XLA Ops:
  225.6 150.2 %collective-permute-start.1 = (bf16[88,3072]{1,0:T(8,128)(2,1)}, bf16[88,3072]{1,0:T(8,128)(2,1)}, u32[]{:S(2)}, u32[]{:S(2)}) collective-permute-start(bf16[88,3072]{1,0:T(8,128)(2,1)} %slice_select_fusion), channel_id=1, source_target_pairs={{0,8},{1,9},{2,10},{3,11},{4,12},{5,13},{6,14},{7,15},{8,0},{9,1},... | collective-permute-start | bytes 1622024 | tf_op jit(solution)/shard_map/ppermute | solution.py:393
  250.8 126.0 %collective-permute-start.2 = (bf16[88,3072]{1,0:T(8,128)(2,1)}, bf16[88,3072]{1,0:T(8,128)(2,1)}, u32[]{:S(2)}, u32[]{:S(2)}) collective-permute-start(bf16[88,3072]{1,0:T(8,128)(2,1)} %slice_select_fusion), channel_id=1, source_target_pairs={{0,16},{1,17},{2,18},{3,19},{4,20},{5,21},{6,22},{7,23},{8,24},{9,... | collective-permute-start | bytes 1622024 | tf_op jit(solution)/shard_map/ppermute | solution.py:393
  250.8 128.4 %collective-permute-start.3 = (bf16[88,3072]{1,0:T(8,128)(2,1)}, bf16[88,3072]{1,0:T(8,128)(2,1)}, u32[]{:S(2)}, u32[]{:S(2)}) collective-permute-start(bf16[88,3072]{1,0:T(8,128)(2,1)} %slice_select_fusion), channel_id=1, source_target_pairs={{0,24},{1,25},{2,26},{3,27},{4,28},{5,29},{6,30},{7,31},{8,16},{9,... | collective-permute-start | bytes 1622024 | tf_op jit(solution)/shard_map/ppermute | solution.py:393
  300.7 87.6 %collective-permute-start = (bf16[256,2816]{0,1:T(8,128)(2,1)}, bf16[256,2816]{0,1:T(8,128)(2,1)}, u32[]{:S(2)}, u32[]{:S(2)}) collective-permute-start(bf16[256,2816]{0,1:T(8,128)(2,1)} %pad_maximum_fusion.22), channel_id=1, source_target_pairs={{0,1},{1,0},{2,3},{3,2},{4,5},{5,4},{6,7},{7,6},{8,9},{9,8},{10,11... | collective-permute-start | bytes 4325384 | tf_op jit(solution)/shard_map/ppermute | solution.py:396
  300.7 122.6 %collective-permute-start.4 = (bf16[384,704]{0,1:T(8,128)(2,1)}, bf16[384,704]{0,1:T(8,128)(2,1)}, u32[]{:S(2)}, u32[]{:S(2)}) collective-permute-start(bf16[384,704]{0,1:T(8,128)(2,1)} %broadcast_select_fusion.12), channel_id=1, source_target_pairs={{0,8},{1,9},{2,10},{3,11},{4,12},{5,13},{6,14},{7,15},{8,0},{9,1},... | collective-permute-start | bytes 1622024 | tf_op jit(solution)/shard_map/ppermute | solution.py:393
  375.8 47.6 %collective-permute-start.5 = (bf16[384,704]{0,1:T(8,128)(2,1)}, bf16[384,704]{0,1:T(8,128)(2,1)S(1)}, u32[]{:S(2)}, u32[]{:S(2)}) collective-permute-start(bf16[384,704]{0,1:T(8,128)(2,1)} %broadcast_select_fusion.12), channel_id=1, source_target_pairs={{0,16},{1,17},{2,18},{3,19},{4,20},{5,21},{6,22},{7,23},{8,24},{9,... | collective-permute-start | bytes 1622024 | tf_op jit(solution)/shard_map/ppermute | solution.py:393
  376.8 46.6 %collective-permute-start.6 = (bf16[384,704]{0,1:T(8,128)(2,1)}, bf16[384,704]{0,1:T(8,128)(2,1)}, u32[]{:S(2)}, u32[]{:S(2)}) collective-permute-start(bf16[384,704]{0,1:T(8,128)(2,1)} %broadcast_select_fusion.12), channel_id=1, source_target_pairs={{0,24},{1,25},{2,26},{3,27},{4,28},{5,29},{6,30},{7,31},{8,16},{9,... | collective-permute-start | bytes 1622024 | tf_op jit(solution)/shard_map/ppermute | solution.py:393
  386.8 60.8 %collective-permute-start.7 = (bf16[352,3072]{1,0:T(8,128)(2,1)}, bf16[352,3072]{1,0:T(8,128)(2,1)}, u32[]{:S(2)}, u32[]{:S(2)}) collective-permute-start(bf16[352,3072]{1,0:T(8,128)(2,1)} %constant_dynamic-update-slice_fusion), channel_id=1, source_target_pairs={{0,2},{1,5},{2,0},{3,7},{4,6},{5,1},{6,4},{7,3},{8,10},{9,13},{10,... | collective-permute-start | bytes 6488072 | tf_op jit(solution)/shard_map/ppermute | solution.py:393
  388.3 59.3 %collective-permute-start.8 = (bf16[352,3072]{1,0:T(8,128)(2,1)}, bf16[352,3072]{1,0:T(8,128)(2,1)}, u32[]{:S(2)}, u32[]{:S(2)}) collective-permute-start(bf16[352,3072]{1,0:T(8,128)(2,1)} %constant_dynamic-update-slice_fusion), channel_id=1, source_target_pairs={{0,4},{1,3},{2,6},{3,1},{4,0},{5,7},{6,2},{7,5},{8,12},{9,11},{10,... | collective-permute-start | bytes 6488072 | tf_op jit(solution)/shard_map/ppermute | solution.py:393
  430.6 52.7 %collective-permute-start.13 = (bf16[1536,704]{0,1:T(8,128)(2,1)}, bf16[1536,704]{0,1:T(8,128)(2,1)}, u32[]{:S(2)}, u32[]{:S(2)}) collective-permute-start(bf16[1536,704]{0,1:T(8,128)(2,1)} %constant_dynamic-update-slice_fusion.4), channel_id=1, source_target_pairs={{0,2},{1,5},{2,0},{3,7},{4,6},{5,1},{6,4},{7,3},{8,10},{9,13},{10,... | collective-permute-start | bytes 6488072 | tf_op jit(solution)/shard_map/ppermute | solution.py:393
  431.8 59.9 %collective-permute-start.14 = (bf16[1536,704]{0,1:T(8,128)(2,1)}, bf16[1536,704]{0,1:T(8,128)(2,1)}, u32[]{:S(2)}, u32[]{:S(2)}) collective-permute-start(bf16[1536,704]{0,1:T(8,128)(2,1)} %constant_dynamic-update-slice_fusion.4), channel_id=1, source_target_pairs={{0,4},{1,3},{2,6},{3,1},{4,0},{5,7},{6,2},{7,5},{8,12},{9,11},{10,... | collective-permute-start | bytes 6488072 | tf_op jit(solution)/shard_map/ppermute | solution.py:393
  447.6 44.1 %collective-permute-start.15 = (bf16[1536,704]{0,1:T(8,128)(2,1)}, bf16[1536,704]{0,1:T(8,128)(2,1)S(1)}, u32[]{:S(2)}, u32[]{:S(2)}) collective-permute-start(bf16[1536,704]{0,1:T(8,128)(2,1)} %constant_dynamic-update-slice_fusion.4), channel_id=1, source_target_pairs={{0,1},{1,0},{2,3},{3,2},{4,5},{5,4},{6,7},{7,6},{8,9},{9,8},{10,11... | collective-permute-start | bytes 6488072 | tf_op jit(solution)/shard_map/ppermute | solution.py:396
  447.7 57.5 %collective-permute-start.10 = (bf16[352,3072]{1,0:T(8,128)(2,1)}, bf16[352,3072]{1,0:T(8,128)(2,1)S(1)}, u32[]{:S(2)}, u32[]{:S(2)}) collective-permute-start(bf16[352,3072]{1,0:T(8,128)(2,1)} %collective-permute-done.7), channel_id=1, source_target_pairs={{0,4},{1,3},{2,6},{3,1},{4,0},{5,7},{6,2},{7,5},{8,12},{9,11},{10,... | collective-permute-start | bytes 6488072 | tf_op jit(solution)/shard_map/ppermute | solution.py:393
  448.9 56.2 %collective-permute-start.11 = (bf16[352,3072]{1,0:T(8,128)(2,1)}, bf16[352,3072]{1,0:T(8,128)(2,1)S(1)}, u32[]{:S(2)}, u32[]{:S(2)}) collective-permute-start(bf16[352,3072]{1,0:T(8,128)(2,1)} %collective-permute-done.7), channel_id=1, source_target_pairs={{0,1},{1,0},{2,3},{3,2},{4,5},{5,4},{6,7},{7,6},{8,9},{9,8},{10,11... | collective-permute-start | bytes 6488072 | tf_op jit(solution)/shard_map/ppermute | solution.py:396
  505.1 27.1 %collective-permute-start.18 = (bf16[1536,704]{0,1:T(8,128)(2,1)}, bf16[1536,704]{0,1:T(8,128)(2,1)}, u32[]{:S(2)}, u32[]{:S(2)}) collective-permute-start(bf16[1536,704]{0,1:T(8,128)(2,1)} %collective-permute-done.13), channel_id=1, source_target_pairs={{0,4},{1,3},{2,6},{3,1},{4,0},{5,7},{6,2},{7,5},{8,12},{9,11},{10,... | collective-permute-start | bytes 6488072 | tf_op jit(solution)/shard_map/ppermute | solution.py:393
  506.5 27.3 %collective-permute-start.16 = (bf16[352,3072]{1,0:T(8,128)(2,1)S(1)}, bf16[352,3072]{1,0:T(8,128)(2,1)}, u32[]{:S(2)}, u32[]{:S(2)}) collective-permute-start(bf16[352,3072]{1,0:T(8,128)(2,1)S(1)} %collective-permute-done.10), channel_id=1, source_target_pairs={{0,1},{1,0},{2,3},{3,2},{4,5},{5,4},{6,7},{7,6},{8,9},{9,8},{10,11... | collective-permute-start | bytes 6488072 | tf_op jit(solution)/shard_map/ppermute | solution.py:396
  577.9 46.3 %collective-permute-start.17 = (bf16[6144,704]{0,1:T(8,128)(2,1)}, bf16[6144,704]{0,1:T(8,128)(2,1)}, u32[]{:S(2)}, u32[]{:S(2)}) collective-permute-start(bf16[6144,704]{0,1:T(8,128)(2,1)} %convolution_convert_fusion.3), channel_id=1, source_target_pairs={{0,1},{1,0},{2,3},{3,2},{4,5},{5,4},{6,7},{7,6},{8,9},{9,8},{10,11... | collective-permute-start | bytes 25952264 | tf_op jit(solution)/shard_map/ppermute | solution.py:396
  596.6 57.8 %collective-permute-start.22 = (bf16[1408,3072]{1,0:T(8,128)(2,1)}, bf16[1408,3072]{1,0:T(8,128)(2,1)}, u32[]{:S(2)}, u32[]{:S(2)}) collective-permute-start(bf16[1408,3072]{1,0:T(8,128)(2,1)} %convolution_convert_fusion.1), channel_id=1, source_target_pairs={{0,1},{1,0},{2,3},{3,2},{4,5},{5,4},{6,7},{7,6},{8,9},{9,8},{10,11... | collective-permute-start | bytes 25952264 | tf_op jit(solution)/shard_map/ppermute | solution.py:396
  634.2 50.2 %collective-permute-start.23 = (bf16[3072,704]{0,1:T(8,128)(2,1)}, bf16[3072,704]{0,1:T(8,128)(2,1)}, u32[]{:S(2)}, u32[]{:S(2)}) collective-permute-start(bf16[3072,704]{0,1:T(8,128)(2,1)} %pad_maximum_fusion.4), channel_id=1, source_target_pairs={{0,4},{1,3},{2,6},{3,1},{4,0},{5,7},{6,2},{7,5},{8,12},{9,11},{10,... | collective-permute-start | bytes 12976136 | tf_op jit(solution)/shard_map/ppermute | solution.py:393
  673.7 76.7 %collective-permute-start.24 = (bf16[704,3072]{1,0:T(8,128)(2,1)}, bf16[704,3072]{1,0:T(8,128)(2,1)}, u32[]{:S(2)}, u32[]{:S(2)}) collective-permute-start(bf16[704,3072]{1,0:T(8,128)(2,1)} %pad_maximum_fusion.5), channel_id=1, source_target_pairs={{0,4},{1,3},{2,6},{3,1},{4,0},{5,7},{6,2},{7,5},{8,12},{9,11},{10,... | collective-permute-start | bytes 12976136 | tf_op jit(solution)/shard_map/ppermute | solution.py:393
  714.0 39.5 %collective-permute-start.25 = (bf16[1536,704]{0,1:T(8,128)(2,1)}, bf16[1536,704]{0,1:T(8,128)(2,1)}, u32[]{:S(2)}, u32[]{:S(2)}) collective-permute-start(bf16[1536,704]{0,1:T(8,128)(2,1)} %fusion.33), channel_id=1, source_target_pairs={{0,2},{1,5},{2,0},{3,7},{4,6},{5,1},{6,4},{7,3},{8,10},{9,13},{10,... | collective-permute-start | bytes 6488072 | tf_op jit(solution)/shard_map/ppermute | solution.py:393
  723.8 80.5 %collective-permute-start.37 = (bf16[1408,704]{0,1:T(8,128)(2,1)}, bf16[1408,704]{0,1:T(8,128)(2,1)}, u32[]{:S(2)}, u32[]{:S(2)}) collective-permute-start(bf16[1408,704]{0,1:T(8,128)(2,1)} %convolution_convert_fusion.8), channel_id=1, source_target_pairs={{0,1},{1,0},{2,3},{3,2},{4,5},{5,4},{6,7},{7,6},{8,9},{9,8},{10,11... | collective-permute-start | bytes 5947400 | tf_op jit(solution)/shard_map/ppermute | solution.py:396
  763.7 39.2 %collective-permute-start.27 = (bf16[384,704]{0,1:T(8,128)(2,1)S(1)}, bf16[384,704]{0,1:T(8,128)(2,1)S(1)}, u32[]{:S(2)}, u32[]{:S(2)}) collective-permute-start(bf16[384,704]{0,1:T(8,128)(2,1)S(1)} %get-tuple-element.315), channel_id=1, source_target_pairs={{0,16},{1,17},{2,18},{3,19},{4,20},{5,21},{6,22},{7,23},{8,24},{9,... | collective-permute-start | bytes 1622024 | tf_op jit(solution)/shard_map/ppermute | solution.py:393
  765.2 37.8 %collective-permute-start.28 = (bf16[384,704]{0,1:T(8,128)(2,1)S(1)}, bf16[384,704]{0,1:T(8,128)(2,1)S(1)}, u32[]{:S(2)}, u32[]{:S(2)}) collective-permute-start(bf16[384,704]{0,1:T(8,128)(2,1)S(1)} %get-tuple-element.314), channel_id=1, source_target_pairs={{0,24},{1,25},{2,26},{3,27},{4,28},{5,29},{6,30},{7,31},{8,16},{9,... | collective-permute-start | bytes 1622024 | tf_op jit(solution)/shard_map/ppermute | solution.py:393
  778.6 56.8 %collective-permute-start.29 = (bf16[352,3072]{1,0:T(8,128)(2,1)}, bf16[352,3072]{1,0:T(8,128)(2,1)}, u32[]{:S(2)}, u32[]{:S(2)}) collective-permute-start(bf16[352,3072]{1,0:T(8,128)(2,1)} %fusion.31), channel_id=1, source_target_pairs={{0,2},{1,5},{2,0},{3,7},{4,6},{5,1},{6,4},{7,3},{8,10},{9,13},{10,... | collective-permute-start | bytes 6488072 | tf_op jit(solution)/shard_map/ppermute | solution.py:393
  787.8 111.9 %collective-permute-start.38 = (bf16[1024,1408]{1,0:T(8,128)(2,1)}, bf16[1024,1408]{1,0:T(8,128)(2,1)}, u32[]{:S(2)}, u32[]{:S(2)}) collective-permute-start(bf16[1024,1408]{1,0:T(8,128)(2,1)} %convolution_convert_fusion.7), channel_id=1, source_target_pairs={{0,1},{1,0},{2,3},{3,2},{4,5},{5,4},{6,7},{7,6},{8,9},{9,8},{10,11... | collective-permute-start | bytes 8650760 | tf_op jit(solution)/shard_map/ppermute | solution.py:396
  817.1 97.7 %collective-permute-start.36 = (bf16[1408,1408]{1,0:T(8,128)(2,1)}, bf16[1408,1408]{1,0:T(8,128)(2,1)}, u32[]{:S(2)}, u32[]{:S(2)}) collective-permute-start(bf16[1408,1408]{1,0:T(8,128)(2,1)} %convolution_convert_fusion.6), channel_id=1, source_target_pairs={{0,1},{1,0},{2,3},{3,2},{4,5},{5,4},{6,7},{7,6},{8,9},{9,8},{10,11... | collective-permute-start | bytes 11894792 | tf_op jit(solution)/shard_map/ppermute | solution.py:396
  844.4 59.7 %collective-permute-start.30 = (bf16[88,3072]{1,0:T(8,128)(2,1)}, bf16[88,3072]{1,0:T(8,128)(2,1)}, u32[]{:S(2)}, u32[]{:S(2)}) collective-permute-start(bf16[88,3072]{1,0:T(8,128)(2,1)} %get-tuple-element.313), channel_id=1, source_target_pairs={{0,8},{1,9},{2,10},{3,11},{4,12},{5,13},{6,14},{7,15},{8,0},{9,1},... | collective-permute-start | bytes 1622024 | tf_op jit(solution)/shard_map/ppermute | solution.py:393
  855.5 48.6 %collective-permute-start.31 = (bf16[88,3072]{1,0:T(8,128)(2,1)}, bf16[88,3072]{1,0:T(8,128)(2,1)}, u32[]{:S(2)}, u32[]{:S(2)}) collective-permute-start(bf16[88,3072]{1,0:T(8,128)(2,1)} %get-tuple-element.312), channel_id=1, source_target_pairs={{0,16},{1,17},{2,18},{3,19},{4,20},{5,21},{6,22},{7,23},{8,24},{9,... | collective-permute-start | bytes 1622024 | tf_op jit(solution)/shard_map/ppermute | solution.py:393
  855.5 48.6 %collective-permute-start.32 = (bf16[88,3072]{1,0:T(8,128)(2,1)}, bf16[88,3072]{1,0:T(8,128)(2,1)}, u32[]{:S(2)}, u32[]{:S(2)}) collective-permute-start(bf16[88,3072]{1,0:T(8,128)(2,1)} %get-tuple-element.311), channel_id=1, source_target_pairs={{0,24},{1,25},{2,26},{3,27},{4,28},{5,29},{6,30},{7,31},{8,16},{9,... | collective-permute-start | bytes 1622024 | tf_op jit(solution)/shard_map/ppermute | solution.py:393
  982.2 57.5 %collective-permute-start.39 = (bf16[1408,2112]{0,1:T(8,128)(2,1)}, bf16[1408,2112]{0,1:T(8,128)(2,1)}, u32[]{:S(2)}, u32[]{:S(2)}) collective-permute-start(bf16[1408,2112]{0,1:T(8,128)(2,1)} %convolution_convert_fusion), channel_id=1, source_target_pairs={{0,1},{1,0},{2,3},{3,2},{4,5},{5,4},{6,7},{7,6},{8,9},{9,8},{10,11... | collective-permute-start | bytes 17842184 | tf_op jit(solution)/shard_map/ppermute | solution.py:396
  988.7 45.3 %collective-permute-start.40 = (bf16[1408,1408]{1,0:T(8,128)(2,1)}, bf16[1408,1408]{1,0:T(8,128)(2,1)}, u32[]{:S(2)}, u32[]{:S(2)}) collective-permute-start(bf16[1408,1408]{1,0:T(8,128)(2,1)} %convolution_convert_fusion.5), channel_id=1, source_target_pairs={{0,1},{1,0},{2,3},{3,2},{4,5},{5,4},{6,7},{7,6},{8,9},{9,8},{10,11... | collective-permute-start | bytes 11894792 | tf_op jit(solution)/shard_map/ppermute | solution.py:396
  (251 other events, 3443.8 us)

commit v2 on v1

--- a/solution.py
+++ b/solution.py
@@ -24,29 +24,6 @@
     center = values - jnp.mean(values, axis=-1, keepdims=True)
     spread = jnp.mean(center * center, axis=-1, keepdims=True)
     return center * lax.rsqrt(spread + norm_eps)
-
-
-def rotary_tables(row_pos, col_pos, head_dim):
-    quarter = head_dim // 4
-    freqs = 10000.0 ** (-jnp.arange(quarter, dtype=f32) / quarter)
-    row_angle = row_pos.astype(f32)[:, None] * freqs[None, :]
-    col_angle = col_pos.astype(f32)[:, None] * freqs[None, :]
-    angles = jnp.stack([row_angle, col_angle], axis=1)
-    return (jnp.cos(angles), jnp.sin(angles))
-
-
-def rotate(values, cosine_table, sine_table):
-    rows, tokens, heads, head_dim = values.shape
-    quarter = head_dim // 4
-    pieces = values.reshape(rows, tokens, heads, 2, 2, quarter)
-    former = pieces[..., 0, :]
-    latter = pieces[..., 1, :]
-    cos_wide = cosine_table[None, :, None, :, :]
-    sin_wide = sine_table[None, :, None, :, :]
-    turned = jnp.stack(
-        [former * cos_wide - latter * sin_wide, latter * cos_wide + former * sin_wide], axis=4
-    )
-    return turned.reshape(rows, tokens, heads, head_dim)
 
 
 def gained_norm(values, gain):
@@ -251,6 +228,8 @@
         )
 
     def block(w, q):
+        if len(source[w].shape) == 4:
+            return source[w].at[:, q]
         return source[w].at[pl.ds(4 * q, 4)]
 
     def give(w, n):
@@ -347,7 +326,7 @@
 
 def scatter(sums, quad, identity):
     count = len(sums)
-    shapes = [s.shape[1:] for s in sums]
+    shapes = [s.shape[-2:] for s in sums]
 
     def buffers(*lead):
         return [pltpu.VMEM((*lead, *s), bf16) for s in shapes]
@@ -371,6 +350,374 @@
             collective_id=identity, has_side_effects=True, vmem_limit_bytes=56 * 2**20
         ),
     )(*sums)
+
+
+def gelu_parts(value):
+    inner = 0.7978845608028654 * (value + 0.044715 * value * value * value)
+    return jnp.tanh(inner)
+
+
+def gelu_of(value):
+    return 0.5 * value * (1.0 + gelu_parts(value))
+
+
+class GatherPlan:
+    def __init__(self, mine, out, send, recv, local):
+        self.mine, self.out = mine, out
+        self.send, self.recv, self.local = send, recv, local
+        self.core, self.first_mask, self.second_mask, self.at, self.sibling = neighbours(4)
+        self.far_peers = [self.at(4 * k) for k in range(1, 4)]
+
+    def peers(self):
+        return [*self.far_peers, self.at(self.first_mask), self.at(self.second_mask), self.sibling]
+
+    def copy(self, w, slot, source, target, peer):
+        return pltpu.make_async_remote_copy(
+            src_ref=source,
+            dst_ref=target,
+            send_sem=self.send.at[w, slot],
+            recv_sem=self.recv.at[w, slot],
+            device_id=peer,
+            device_id_type=MESH,
+        )
+
+    def block(self, w, q):
+        return self.out[w].at[self.core, :, q]
+
+    def far(self, w, k):
+        return self.copy(
+            w, k - 1, self.mine[w], self.out[w].at[self.core, k, 0], self.far_peers[k - 1]
+        )
+
+    def keep(self, w):
+        return pltpu.make_async_copy(
+            self.mine[w], self.out[w].at[self.core, 0, 0], self.local.at[w]
+        )
+
+    def first(self, w):
+        mask = self.first_mask
+        return self.copy(w, 3, self.block(w, 0), self.block(w, mask), self.at(mask))
+
+    def second(self, w):
+        mask = self.second_mask
+        return self.copy(w, 4, self.block(w, 0), self.block(w, mask), self.at(mask))
+
+    def both(self, w):
+        return self.copy(
+            w, 5, self.block(w, self.first_mask), self.block(w, 3), self.at(self.second_mask)
+        )
+
+    def twin(self, w, n):
+        q = (0, self.first_mask, self.second_mask, 3)[n]
+        return self.copy(w, 6 + n, self.block(w, q), self.block(w, q), self.sibling)
+
+    def begin(self, w):
+        self.keep(w).start()
+        for k in range(1, 4):
+            self.far(w, k).start()
+
+    def spread(self, w):
+        self.keep(w).wait()
+        for k in range(1, 4):
+            self.far(w, k).wait_recv()
+        self.first(w).start()
+        self.second(w).start()
+        self.twin(w, 0).start()
+
+    def cross(self, w):
+        self.first(w).wait_recv()
+        self.both(w).start()
+        self.twin(w, 1).start()
+        self.second(w).wait_recv()
+        self.twin(w, 2).start()
+
+    def close(self, w):
+        self.both(w).wait_recv()
+        self.twin(w, 3).start()
+
+    def ready(self, w):
+        for n in range(4):
+            self.twin(w, n).wait_recv()
+
+    def finish(self, w):
+        for k in range(1, 4):
+            self.far(w, k).wait_send()
+        self.first(w).wait_send()
+        self.second(w).wait_send()
+        self.both(w).wait_send()
+        for n in range(4):
+            self.twin(w, n).wait_send()
+
+
+def stream(weight, tiles, buffer, semaphore, body):
+    depth = buffer.shape[0]
+    height = weight.shape[3]
+
+    def copy(index):
+        half, start, size = tiles[index]
+        slot = index % depth
+        return pltpu.make_async_copy(
+            weight.at[half, :, :, :, pl.ds(start, size)],
+            buffer.at[slot, :, :, pl.ds(0, height), pl.ds(0, size)],
+            semaphore.at[slot],
+        )
+
+    for index in range(min(depth - 1, len(tiles))):
+        copy(index).start()
+    for index, (_, _, size) in enumerate(tiles):
+        if index + depth - 1 < len(tiles):
+            copy(index + depth - 1).start()
+        copy(index).wait()
+        body(index, buffer[index % depth, :, :, :height, :size].reshape(16 * height, size))
+
+
+def tiles_of(width, size, halves=(0, 1)):
+    return [
+        (half, start, min(size, width - start)) for half in halves for start in range(0, width, size)
+    ]
+
+
+def forward_body(batch, scaling, *refs):
+    refs = list(refs)
+    take = refs.pop
+    latent, skip, skip_gain, gains, shift = (take(0) for _ in range(5))
+    order, order_skip, heads_ref = (take(0) for _ in range(3))
+    tables = [take(0) for _ in range(3)]
+    text, valid = take(0), take(0)
+    mine = [take(0) for _ in range(7)]
+    out = [take(0) for _ in range(7)]
+    normed, hidden, attn_in, qkv, keyval_here, keyval_there = (take(0) for _ in range(6))
+    attn_cat, after_self, cross_in, cq_proj, ckey_mine, cross_keyval = (take(0) for _ in range(6))
+    cross_cat, after_cross, mlp_in, upper, activated = (take(0) for _ in range(5))
+    self_peak, cross_peak = take(0), take(0)
+    wide, narrow, buffer, semaphore, send, recv, local, twin_send, twin_recv = refs
+    rows, width = hidden.shape
+    size = rows // batch
+    me = lax.axis_index("fsdp")
+    core = lax.axis_index("seq")
+    plan = GatherPlan(mine, out, send, recv, local)
+    skip_w, qkv_w, pair_w, query_w, keyval_w, up_w, down_w = range(7)
+
+    greet(plan.peers())
+    for w in range(7):
+        plan.begin(w)
+
+    def each(body):
+        for b in range(batch):
+            body(b, pl.ds(b * size, size))
+
+    def reorder(value):
+        return dot_plain(value, order[...]).astype(bf16)
+
+    upper_half = me >= 8
+
+    def normed_part(b, rows_b):
+        left = latent[rows_b, :].astype(f32)
+        right = skip[rows_b, :].astype(f32)
+        mean = (
+            jnp.sum(left, axis=1, keepdims=True) + jnp.sum(right, axis=1, keepdims=True)
+        ) / (2 * width)
+        left, right = left - mean, right - mean
+        spread = (
+            jnp.sum(left * left, axis=1, keepdims=True)
+            + jnp.sum(right * right, axis=1, keepdims=True)
+        ) / (2 * width)
+        factor = lax.rsqrt(spread + norm_eps)
+        left = (left * factor * skip_gain[:, :width]).astype(bf16)
+        right = (right * factor * skip_gain[:, width:]).astype(bf16)
+        near = jnp.where(upper_half, right, left)
+        away = jnp.where(upper_half, left, right)
+        for half in range(2):
+            normed[half, 0, rows_b, :] = dot_plain(near, order_skip[half]).astype(bf16)
+            normed[half, 1, rows_b, :] = dot_plain(away, order_skip[half]).astype(bf16)
+
+    each(normed_part)
+    plan.spread(skip_w)
+    plan.spread(qkv_w)
+    plan.cross(skip_w)
+    plan.spread(pair_w)
+    plan.cross(qkv_w)
+    plan.close(skip_w)
+    plan.ready(skip_w)
+
+    skip_tiles = tiles_of(width, 512)
+
+    def skip_product(index, tile):
+        half, start, extent = skip_tiles[index]
+        cut = tile.shape[0] // 2
+        value = dot_plain(normed[half, 0], tile[:cut]) + dot_plain(normed[half, 1], tile[cut:])
+        lanes = pl.ds(start, extent)
+        if half == 0:
+            hidden[:, lanes] = value
+        else:
+            hidden[:, lanes] += value
+
+    stream(out[skip_w], skip_tiles, buffer, semaphore, skip_product)
+
+    def attn_in_part(b, rows_b):
+        value = layer_norm(hidden[rows_b, :]) * gains[0:1, :] + shift[b : b + 1, :]
+        attn_in[rows_b, :] = reorder(value.astype(bf16))
+
+    each(attn_in_part)
+    plan.spread(query_w)
+    plan.cross(pair_w)
+    plan.close(qkv_w)
+    plan.ready(qkv_w)
+
+    qkv_tiles = tiles_of(out[qkv_w].shape[4], 512)
+
+    def qkv_product(index, tile):
+        half, start, extent = qkv_tiles[index]
+        value = dot_plain(attn_in[...], tile)
+        for at in range(0, extent, 128):
+            lane = start + at
+            piece = value[:, at : at + 128]
+            if lane < width:
+                qkv[:, pl.ds(half * width + lane, 128)] = piece
+            else:
+                place = lane - width + half * 768
+                if place < width:
+                    keyval_here[:, pl.ds(width + place, 128)] = piece.astype(bf16)
+
+    stream(out[qkv_w], qkv_tiles, buffer, semaphore, qkv_product)
+
+    def key_part(b, rows_b):
+        value, _ = head_norm(qkv[rows_b, pl.ds(width, width)], heads_ref)
+        keyval_here[rows_b, pl.ds(0, width)] = turn(value, tables).astype(bf16)
+
+    each(key_part)
+    exchange = pltpu.make_async_remote_copy(
+        src_ref=keyval_here,
+        dst_ref=keyval_there,
+        send_sem=twin_send,
+        recv_sem=twin_recv,
+        device_id=plan.sibling,
+        device_id_type=MESH,
+    )
+    exchange.start()
+
+    def query_part(b, rows_b):
+        value, _ = head_norm(qkv[rows_b, pl.ds(0, width)], heads_ref)
+        narrow[rows_b, :] = turn(value, tables).astype(bf16)
+
+    each(query_part)
+    plan.spread(keyval_w)
+    plan.cross(query_w)
+    plan.close(pair_w)
+    exchange.wait()
+
+    def attend(sources, peak, target, masked):
+        peak[...] = jnp.full_like(peak, masked_value)
+        wide[...] = jnp.zeros_like(wide)
+
+        @pl.loop(0, batch)
+        def _(b):
+            rows_b = pl.ds(pl.multiple_of(b * size, size), size)
+            for head in range(HEADS):
+                lanes, inside = window_of(head, width)
+                query = narrow[rows_b, lanes] * inside.astype(bf16)
+                scores = dot_right_t(query, pair_rows(sources, b, size, lanes)) * scaling
+                if masked:
+                    scores = jnp.where(valid[pl.ds(b, 1), :] > 0.5, scores, masked_value)
+                probs, largest = softmax_of(scores)
+                largest = jnp.max(largest, axis=0, keepdims=True)
+                peak[head : head + 1, :] = jnp.maximum(
+                    peak[head : head + 1, :], jnp.broadcast_to(largest, (1, 128))
+                )
+                value = pair_rows(sources, b, size, shift_lanes(lanes, width))
+                wide[rows_b, lanes] += dot_plain(probs.astype(bf16), value) * inside
+
+        target[...] = reorder(wide[...].astype(bf16))
+
+    attend([keyval_here, keyval_there], self_peak, attn_cat, False)
+    plan.ready(pair_w)
+    pair_tiles = tiles_of(width, 512)
+
+    def out_product(source, before, after):
+        def body(index, tile):
+            lanes = pl.ds(pair_tiles[index][1], pair_tiles[index][2])
+            after[:, lanes] = before[:, lanes] + dot_plain(source[...], tile)
+
+        return body
+
+    pair_body = out_product(attn_cat, hidden, after_self)
+    stream(out[pair_w], tiles_of(width, 512, (0,)), buffer, semaphore, pair_body)
+
+    def cross_in_part(b, rows_b):
+        value = layer_norm(after_self[rows_b, :]) * gains[1:2, :]
+        cross_in[rows_b, :] = reorder(value.astype(bf16))
+
+    each(cross_in_part)
+    plan.spread(up_w)
+    plan.cross(keyval_w)
+    plan.close(query_w)
+    plan.ready(query_w)
+    query_tiles = tiles_of(out[query_w].shape[4], 512)
+
+    def query_product(index, tile):
+        half, start, extent = query_tiles[index]
+        place = half * out[query_w].shape[4] + start
+        extent = min(extent, width - place)
+        cq_proj[:, pl.ds(place, extent)] = dot_plain(cross_in[...], tile)[:, :extent]
+
+    stream(out[query_w], query_tiles, buffer, semaphore, query_product)
+
+    def cross_query_part(b, rows_b):
+        narrow[rows_b, :] = head_norm(cq_proj[rows_b, :], heads_ref)[0].astype(bf16)
+
+    each(cross_query_part)
+    plan.spread(down_w)
+    plan.close(keyval_w)
+    plan.ready(keyval_w)
+    keyval_tiles = tiles_of(width, 512)
+
+    def keyval_product(index, tile):
+        half, start, extent = keyval_tiles[index]
+        value = dot_plain(text[...], tile)
+        if half == 0:
+            upper[:, pl.ds(start, extent)] = value[:rows]
+            upper[:, pl.ds(width + start, extent)] = value[rows:]
+        else:
+            cross_keyval[:, pl.ds(width + start, extent)] = value.astype(bf16)
+
+    stream(out[keyval_w], keyval_tiles, buffer, semaphore, keyval_product)
+    for b in range(batch):
+        for at in range(2):
+            part = pl.ds(at * size, size)
+            lanes = pl.ds(b * width, width)
+            cross_keyval[pl.ds(b * 2 * size + at * size, size), pl.ds(0, width)] = head_norm(
+                upper[part, lanes], heads_ref
+            )[0].astype(bf16)
+        ckey_mine[pl.ds(b * size, size), :] = upper[
+            pl.ds(pl.multiple_of(core * size, size), size), pl.ds(b * width, width)
+        ]
+    attend([cross_keyval], cross_peak, cross_cat, True)
+    pair_body = out_product(cross_cat, after_self, after_cross)
+    stream(out[pair_w], tiles_of(width, 512, (1,)), buffer, semaphore, pair_body)
+
+    def mlp_in_part(b, rows_b):
+        value = layer_norm(after_cross[rows_b, :]) * gains[2:3, :]
+        mlp_in[rows_b, :] = reorder(value.astype(bf16))
+
+    each(mlp_in_part)
+    plan.cross(up_w)
+    plan.close(up_w)
+    plan.ready(up_w)
+    block = activated.shape[1] // 16
+    up_tiles = tiles_of(out[up_w].shape[4], block)
+
+    def up_product(index, tile):
+        value = dot_plain(mlp_in[...], tile)
+        upper[:, pl.ds(index * block, block)] = value
+        slot = jnp.bitwise_xor(me, index)
+        activated[:, pl.ds(pl.multiple_of(slot * block, block), block)] = gelu_of(value).astype(bf16)
+
+    stream(out[up_w], up_tiles, buffer, semaphore, up_product)
+    plan.cross(down_w)
+    plan.close(down_w)
+    plan.ready(down_w)
+    for w in range(7):
+        plan.finish(w)
 
 
 class Links:
@@ -637,6 +984,228 @@
     return value
 
 
+def parts_of(value):
+    high = value.astype(bf16)
+    return high, (value - high.astype(f32)).astype(bf16)
+
+
+def sum_heads(value, heads_ref):
+    high, low = parts_of(value)
+    return dot_plain(high, heads_ref[...]) + dot_plain(low, heads_ref[...])
+
+
+def spread_heads(value, heads_ref):
+    high, low = parts_of(value)
+    return dot_right_t(high, heads_ref[...]) + dot_right_t(low, heads_ref[...])
+
+
+def head_norm(value, heads_ref):
+    center = value - spread_heads(sum_heads(value, heads_ref) * (1.0 / HD), heads_ref)
+    spread = sum_heads(center * center, heads_ref) * (1.0 / HD)
+    factor = spread_heads(lax.rsqrt(spread + norm_eps), heads_ref)
+    return center * factor, factor
+
+
+def head_norm_back(grad, normed, factor, heads_ref):
+    first = sum_heads(grad, heads_ref) * (1.0 / HD)
+    second = sum_heads(grad * normed, heads_ref) * (1.0 / HD)
+    return factor * (
+        grad - spread_heads(first, heads_ref) - normed * spread_heads(second, heads_ref)
+    )
+
+
+def partner(value, former):
+    quarter = HD // 4
+    width = value.shape[1]
+    up = pltpu.roll(value, width - quarter, 1)
+    down = pltpu.roll(value, quarter, 1)
+    return jnp.where(former > 0.5, up, down)
+
+
+def turn(value, table_refs):
+    cosine, sine, former = table_refs
+    return value * cosine[...] + partner(value, former[...]) * sine[...]
+
+
+def turn_back(value, table_refs):
+    cosine, sine, former = table_refs
+    return value * cosine[...] - partner(value, former[...]) * sine[...]
+
+
+def window_of(head, width):
+    start = min(head * HD // 128 * 128, width - 256)
+    lane = lax.broadcasted_iota(jnp.int32, (1, 256), 1) + start
+    inside = jnp.logical_and(lane >= head * HD, lane < (head + 1) * HD)
+    return pl.ds(start, 256), inside.astype(f32)
+
+
+def normed_rows(proj_ref, heads_ref, table_refs, rows):
+    value, factor = head_norm(proj_ref[rows, :], heads_ref)
+    turned = turn(value, table_refs) if table_refs else value
+    return value, factor, turned
+
+
+def keys_body(batch, turned, *refs):
+    key_ref, value_ref, heads_ref = refs[:3]
+    table_refs, out_ref = refs[3:-1], refs[-1]
+    width = key_ref.shape[1]
+    size = key_ref.shape[0] // batch
+    for b in range(batch):
+        rows = pl.ds(b * size, size)
+        out_ref[rows, :width] = normed_rows(key_ref, heads_ref, table_refs, rows)[2].astype(bf16)
+        out_ref[rows, width:] = value_ref[rows, :].astype(bf16)
+
+
+def pair_rows(refs, b, size, lanes):
+    if len(refs) == 2:
+        return jnp.concatenate([ref[pl.ds(b * size, size), lanes] for ref in refs], axis=0)
+    return refs[0][pl.ds(b * 2 * size, 2 * size), lanes]
+
+
+def shift_lanes(lanes, width):
+    return pl.ds(lanes.start + width, lanes.size)
+
+
+def scores_of(query, key, lengths_ref, b, scaling):
+    scores = dot_right_t(query, key) * scaling
+    if lengths_ref is not None:
+        column = lax.broadcasted_iota(jnp.int32, scores.shape, 1)
+        scores = jnp.where(column < lengths_ref[b], scores, masked_value)
+    return scores
+
+
+def softmax_of(scores):
+    largest = jnp.max(scores, axis=1, keepdims=True)
+    raised = jnp.exp(scores - largest)
+    return raised / jnp.sum(raised, axis=1, keepdims=True), largest
+
+
+def attention_body(batch, masked, turned, sources, scaling, *refs):
+    refs = list(refs)
+    lengths_ref = refs.pop(0) if masked else None
+    proj_ref, heads_ref = refs.pop(0), refs.pop(0)
+    table_refs = [refs.pop(0) for _ in range(3)] if turned else []
+    keyval_refs = [refs.pop(0) for _ in range(sources)]
+    out_ref, peak_ref, query_ref, mixed_ref = refs
+    size, width = proj_ref.shape[0] // batch, proj_ref.shape[1]
+    peak_ref[...] = jnp.full_like(peak_ref, masked_value)
+    mixed_ref[...] = jnp.zeros_like(mixed_ref)
+    for b in range(batch):
+        rows = pl.ds(b * size, size)
+        query_ref[rows, :] = normed_rows(proj_ref, heads_ref, table_refs, rows)[2].astype(bf16)
+
+    @pl.loop(0, batch)
+    def _(b):
+        rows = pl.ds(pl.multiple_of(b * size, size), size)
+        for head in range(HEADS):
+            lanes, inside = window_of(head, width)
+            query = query_ref[rows, lanes] * inside.astype(bf16)
+            key = pair_rows(keyval_refs, b, size, lanes)
+            scores = scores_of(query, key, lengths_ref, b, scaling)
+            probs, largest = softmax_of(scores)
+            largest = jnp.max(largest, axis=0, keepdims=True)
+            peak_ref[head : head + 1, :] = jnp.maximum(
+                peak_ref[head : head + 1, :], jnp.broadcast_to(largest, (1, 128))
+            )
+            value = pair_rows(keyval_refs, b, size, shift_lanes(lanes, width))
+            mixed_ref[rows, lanes] += dot_plain(probs.astype(bf16), value) * inside
+
+    out_ref[...] = mixed_ref[...].astype(bf16)
+
+
+def attention_back_body(batch, masked, turned, sources, scaling, *refs):
+    refs = list(refs)
+    lengths_ref = refs.pop(0) if masked else None
+    proj_ref, grad_ref, heads_ref = refs.pop(0), refs.pop(0), refs.pop(0)
+    table_refs = [refs.pop(0) for _ in range(3)] if turned else []
+    keyval_refs = [refs.pop(0) for _ in range(sources)]
+    out_ref, here_ref, there_ref, normed_ref, factor_ref, query_ref, back_ref, total_ref = refs
+    size, width = proj_ref.shape[0] // batch, proj_ref.shape[1]
+    back_ref[...] = jnp.zeros_like(back_ref)
+    total_ref[...] = jnp.zeros_like(total_ref)
+    for b in range(batch):
+        rows = pl.ds(b * size, size)
+        normed, factor, query = normed_rows(proj_ref, heads_ref, table_refs, rows)
+        normed_ref[rows, :] = normed
+        factor_ref[rows, :] = factor
+        query_ref[rows, :] = query.astype(bf16)
+
+    @pl.loop(0, batch)
+    def _(b):
+        rows = pl.ds(pl.multiple_of(b * size, size), size)
+        for head in range(HEADS):
+            lanes, inside = window_of(head, width)
+            behind = shift_lanes(lanes, width)
+            query = query_ref[rows, lanes] * inside.astype(bf16)
+            key = pair_rows(keyval_refs, b, size, lanes)
+            probs, _ = softmax_of(scores_of(query, key, lengths_ref, b, scaling))
+            grad = grad_ref[rows, lanes] * inside.astype(bf16)
+            value = pair_rows(keyval_refs, b, size, behind)
+            prob_grad = dot_right_t(grad, value)
+            score_grad = softmax_back(probs, prob_grad).astype(bf16)
+            value_grad = dot_left_t(probs.astype(bf16), grad)
+            key_grad = dot_left_t(score_grad, query) * scaling
+            back_ref[rows, lanes] += dot_plain(score_grad, key) * (inside * scaling)
+            for at in range(2):
+                part = slice(at * size, (at + 1) * size)
+                total_ref[at, rows, lanes] += key_grad[part]
+                total_ref[at, rows, behind] += value_grad[part]
+
+    for b in range(batch):
+        rows = pl.ds(b * size, size)
+        grad = back_ref[rows, :]
+        if table_refs:
+            grad = turn_back(grad, table_refs)
+        out_ref[rows, :] = head_norm_back(
+            grad, normed_ref[rows, :], factor_ref[rows, :], heads_ref
+        ).astype(bf16)
+    mine = lax.axis_index("seq") if masked else 0
+    here_ref[...] = total_ref[mine]
+    there_ref[...] = total_ref[1 - mine].astype(bf16)
+
+
+def keys_back_body(batch, turned, *refs):
+    key_ref, here_ref, from_there_ref, heads_ref = refs[:4]
+    table_refs, out_ref = refs[4:-1], refs[-1]
+    width = key_ref.shape[1]
+    size = key_ref.shape[0] // batch
+    for b in range(batch):
+        rows = pl.ds(b * size, size)
+        normed, factor, _ = normed_rows(key_ref, heads_ref, (), rows)
+        grad = here_ref[rows, :width] + from_there_ref[rows, :width].astype(f32)
+        if table_refs:
+            grad = turn_back(grad, table_refs)
+        out_ref[rows, :width] = head_norm_back(grad, normed, factor, heads_ref).astype(bf16)
+        out_ref[rows, width:] = (
+            here_ref[rows, width:] + from_there_ref[rows, width:].astype(f32)
+        ).astype(bf16)
+
+
+def plain_call(body, outs, blocks, scratch=(), lengths=None):
+    def spec(array, column):
+        if column is None:
+            return pl.BlockSpec(array.shape, lambda i, *_: (0,) * array.ndim)
+        return pl.BlockSpec((array.shape[0], column[1]), lambda i, *_: (0, column[0]))
+
+    def out_spec(shape):
+        return pl.BlockSpec(shape.shape, lambda i, *_: (0,) * len(shape.shape))
+
+    grid_spec = pltpu.PrefetchScalarGridSpec(
+        num_scalar_prefetch=0 if lengths is None else 1,
+        grid=(1,),
+        in_specs=[spec(*block) for block in blocks],
+        out_specs=[out_spec(shape) for shape in outs],
+        scratch_shapes=list(scratch),
+    )
+    given = [] if lengths is None else [lengths]
+    return pl.pallas_call(
+        body,
+        grid_spec=grid_spec,
+        out_shape=list(outs),
+        compiler_params=pltpu.CompilerParams(vmem_limit_bytes=50 * 2**20),
+    )(*given, *[array for array, _ in blocks])
+
+
 def lanes_of(value, multiple):
     size = 128 * multiple
     spare = -value.shape[-1] % size
@@ -648,18 +1217,6 @@
     high = value.astype(bf16)
     low = (value - high.astype(f32)).astype(bf16)
     return dot_right_t(high, matrix) + dot_right_t(low, matrix)
-
-
-def attend(queries, keys, scaling):
-    return jnp.einsum("bqhd,bkhd->bhqk", queries, keys, preferred_element_type=f32) * scaling
-
-
-def mix(probs, values):
-    return jnp.einsum("bhqk,bkhd->bqhd", probs, values, preferred_element_type=f32)
-
-
-def mix_back(probs, grads):
-    return jnp.einsum("bhqk,bqhd->bkhd", probs, grads, preferred_element_type=f32)
 
 
 def local(
@@ -692,7 +1249,18 @@
     count = links.count
 
     positions = core * tokens + jnp.arange(tokens)
-    cosine_table, sine_table = rotary_tables(positions // GRID_W, positions % GRID_W, HD)
+    feature = jnp.arange(width) % HD
+    freqs = 10000.0 ** (-(feature % (HD // 4)).astype(f32) / (HD // 4))
+    place = jnp.where(
+        feature[None, :] < HD // 2, (positions // GRID_W)[:, None], (positions % GRID_W)[:, None]
+    )
+    angles = place.astype(f32) * freqs[None, :]
+    former = (feature % (HD // 2) < HD // 4)[None, :]
+    cosine = jnp.cos(angles)
+    sine = jnp.where(former, -jnp.sin(angles), jnp.sin(angles))
+    tables = [(cosine, None), (sine, None), (former.astype(f32), None)]
+    head_at = jnp.arange(width)[:, None] // HD == jnp.arange(128)[None, :]
+    head_at = (head_at.astype(bf16), None)
 
     gain_rows = skip_gain.shape[0]
     third = norm_gains.shape[1]
@@ -775,9 +1343,6 @@
     def restore(value):
         return dot_right_t(value.astype(bf16), order).astype(bf16)
 
-    def heads_of(value):
-        return value.reshape(batch, -1, HEADS, HD)
-
     joined = jnp.concatenate(
         [latent.reshape(rows, width), skip_input.reshape(rows, width)], axis=1
     ).astype(f32)
@@ -797,48 +1362,49 @@
 
     attn_in = reorder(shifted(hidden, gains[0], shift).astype(bf16))
     qkv_proj = product(attn_in, w_qkv)
-    query_proj = heads_of(qkv_proj[:, :width])
-    key_proj = heads_of(qkv_proj[:, width : 2 * width])
-
-    def norm_rotate(values):
-        return rotate(layer_norm(values), cosine_table, sine_table)
-
-    queries = norm_rotate(query_proj).astype(bf16)
-    keys_here = norm_rotate(key_proj).astype(bf16)
-    values_here = heads_of(qkv_proj[:, 2 * width :].astype(bf16))
-    keyval_here = jnp.concatenate(
-        [keys_here.reshape(rows, width), values_here.reshape(rows, width)], axis=1
+    query_block, key_block, value_block = ((qkv_proj, (at, width)) for at in range(3))
+
+    def shaped(height, breadth, dtype):
+        return jax.ShapeDtypeStruct((height, breadth), dtype)
+
+    (keyval_here,) = plain_call(
+        functools.partial(keys_body, batch, True),
+        [shaped(rows, 2 * width, bf16)],
+        [key_block, value_block, head_at, *tables],
     )
     keyval_there = links.sibling(keyval_here)
-    keys_all = jnp.concatenate([keys_here, heads_of(keyval_there[:, :width])], axis=1)
-    values_all = jnp.concatenate([values_here, heads_of(keyval_there[:, width:])], axis=1)
-    queries = tie(queries, get_up)
-    scores = attend(queries, keys_all, scaling)
-    self_peak = jnp.max(scores, axis=(0, 2, 3))
-    probs = jax.nn.softmax(scores, axis=-1)
-    mixed = mix(probs.astype(bf16), values_all)
-    attn_cat = reorder(mixed.reshape(rows, width).astype(bf16))
+    qkv_proj = tie(qkv_proj, get_up)
+    keyvals = [(keyval_here, None), (keyval_there, None)]
+    attention_scratch = [pltpu.VMEM((rows, width), bf16), pltpu.VMEM((rows, width), f32)]
+    attn_cat, self_peak = plain_call(
+        functools.partial(attention_body, batch, False, True, 2, scaling),
+        [shaped(rows, width, bf16), shaped(HEADS, 128, f32)],
+        [query_block, head_at, *tables, *keyvals],
+        attention_scratch,
+    )
+    attn_cat = reorder(attn_cat)
     attn_cat = tie(attn_cat, get_down)
     after_self = hidden + dot_plain(attn_cat, w_self_out)
     cross_in = reorder(gained_norm(after_self, gains[1]).astype(bf16))
-    cq_proj = heads_of(product(cross_in, w_query))
-    cross_queries = layer_norm(cq_proj).astype(bf16)
+    cq_proj = product(cross_in, w_query)
 
     text = text_encoder_states.reshape(batch * text_rows, text_width)
     text_ordered = dot_plain(text, order_text).astype(bf16)
     ckv_proj = product(text_ordered, w_keyval)
-    ckey_proj = heads_of(ckv_proj[:, :width])
-    cross_keys = layer_norm(ckey_proj).astype(bf16)
-    cross_values = heads_of(ckv_proj[:, width:].astype(bf16))
-    text_valid = jnp.arange(text_rows)[None, :] < text_lengths[:, None]
-    cross_queries = tie(cross_queries, get_up)
-    cross_scores = jnp.where(
-        text_valid[:, None, None, :], attend(cross_queries, cross_keys, scaling), masked_value
-    )
-    cross_peak = jnp.max(cross_scores, axis=(0, 2, 3))
-    cross_probs = jax.nn.softmax(cross_scores, axis=-1)
-    cross_mixed = mix(cross_probs.astype(bf16), cross_values)
-    cross_cat = reorder(cross_mixed.reshape(rows, width).astype(bf16))
+    (cross_keyval_all,) = plain_call(
+        functools.partial(keys_body, batch, False),
+        [shaped(batch * text_rows, 2 * width, bf16)],
+        [(ckv_proj, (0, width)), (ckv_proj, (1, width)), head_at],
+    )
+    cq_proj = tie(cq_proj, get_up)
+    cross_cat, cross_peak = plain_call(
+        functools.partial(attention_body, batch, True, False, 1, scaling),
+        [shaped(rows, width, bf16), shaped(HEADS, 128, f32)],
+        [(cq_proj, None), head_at, (cross_keyval_all, None)],
+        attention_scratch,
+        text_lengths,
+    )
+    cross_cat = reorder(cross_cat)
     after_cross = after_self + dot_plain(cross_cat, w_cross_out)
     mlp_in = reorder(gained_norm(after_cross, gains[2]).astype(bf16))
     mlp_in = tie(mlp_in, get_up, get_down)
@@ -863,14 +1429,25 @@
     cross_part, gain_third = jax.vjp(gained_norm, after_cross, gains[2])[1](mlp_in_grad)
     cross_grad = result_grad + cross_part
     cross_bf = tie(cross_grad.astype(bf16), put_up)
-    cmix_grad = heads_of(restore(dot_right_t(cross_bf, w_cross_out)))
-    cval_grad = mix_back(cross_probs.astype(bf16), cmix_grad)
+    cmix_grad = restore(dot_right_t(cross_bf, w_cross_out))
     cmix_grad = tie(cmix_grad, put_down)
-    cprob_grad = jnp.einsum("bqhd,bkhd->bhqk", cmix_grad, cross_values, preferred_element_type=f32)
-    cscore_grad = softmax_back(cross_probs, cprob_grad).astype(bf16)
-    cquery_grad = mix(cscore_grad, cross_keys) * scaling
-    ckey_grad = mix_back(cscore_grad, cross_queries) * scaling
-    cq_grad = jax.vjp(layer_norm, cq_proj)[1](cquery_grad)[0].reshape(rows, width).astype(bf16)
+    back_scratch = [
+        pltpu.VMEM((rows, width), f32),
+        pltpu.VMEM((rows, width), f32),
+        pltpu.VMEM((rows, width), bf16),
+        pltpu.VMEM((rows, width), f32),
+        pltpu.VMEM((2, rows, 2 * width), f32),
+    ]
+    back_outs = [
+        shaped(rows, width, bf16), shaped(rows, 2 * width, f32), shaped(rows, 2 * width, bf16)
+    ]
+    cq_grad, ckeyval_mine, ckeyval_theirs = plain_call(
+        functools.partial(attention_back_body, batch, True, False, 1, scaling),
+        back_outs,
+        [(cq_proj, None), (cmix_grad, None), head_at, (cross_keyval_all, None)],
+        back_scratch,
+        text_lengths,
+    )
     put_query = column_grad(cross_in, cq_grad)
     cq_grad = tie(cq_grad, put_up, put_down)
     cross_in_grad = exact_restore(order, product_back(cq_grad, w_query))
@@ -878,22 +1455,19 @@
     self_grad = cross_grad + self_part
 
     text_half = text_rows // 2
-    ckeyval = jnp.concatenate(
+    ckey_mine = lax.dynamic_slice_in_dim(
+        ckv_proj.reshape(batch, text_rows, 2 * width)[:, :, :width], core * text_half, text_half, 1
+    ).reshape(batch * text_half, width)
+    (keyval_grad,) = plain_call(
+        functools.partial(keys_back_body, batch, False),
+        [shaped(batch * text_half, 2 * width, bf16)],
         [
-            ckey_grad.reshape(batch, text_rows, width),
-            cval_grad.reshape(batch, text_rows, width),
+            (ckey_mine, None),
+            (ckeyval_mine, None),
+            (links.sibling(ckeyval_theirs), None),
+            head_at,
         ],
-        axis=2,
-    ).astype(bf16)
-    ckeyval_mine = lax.dynamic_slice_in_dim(ckeyval, core * text_half, text_half, 1)
-    ckeyval_theirs = lax.dynamic_slice_in_dim(ckeyval, (1 - core) * text_half, text_half, 1)
-    ckeyval_sum = ckeyval_mine.astype(f32) + links.sibling(ckeyval_theirs).astype(f32)
-    ckey_mine = lax.dynamic_slice_in_dim(ckey_proj, core * text_half, text_half, 1)
-    ckey_pre = jax.vjp(layer_norm, ckey_mine)[1](heads_of(ckeyval_sum[..., :width]))[0]
-    keyval_grad = jnp.concatenate(
-        [ckey_pre.reshape(batch * text_half, width), ckeyval_sum[..., width:].reshape(-1, width)],
-        axis=1,
-    ).astype(bf16)
+    )
     text_mine = lax.dynamic_slice_in_dim(
         text_ordered.reshape(batch, text_rows, text_width), core * text_half, text_half, 1
     ).reshape(-1, text_width)
@@ -907,26 +1481,21 @@
         (links.pick(cross_cat, attn_cat), links.pick(cross_bf, self_bf)),
     )
     self_bf = tie(self_bf, put_down)
-    mix_grad = heads_of(restore(dot_right_t(self_bf, w_self_out)))
+    mix_grad = restore(dot_right_t(self_bf, w_self_out))
     mix_grad = tie(mix_grad, put_up)
-    value_grad = mix_back(probs.astype(bf16), mix_grad)
-    prob_grad = jnp.einsum("bqhd,bkhd->bhqk", mix_grad, values_all, preferred_element_type=f32)
-    score_grad = softmax_back(probs, prob_grad).astype(bf16)
-    score_grad = tie(score_grad, put_up)
-    query_grad = mix(score_grad, keys_all) * scaling
-    key_grad = mix_back(score_grad, queries) * scaling
-    there = jnp.concatenate(
-        [key_grad[:, tokens:].reshape(rows, width), value_grad[:, tokens:].reshape(rows, width)],
-        axis=1,
-    ).astype(bf16)
-    from_there = links.sibling(there).astype(f32)
-    key_here = key_grad[:, :tokens] + heads_of(from_there[:, :width])
-    value_here = value_grad[:, :tokens].reshape(rows, width) + from_there[:, width:]
-    query_pre = jax.vjp(norm_rotate, query_proj)[1](query_grad)[0]
-    key_pre = jax.vjp(norm_rotate, key_proj)[1](key_here)[0]
-    qkv_grad = jnp.concatenate(
-        [query_pre.reshape(rows, width), key_pre.reshape(rows, width), value_here], axis=1
-    ).astype(bf16)
+    query_grad, here, there = plain_call(
+        functools.partial(attention_back_body, batch, False, True, 2, scaling),
+        back_outs,
+        [query_block, (mix_grad, None), head_at, *tables, *keyvals],
+        back_scratch,
+    )
+    here = tie(here, put_up)
+    (key_value_grad,) = plain_call(
+        functools.partial(keys_back_body, batch, True),
+        [shaped(rows, 2 * width, bf16)],
+        [key_block, (here, None), (links.sibling(there), None), head_at, *tables],
+    )
+    qkv_grad = jnp.concatenate([query_grad, key_value_grad], axis=1)
     put_qkv = column_grad(attn_in, qkv_grad)
     attn_in_grad = exact_restore(order, product_back(qkv_grad, w_qkv))
     hidden_part, gain_first, shift_grad = jax.vjp(shifted, hidden, gains[0], shift)[1](
@@ -966,7 +1535,7 @@
     gains_grad = jnp.stack([gain_first, gain_second, gain_third])
     gains_grad = gains_grad.reshape(3, count, third).transpose(1, 0, 2).reshape(count, 3 * third)
     gains_grad = jnp.concatenate([skip_gain_grad.reshape(count, gain_rows), gains_grad], axis=1)
-    peaks = jnp.stack([self_peak, cross_peak])
+    peaks = jnp.stack([self_peak[:, 0], cross_peak[:, 0]])
     cores = jnp.concatenate([shift_grad.reshape(-1), gains_grad.reshape(-1), peaks.reshape(-1)])
     there = links.sibling(cores)
     peaks = jnp.maximum(cores, there)[-2 * HEADS :]
@@ -1024,6 +1593,406 @@
     )
 
 
+def local_sixteen(
+    latent,
+    skip_input,
+    condition,
+    text_encoder_states,
+    text_lengths,
+    out_grad,
+    skip_gain,
+    norm_gains,
+    skip_linear,
+    shift_linear,
+    self_qkv,
+    self_out,
+    cross_query,
+    cross_keyval,
+    cross_out,
+    mlp_up,
+    mlp_down,
+    thresholds,
+):
+    batch, tokens, width = latent.shape
+    rows = batch * tokens
+    text_rows = text_encoder_states.shape[1]
+    text_width = text_encoder_states.shape[2]
+    scaling = HD ** (-0.5)
+    links = Links(lax.axis_size("fsdp"))
+    me, core = links.me, links.core
+    count = links.count
+
+    positions = core * tokens + jnp.arange(tokens)
+    feature = jnp.arange(width) % HD
+    freqs = 10000.0 ** (-(feature % (HD // 4)).astype(f32) / (HD // 4))
+    place = jnp.where(
+        feature[None, :] < HD // 2, (positions // GRID_W)[:, None], (positions % GRID_W)[:, None]
+    )
+    angles = place.astype(f32) * freqs[None, :]
+    former = (feature % (HD // 2) < HD // 4)[None, :]
+    cosine = jnp.cos(angles)
+    sine = jnp.where(former, -jnp.sin(angles), jnp.sin(angles))
+    tables = [(cosine, None), (sine, None), (former.astype(f32), None)]
+    head_at = jnp.arange(width)[:, None] // HD == jnp.arange(128)[None, :]
+    head_at = (head_at.astype(bf16), None)
+
+    gain_rows = skip_gain.shape[0]
+    third = norm_gains.shape[1]
+    cond_act = jax.nn.silu(condition.astype(f32)).astype(bf16)
+    small = jnp.concatenate([skip_gain, norm_gains.reshape(-1), cond_act.reshape(-1)])
+    small = trade(lanes_of(small, 16), count, True, 1).reshape(count, -1)
+    skip_gain_all = small[:, :gain_rows].reshape(-1).astype(f32)
+    cond_start = gain_rows + 3 * third
+    gains = small[:, gain_rows:cond_start].reshape(count, 3, third)
+    gains = gains.transpose(1, 0, 2).reshape(3, width).astype(f32)
+    cond_all = small[:, cond_start : cond_start + batch * width].reshape(count * batch, width)
+    shift_rows = shift_linear.shape[0]
+    cond_cut = lax.dynamic_slice_in_dim(cond_all, me * shift_rows, shift_rows, 1)
+    shift_parts = dot_plain(cond_cut, shift_linear).reshape(count, batch * width)
+    shift_parts = trade(lanes_of(shift_parts, 8), count, False, 2)
+    shift = jnp.sum(shift_parts.reshape(count, -1), axis=0)[: batch * width].reshape(batch, width)
+
+    def halves_of(weight):
+        cut = (weight.shape[1] // 2 + 127) // 128 * 128
+        first, second = weight[:, :cut], weight[:, cut:]
+        return first, jnp.pad(second, ((0, 0), (0, cut - second.shape[1])))
+
+    def qkv_halves(value):
+        edge = 2 * width + 768
+        first = jnp.concatenate([value[:, :width], value[:, 2 * width : edge]], axis=1)
+        rest = jnp.pad(value[:, edge:], ((0, 0), (0, 2 * 768 - width)))
+        return first, jnp.concatenate([value[:, width : 2 * width], rest], axis=1)
+
+    def qkv_whole(first, second):
+        last = second[:, width : 2 * width - 768]
+        return jnp.concatenate(
+            [first[:, :width], second[:, :width], first[:, width:], last], axis=1
+        )
+
+    skip_half = skip_linear.shape[0] // 2
+    shards = [
+        links.pick(skip_linear[:skip_half], skip_linear[skip_half:]),
+        links.pick(*qkv_halves(self_qkv)),
+        links.pick(self_out, cross_out),
+        links.pick(*halves_of(cross_query)),
+        links.pick(*halves_of(cross_keyval)),
+        links.pick(*halves_of(mlp_up)),
+        links.pick(*halves_of(mlp_down)),
+    ]
+    block = width // 16
+
+    def one_hot(starts, size, height):
+        wanted = (starts[:, None] + jnp.arange(size, dtype=jnp.int32)).reshape(1, -1)
+        rows_at = lax.broadcasted_iota(jnp.int32, (height, wanted.shape[1]), 0)
+        return (rows_at == wanted).astype(bf16)
+
+    slots = jnp.arange(16, dtype=jnp.int32)
+    order = one_hot(jnp.bitwise_xor(me, slots) * block, block, width)
+    text_block = text_width // 16
+    order_text = one_hot(jnp.bitwise_xor(me, slots) * text_block, text_block, text_width)
+    lower = jnp.bitwise_xor(jnp.bitwise_and(me, 7), slots[:8]) * (2 * block)
+    order_skip = jnp.stack([one_hot(lower + at * block, block, width) for at in range(2)])
+    text = text_encoder_states.reshape(batch * text_rows, text_width)
+    text_ordered = dot_plain(text, order_text).astype(bf16)
+    valid = (jnp.arange(text_rows)[None, :] < text_lengths[:, None]).astype(f32)
+    head_at = (jnp.arange(width)[:, None] // HD == jnp.arange(128)[None, :]).astype(bf16)
+    table_arrays = [table for table, _ in tables]
+
+    def shaped(*shape, dtype=f32):
+        return jax.ShapeDtypeStruct(shape, dtype)
+
+    flat, flat_low = shaped(rows, width), shaped(rows, width, dtype=bf16)
+    double_low = shaped(rows, 2 * width, dtype=bf16)
+    inner = mlp_down.shape[0] * 16
+    given = [
+        latent.reshape(rows, width),
+        skip_input.reshape(rows, width),
+        skip_gain_all[None, :],
+        gains,
+        shift,
+        order,
+        order_skip,
+        head_at,
+        *table_arrays,
+        text_ordered,
+        valid,
+    ]
+    saved = [
+        shaped(2, 2, rows, width // 2, dtype=bf16),
+        flat,
+        flat_low,
+        shaped(rows, 2 * width),
+        double_low,
+        double_low,
+        flat_low,
+        flat,
+        flat_low,
+        flat,
+        flat,
+        shaped(batch * text_rows, 2 * width, dtype=bf16),
+        flat_low,
+        flat,
+        flat_low,
+        shaped(rows, inner),
+        shaped(rows, inner, dtype=bf16),
+        shaped(HEADS, 128),
+        shaped(HEADS, 128),
+    ]
+    (
+        *gathered,
+        normed,
+        hidden,
+        attn_in,
+        qkv_proj,
+        keyval_here,
+        keyval_there,
+        attn_cat,
+        after_self,
+        cross_in,
+        cq_proj,
+        ckey_mine,
+        cross_keyval_all,
+        cross_cat,
+        after_cross,
+        mlp_in,
+        upper,
+        activated,
+        self_peak,
+        cross_peak,
+    ) = pl.pallas_call(
+        functools.partial(forward_body, batch, scaling),
+        out_shape=[shaped(2, 4, 4, *shard.shape, dtype=bf16) for shard in shards] + saved,
+        in_specs=[IN_VMEM] * len(given) + [ANYWHERE] * 7,
+        out_specs=[ANYWHERE] * 7 + [IN_VMEM] * len(saved),
+        scratch_shapes=[
+            pltpu.VMEM((rows, width), f32),
+            pltpu.VMEM((rows, width), bf16),
+            pltpu.VMEM((3, 4, 4, block, 512), bf16),
+            pltpu.SemaphoreType.DMA((3,)),
+            pltpu.SemaphoreType.DMA((7, 10)),
+            pltpu.SemaphoreType.DMA((7, 10)),
+            pltpu.SemaphoreType.DMA((7,)),
+            pltpu.SemaphoreType.DMA,
+            pltpu.SemaphoreType.DMA,
+        ],
+        compiler_params=pltpu.CompilerParams(
+            collective_id=7, has_side_effects=True, vmem_limit_bytes=62 * 2**20
+        ),
+    )(*given, *shards)
+    w_skip, w_qkv, w_pair, w_query, w_keyval, w_up, w_down = (
+        g.reshape(2, 16 * g.shape[3], g.shape[4]) for g in gathered
+    )
+
+    def cut_halves(value):
+        cut = (value.shape[1] // 2 + 127) // 128 * 128
+        second = value[:, cut:]
+        return value[:, :cut], jnp.pad(second, ((0, 0), (0, cut - second.shape[1])))
+
+    def product(halves, weight):
+        return dot_plain(halves[0], weight[0]) + dot_plain(halves[1], weight[1])
+
+    def product_back(halves, weight):
+        return dot_right_t(halves[0], weight[0]) + dot_right_t(halves[1], weight[1])
+
+    def sum_twins(*pairs):
+        (left, right), (left_two, right_two) = pairs
+        there = dot_left_t(links.pick(left_two, left), links.pick(right_two, right)).astype(bf16)
+        mine = dot_left_t(links.pick(left, left_two), links.pick(right, right_two))
+        value = (mine + links.sibling(there).astype(f32)).astype(bf16)
+        return value.reshape(4, 4, value.shape[0] // 16, value.shape[1])
+
+    def column_grad(value, halves):
+        return sum_twins((value, halves[0]), (value, halves[1]))
+
+    def restore(value):
+        return dot_right_t(value.astype(bf16), order).astype(bf16)
+
+    def blocks_moved(value):
+        size = value.shape[1] // 16
+        return jnp.concatenate(
+            [
+                lax.dynamic_slice_in_dim(value, jnp.bitwise_xor(me, at) * size, size, 1)
+                for at in range(16)
+            ],
+            axis=1,
+        )
+
+    down_in = out_grad.reshape(rows, width)
+    result_grad = down_in.astype(f32)
+    down_halves = cut_halves(down_in)
+    put_down = column_grad(activated, down_halves)
+    result = [dot_plain(activated, w_down[0]), dot_plain(activated, w_down[1])]
+    result = jnp.concatenate([result[0], result[1][:, : width - result[0].shape[1]]], axis=1)
+    block_out = (after_cross + result).astype(bf16)
+    act_grad = blocks_moved(product_back(down_halves, w_down))
+    upper_grad = jax.vjp(gelu_tanh, upper)[1](act_grad)[0].astype(bf16)
+    upper_halves = cut_halves(upper_grad)
+    put_up = column_grad(mlp_in, upper_halves)
+    mlp_in_grad = exact_restore(order, product_back(upper_halves, w_up))
+    cross_part, gain_third = jax.vjp(gained_norm, after_cross, gains[2])[1](mlp_in_grad)
+    cross_grad = result_grad + cross_part
+    cross_bf = cross_grad.astype(bf16)
+    cmix_grad = restore(dot_right_t(cross_bf, w_pair[1]))
+    back_scratch = [
+        pltpu.VMEM((rows, width), f32),
+        pltpu.VMEM((rows, width), f32),
+        pltpu.VMEM((rows, width), bf16),
+        pltpu.VMEM((rows, width), f32),
+        pltpu.VMEM((2, rows, 2 * width), f32),
+    ]
+    back_outs = [flat_low, shaped(rows, 2 * width), double_low]
+    heads_block = (head_at, None)
+    cq_grad, ckeyval_mine, ckeyval_theirs = plain_call(
+        functools.partial(attention_back_body, batch, True, False, 1, scaling),
+        back_outs,
+        [(cq_proj, None), (cmix_grad, None), heads_block, (cross_keyval_all, None)],
+        back_scratch,
+        text_lengths,
+    )
+    cq_halves = cut_halves(cq_grad)
+    put_query = column_grad(cross_in, cq_halves)
+    cross_in_grad = exact_restore(order, product_back(cq_halves, w_query))
+    self_part, gain_second = jax.vjp(gained_norm, after_self, gains[1])[1](cross_in_grad)
+    self_grad = cross_grad + self_part
+
+    text_half = text_rows // 2
+    (keyval_grad,) = plain_call(
+        functools.partial(keys_back_body, batch, False),
+        [double_low],
+        [
+            (ckey_mine, None),
+            (ckeyval_mine, None),
+            (links.sibling(ckeyval_theirs), None),
+            heads_block,
+        ],
+    )
+    text_mine = lax.dynamic_slice_in_dim(
+        text_ordered.reshape(batch, text_rows, text_width), core * text_half, text_half, 1
+    ).reshape(-1, text_width)
+    keyval_halves = cut_halves(keyval_grad)
+    put_keyval = column_grad(text_mine, keyval_halves)
+    grad_text = exact_restore(order_text, product_back(keyval_halves, w_keyval))
+    grad_text = grad_text.reshape(batch, text_half, text_width)
+
+    self_bf = self_grad.astype(bf16)
+    put_pair = sum_twins((attn_cat, self_bf), (cross_cat, cross_bf))
+    mix_grad = restore(dot_right_t(self_bf, w_pair[0]))
+    query_grad, here, there = plain_call(
+        functools.partial(attention_back_body, batch, False, True, 2, scaling),
+        back_outs,
+        [
+            (qkv_proj, (0, width)),
+            (mix_grad, None),
+            heads_block,
+            *tables,
+            (keyval_here, None),
+            (keyval_there, None),
+        ],
+        back_scratch,
+    )
+    (key_value_grad,) = plain_call(
+        functools.partial(keys_back_body, batch, True),
+        [double_low],
+        [(qkv_proj, (1, width)), (here, None), (links.sibling(there), None), heads_block, *tables],
+    )
+    qkv_grad = qkv_halves(jnp.concatenate([query_grad, key_value_grad], axis=1))
+    put_qkv = column_grad(attn_in, qkv_grad)
+    attn_in_grad = exact_restore(order, product_back(qkv_grad, w_qkv))
+
+    def shifted(values, gain, moved):
+        wide = jnp.broadcast_to(moved[:, None, :], (batch, tokens, width)).reshape(rows, width)
+        return layer_norm(values) * gain + wide
+
+    hidden_part, gain_first, shift_grad = jax.vjp(shifted, hidden, gains[0], shift)[1](
+        attn_in_grad
+    )
+    hidden_grad = self_grad + hidden_part
+    hidden_bf = hidden_grad.astype(bf16)
+    normed_halves = [jnp.concatenate([normed[c, 0], normed[c, 1]], axis=1) for c in range(2)]
+    put_skip = sum_twins((normed_halves[0], hidden_bf), (normed_halves[1], hidden_bf))
+    near_grad, away_grad = 0.0, 0.0
+    for at in range(2):
+        part = dot_right_t(hidden_bf, w_skip[at])
+        near_grad = near_grad + exact_restore(order_skip[at], part[:, : width // 2])
+        away_grad = away_grad + exact_restore(order_skip[at], part[:, width // 2 :])
+    normed_grad = jnp.concatenate(
+        [jnp.where(me < 8, near_grad, away_grad), jnp.where(me < 8, away_grad, near_grad)], axis=1
+    )
+    joined = jnp.concatenate(
+        [latent.reshape(rows, width), skip_input.reshape(rows, width)], axis=1
+    ).astype(f32)
+    joined_grad, skip_gain_grad = jax.vjp(gained_norm, joined, skip_gain_all)[1](normed_grad)
+    grads_down, grads_up = scatter([put_down, put_up], 4, 8)
+    grads = scatter([put_pair, put_query, put_keyval, put_qkv, put_skip], 4, 4)
+    grad_down = jnp.concatenate([grads_down[0], grads_down[1]], axis=1)[:, :width]
+    grad_up = jnp.concatenate([grads_up[0], grads_up[1]], axis=1)
+    grad_self_out, grad_cross_out = grads[0][0], grads[0][1]
+    grad_cross_query = jnp.concatenate([grads[1][0], grads[1][1]], axis=1)[:, :width]
+    grad_keyval = jnp.concatenate([grads[2][0], grads[2][1]], axis=1)
+    grad_qkv = qkv_whole(grads[3][0], grads[3][1])
+    grad_skip_linear = grads[4].reshape(skip_linear.shape)
+
+    gains_grad = jnp.stack([gain_first, gain_second, gain_third])
+    gains_grad = gains_grad.reshape(3, count, third).transpose(1, 0, 2).reshape(count, 3 * third)
+    gains_grad = jnp.concatenate([skip_gain_grad.reshape(count, gain_rows), gains_grad], axis=1)
+    peaks = jnp.stack([self_peak[:, 0], cross_peak[:, 0]])
+    cores = jnp.concatenate([shift_grad.reshape(-1), gains_grad.reshape(-1), peaks.reshape(-1)])
+    there = links.sibling(cores)
+    peaks = jnp.maximum(cores, there)[-2 * HEADS :]
+    cores = cores + there
+    ends = (batch * width, batch * width + count * cond_start)
+    gains_grad = cores[ends[0] : ends[1]].reshape(count, cond_start)
+    shift_bf = cores[: ends[0]].astype(bf16).astype(f32)
+    shared = trade(lanes_of(jnp.concatenate([shift_bf, peaks]), 8), count, True, 5)
+    shared = shared.reshape(count, -1)
+    shift_all = shared[:, : ends[0]].reshape(count * batch, width).astype(bf16)
+    peaks = jnp.max(shared[:, ends[0] : ends[0] + 2 * HEADS], axis=0).reshape(2, HEADS)
+    grad_shift = dot_left_t(cond_cut, shift_all)
+    cond_back = dot_right_t(shift_all, shift_linear).reshape(count, batch * shift_rows)
+    owned = trade(lanes_of(jnp.concatenate([cond_back, gains_grad], axis=1), 8), count, False, 6)
+    owned = owned.reshape(count, -1)
+    cond_mine = owned[:, : batch * shift_rows].reshape(count, batch, shift_rows)
+    cond_mine = cond_mine.transpose(1, 0, 2).reshape(batch, width)
+    grad_cond = jax.vjp(jax.nn.silu, condition.astype(f32))[1](cond_mine)[0]
+    own_gains = jnp.sum(owned[:, batch * shift_rows : batch * shift_rows + cond_start], axis=0)
+    grad_skip_gain = own_gains[:gain_rows]
+    grad_gains = own_gains[gain_rows:].reshape(3, third)
+
+    roots = jnp.sqrt(thresholds / jnp.maximum(peaks, thresholds))
+    self_cols = jnp.repeat(roots[0], HD)
+    cross_cols = jnp.repeat(roots[1], HD)
+    unit_cols = jnp.ones((width,), f32)
+    clipped_qkv = (
+        self_qkv.astype(f32) * jnp.concatenate([self_cols, self_cols, unit_cols])[None, :]
+    ).astype(bf16)
+    clipped_query = (cross_query.astype(f32) * cross_cols[None, :]).astype(bf16)
+    clipped_keyval = (
+        cross_keyval.astype(f32) * jnp.concatenate([cross_cols, unit_cols])[None, :]
+    ).astype(bf16)
+    return (
+        block_out.reshape(batch, tokens, width),
+        joined_grad[:, :width].reshape(batch, tokens, width),
+        joined_grad[:, width:].reshape(batch, tokens, width),
+        grad_cond,
+        grad_text,
+        grad_skip_gain,
+        grad_gains,
+        grad_skip_linear,
+        grad_shift,
+        grad_qkv,
+        grad_self_out,
+        grad_cross_query,
+        grad_keyval,
+        grad_cross_out,
+        grad_up,
+        grad_down,
+        clipped_qkv,
+        clipped_query,
+        clipped_keyval,
+        peaks,
+    )
+
+
 def solution(mesh):
     rows = P("fsdp", None)
     tokens = P("fsdp", "seq", None)
@@ -1048,4 +2017,5 @@
         *([rows] * 12),
         P(),
     )
-    return jax.shard_map(local, mesh=mesh, in_specs=in_specs, out_specs=out_specs, check_vma=False)
+    step = local_sixteen if mesh.shape["fsdp"] == 16 else local
+    return jax.shard_map(step, mesh=mesh, in_specs=in_specs, out_specs=out_specs, check_vma=False)

time: 1270 us -> 1250 us (0.984)
  Pallas kernels: 421 us -> 907 us
  local copies, waits for them, and re-layouts: 219 us -> 96.7 us
  other arithmetic: 183 us -> 65.4 us
  matrix products: 261 us -> 160 us
  waiting for transfers between devices: 80.6 us -> 0.03 us
  starting transfers between devices: 75.6 us -> 2.74 us
  between operations: 15.9 us -> 3.19 us
    pallas_call x1 -> x5, Pallas kernels: 185 us -> 449 us  [the longest x1 380 us: local_sixteen(): pl.pallas_call(functools.partial(forward_body, batch, scaling), out_shape...]
    pallas_call x1 -> x2, Pallas kernels: 192 us -> 391 us  [scatter(): pl.pallas_call(functools.partial(scatter_body, count, quad), out_shape=[j...]
    ppermute x22 -> x0, waiting for transfers between devices: 80.6 us -> none  [swap(): return lax.ppermute(value, ('fsdp', 'seq'), pairs)]
    ppermute x22 -> x0, starting transfers between devices: 72.4 us -> none  [swap(): return lax.ppermute(value, ('fsdp', 'seq'), pairs)]
    dot_general x23 -> x4, matrix products: 66.2 us -> 10.7 us  [dot_plain(): return jnp.dot(left, right, preferred_element_type=f32)]
    reshape x34 -> x18, local copies, waits for them, and re-layouts: 49 us -> 3.7 us  [the longest x1 0.76 us: local_sixteen(): norm_gains.reshape(-1)]
    dot_general x12 -> x0, matrix products: 41.6 us -> none  [the longest x4 16.9 us: mix_back(): jnp.einsum('bhqk,bqhd->bkhd', probs, grads, preferred_element_type=f32)]
    convert_element_type x27 -> x14, other arithmetic: 59.7 us -> 18.7 us  [the longest x1 6.15 us: local_sixteen(): upper_grad = jax.vjp(gelu_tanh, upper)[1](act_grad)[0].astype(bf16)]
  transfers between devices with their start and end apart: 43 -> 10, of which waited for: 7 -> 0; matrix products, arithmetic and copies ran while one was open for 41% -> 17% of each run, Pallas kernels for 2% -> 25%
where the time goes in v2:
time: 1250 us; the launch traced here: 1230 us
  Pallas kernels  907 us (73%)
  matrix products  160 us (13%)
  local copies, waits for them, and re-layouts  96.7 us (8%)
  other arithmetic  65.4 us (5%)
    pallas_call x2, Pallas kernels, scatter(): pl.pallas_call(functools.partial(scatter_body, count, quad), out_shape=[j...  391 us
    pallas_call x1, Pallas kernels, local_sixteen(): pl.pallas_call(functools.partial(forward_body, batch, scaling), out_shape...  380 us
    dot_general x15, matrix products, dot_left_t(): lax.dot_general(left, right, (((0,), (0,)), ((), ())), preferred_element_...  74.6 us
    dot_general x31, matrix products, dot_right_t(): lax.dot_general(left, right, (((1,), (1,)), ((), ())), preferred_element_...  74.3 us
    pallas_call x4, Pallas kernels, plain_call(): pl.pallas_call(body, grid_spec=grid_spec, out_shape=list(outs), compiler_...  68.3 us
    pallas_call x4, Pallas kernels, trade(): pl.pallas_call(functools.partial(trade_body, count, same), out_shape=jax....  67.4 us
    slice x4, local copies, waits for them, and re-layouts, product_back(): return dot_right_t(halves[0], weight[0]) + dot_right_t(halves[1], weight[1])  27.4 us
  transfers between devices with their start and end apart: 10, of which 0 were waited for; matrix products, arithmetic and copies ran while one was open for 17% of the time, Pallas kernels for 25%

profile of v2, /device:TPU:0, one launch (start us, length us, event | category | flops | bytes accessed | tf_op | source)
XLA Modules:
  0.0 1234.9 jit_solution(444834305905853006)
XLA Ops:
  6.1 12.0 shard_map.329
  28.4 10.7 shard_map.330
  64.0 380.5 %shard_map.331 = (bf16[2,4,4,88,1408]{4,3,2,1,0:T(8,128)(2,1)}, bf16[2,4,4,88,2176]{4,3,2,1,0:T(8,128)(2,1)}, bf16[2,4,4,88,1408]{4,3,2,1,0:T(8,128)(2,1)}, bf16...) custom-call(bf16[256,1408]{1,0:T(8,128)(2,1)} %bitcast.155, ...), custom_call_target="tpu_custom_call" | custom-call | tf_op jit(solution)/shard_map/pallas_call | solution.py:1762
  444.5 11.5 fusion.228
  459.6 4.7 convolution_bitcast_fusion
  464.2 11.0 convolution_add_fusion
  476.2 6.2 fusion.17
  482.4 6.8 convolution_convert_fusion
  489.8 6.1 convolution_convert_fusion.2
  496.1 5.5 fusion.9
  508.2 4.6 fusion.234
  512.8 5.5 fusion.232
  518.3 7.3 fusion.229
  537.4 5.1 fusion.54.refs_2_
  542.5 27.0 %shard_map.332 = (bf16[256,1408]{1,0:T(8,128)(2,1)S(1)}, f32[256,2816]{1,0:T(8,128)}, bf16[256,2816]{1,0:T(8,128)(2,1)}) custom-call(s32[2]{0:T(128)S(1)} %copy-done.7, f32[256,1408]{1,0:T(8,128)} %get-tuple-element.64.refs_1_, bf16[256,1408]{1,0:T(8,128)(2,1)S(1)} %fusion.54.refs_2_, bf16[1408,128]{1,0:T(8,128)(2,1)S(1)} %copy-done.2, ...), custom_call_target="tpu_custom_call" | custom-call | tf_op jit(solution)/shard_map/pallas_call | solution.py:1201
  579.1 5.6 fusion.55.refs_1_
  584.7 27.3 %shard_map.333 = (bf16[256,1408]{1,0:T(8,128)(2,1)S(1)}, f32[256,2816]{1,0:T(8,128)}, bf16[256,2816]{1,0:T(8,128)(2,1)}) custom-call(f32[256,2816]{1,0:T(8,128)} %get-tuple-element.70.refs_0_, bf16[256,1408]{1,0:T(8,128)(2,1)S(1)} %fusion.55.refs_1_, bf16[1408,128]{1,0:T(8,128)(2,1)S(1)} %copy-done.2, f32[128,1408]{1,0:T(8,128)S(1)} %copy-done.4, ...), custom_call_target="tpu_custom_call" | custom-call | tf_op jit(solution)/shard_map/pallas_call | solution.py:1201
  625.4 5.7 fusion.233
  634.9 5.0 convolution_convert_fusion.4
  640.7 9.8 fusion.230
  650.6 7.3 shard_map.334
  695.6 6.7 shard_map.337
  725.2 35.2 %shard_map.335 = f32[16,24,128]{2,1,0:T(8,128)} custom-call(f32[24,128]{1,0:T(8,128)} %fusion.166.source), custom_call_target="tpu_custom_call" | custom-call | tf_op jit(solution)/shard_map/pallas_call | solution.py:95
  765.5 9.5 shard_map.336
  791.1 5.5 add_convert_fusion.5
  796.6 4.5 add_convert_fusion.6
  801.3 5.9 add_convert_fusion.4
  807.2 7.2 add_convert_fusion.2
  814.4 191.6 %shard_map.338 = (f32[2,88,1408]{2,1,0:T(8,128)}, f32[2,88,768]{2,1,0:T(8,128)}, f32[2,64,1408]{2,1,0:T(8,128)}, f32[2,88,2176]{2,1,0:T(8,128)}, f32[2,88,1408]{2,1,0:T(8,128)}) custom-call(bf16[4,4,88,1408]{3,2,1,0:T(8,128)(2,1)} %bitcast.165, bf16[4,4,88,768]{3,2,1,0:T(8,128)(2,1)} %bitcast.172, bf16[4,4,64,1408]{3,2,1,0:T(8,128)(2,1)} %bitcast.190, ...), custom_call_target="tpu_custom_call" | custom-call | tf_op jit(solution)/shard_map/pallas_call | solution.py:334
  1013.3 7.2 add_convert_fusion.1
  1020.5 7.6 add_convert_fusion
  1028.2 199.6 %shard_map.339 = (f32[2,384,768]{2,1,0:T(8,128)}, f32[2,88,3072]{2,1,0:T(8,128)}) custom-call(bf16[4,4,384,768]{3,2,1,0:T(8,128)(2,1)} %bitcast.145, bf16[4,4,88,3072]{3,2,1,0:T(8,128)(2,1)} %bitcast.146), custom_call_target="tpu_custom_call" | custom-call | tf_op jit(solution)/shard_map/pallas_call | solution.py:334
  (521 shorter events, 186.1 us)
Async XLA Ops:
  0.7 52.1 %copy-start = (bf16[2,256,1024]{2,1,0:T(8,128)(2,1)S(1)}, bf16[2,256,1024]{2,1,0:T(8,128)(2,1)}, u32[]{:S(2)}) copy-start(bf16[2,256,1024]{2,1,0:T(8,128)(2,1)} %param.21) | copy-start | bytes 3145732
  0.7 21.1 %copy-start.7 = (s32[2]{0:T(128)S(1)}, s32[2]{0:T(128)}, u32[]{:S(2)}) copy-start(s32[2]{0:T(128)} %refs_0_.1) | copy-start | bytes 28
  0.7 25.1 %copy-start.77 = (bf16[88,1408]{1,0:T(8,128)(2,1)S(1)}, bf16[88,1408]{1,0:T(8,128)(2,1)}, u32[]{:S(2)}) copy-start(bf16[88,1408]{1,0:T(8,128)(2,1)} %param.27) | copy-start | bytes 743428
  19.3 21.4 %copy-start.73 = (bf16[88,1408]{1,0:T(8,128)(2,1)S(1)}, bf16[88,1408]{1,0:T(8,128)(2,1)}, u32[]{:S(2)}) copy-start(bf16[88,1408]{1,0:T(8,128)(2,1)} %param.30) | copy-start | bytes 743428
  19.3 21.4 %slice-start.13 = ((bf16[88,1408]{1,0:T(8,128)(2,1)}), bf16[88,640]{1,0:T(8,128)(2,1)S(1)}, s32[]{:S(2)}) async-start(bf16[88,1408]{1,0:T(8,128)(2,1)} %param.30), calls=%async_computation.13 | async-start | bytes 225280 | tf_op jit(solution)/shard_map/slice | solution.py:1657
  19.3 22.1 %copy-start.70 = (bf16[64,2816]{1,0:T(8,128)(2,1)S(1)}, bf16[64,2816]{1,0:T(8,128)(2,1)}, u32[]{:S(2)}) copy-start(bf16[64,2816]{1,0:T(8,128)(2,1)} %param.31) | copy-start | bytes 1081348
  19.4 22.8 %copy-start.30 = (bf16[2,128,1408]{2,1,0:T(8,128)(2,1)S(1)}, bf16[2,128,1408]{2,1,0:T(8,128)(2,1)}, u32[]{:S(2)}) copy-start(bf16[2,128,1408]{2,1,0:T(8,128)(2,1)} %param.23) | copy-start | bytes 2162692
  22.6 25.7 %copy-start.109 = (s32[704]{0:T(1024)}, s32[704]{0:T(1024)S(1)}, u32[]{:S(2)}) copy-start(s32[704]{0:T(1024)S(1)} %add.401) | copy-start | bytes 8452
  22.7 24.8 %copy-start.103 = (s32[704]{0:T(1024)}, s32[704]{0:T(1024)S(1)}, u32[]{:S(2)}) copy-start(s32[704]{0:T(1024)S(1)} %add.396) | copy-start | bytes 8452
  25.0 19.6 %copy-start.95 = (f32[16,3,88]{2,1,0:T(4,128)}, f32[16,3,88]{2,1,0:T(4,128)S(1)}, u32[]{:S(2)}) copy-start(f32[16,3,88]{2,1,0:T(4,128)S(1)} %reshape.668) | copy-start | bytes 50692
  26.7 17.9 %slice-start.12 = ((bf16[384,1408]{1,0:T(8,128)(2,1)}), bf16[384,640]{1,0:T(8,128)(2,1)S(1)}, s32[]{:S(2)}) async-start(bf16[384,1408]{1,0:T(8,128)(2,1)} %param.34), calls=%async_computation.12 | async-start | bytes 983040 | tf_op jit(solution)/shard_map/slice | solution.py:1657
  482.4 13.6 %slice-start = ((s8[9437184]{0:T(1024)(128)(4,1)}), s8[4194304]{0:T(1024)(128)(4,1)S(1)}, s32[]{:S(2)}) async-start(s8[9437184]{0:T(1024)(128)(4,1)} %bitcast.148), calls=%async_computation | async-start | bytes 8388608
  489.3 523.3 %collective-permute-start.9 = (bf16[1408,3072]{1,0:T(8,128)(2,1)}, bf16[1408,3072]{1,0:T(8,128)(2,1)}, u32[]{:S(2)}, u32[]{:S(2)}) collective-permute-start(bf16[1408,3072]{1,0:T(8,128)(2,1)} %convolution_convert_fusion), channel_id=1, source_target_pairs={{0,1},{1,0},{2,3},{3,2},{4,5},{5,4},{6,7},{7,6},{8,9},{9,8},{10,11... | collective-permute-start | bytes 25952264 | tf_op jit(solution)/shard_map/ppermute | solution.py:743
  495.9 524.6 %collective-permute-start.8 = (bf16[6144,768]{1,0:T(8,128)(2,1)}, bf16[6144,768]{1,0:T(8,128)(2,1)}, u32[]{:S(2)}, u32[]{:S(2)}) collective-permute-start(bf16[6144,768]{1,0:T(8,128)(2,1)} %convolution_convert_fusion.2), channel_id=1, source_target_pairs={{0,1},{1,0},{2,3},{3,2},{4,5},{5,4},{6,7},{7,6},{8,9},{9,8},{10,11... | collective-permute-start | bytes 28311560 | tf_op jit(solution)/shard_map/ppermute | solution.py:743
  542.5 27.1 %copy-start.34 = (bf16[1,4,4,88,768]{4,3,2,1,0:T(8,128)(2,1)S(1)}, bf16[1,4,4,88,768]{4,3,2,1,0:T(8,128)(2,1)}, u32[]{:S(2)}) copy-start(bf16[1,4,4,88,768]{4,3,2,1,0:T(8,128)(2,1)} %get-tuple-element.132) | copy-start | bytes 6488068
  584.7 28.7 %copy-start.42 = (bf16[256,640]{1,0:T(8,128)(2,1)S(1)}, bf16[256,640]{1,0:T(8,128)(2,1)}, u32[]{:S(2)}) copy-start(bf16[256,640]{1,0:T(8,128)(2,1)} %copy-done.41) | copy-start | bytes 983044
  584.7 28.7 %copy-start.52 = (bf16[256,1408]{1,0:T(8,128)(2,1)S(1)}, bf16[256,1408]{1,0:T(8,128)(2,1)}, u32[]{:S(2)}) copy-start(bf16[256,1408]{1,0:T(8,128)(2,1)} %get-tuple-element.87) | copy-start | bytes 2162692
  612.8 37.7 %collective-permute-start = (bf16[256,2816]{1,0:T(8,128)(2,1)}, bf16[256,2816]{1,0:T(8,128)(2,1)}, u32[]{:S(2)}, u32[]{:S(2)}) collective-permute-start(bf16[256,2816]{1,0:T(8,128)(2,1)} %get-tuple-element.75), channel_id=1, source_target_pairs={{0,1},{1,0},{2,3},{3,2},{4,5},{5,4},{6,7},{7,6},{8,9},{9,8},{10,11... | collective-permute-start | bytes 4325384 | tf_op jit(solution)/shard_map/ppermute | solution.py:743
  613.3 81.7 %collective-permute-start.2 = (bf16[256,2816]{1,0:T(8,128)(2,1)}, bf16[256,2816]{1,0:T(8,128)(2,1)}, u32[]{:S(2)}, u32[]{:S(2)}) collective-permute-start(bf16[256,2816]{1,0:T(8,128)(2,1)} %get-tuple-element.83), channel_id=1, source_target_pairs={{0,1},{1,0},{2,3},{3,2},{4,5},{5,4},{6,7},{7,6},{8,9},{9,8},{10,11... | collective-permute-start | bytes 4325384 | tf_op jit(solution)/shard_map/ppermute | solution.py:743
  615.5 163.9 %collective-permute-start.4 = (bf16[1408,768]{1,0:T(8,128)(2,1)}, bf16[1408,768]{1,0:T(8,128)(2,1)}, u32[]{:S(2)}, u32[]{:S(2)}) collective-permute-start(bf16[1408,768]{1,0:T(8,128)(2,1)} %convolution_convert_fusion.6), channel_id=1, source_target_pairs={{0,1},{1,0},{2,3},{3,2},{4,5},{5,4},{6,7},{7,6},{8,9},{9,8},{10,11... | collective-permute-start | bytes 6488072 | tf_op jit(solution)/shard_map/ppermute | solution.py:743
  650.5 129.8 %collective-permute-start.3 = (bf16[1408,1408]{1,0:T(8,128)(2,1)}, bf16[1408,1408]{1,0:T(8,128)(2,1)}, u32[]{:S(2)}, u32[]{:S(2)}) collective-permute-start(bf16[1408,1408]{1,0:T(8,128)(2,1)} %convolution_convert_fusion.4), channel_id=1, source_target_pairs={{0,1},{1,0},{2,3},{3,2},{4,5},{5,4},{6,7},{7,6},{8,9},{9,8},{10,11... | collective-permute-start | bytes 11894792 | tf_op jit(solution)/shard_map/ppermute | solution.py:743
  672.0 14.3 %copy-start.60 = (f32[256,1408]{1,0:T(8,128)}, f32[256,1408]{1,0:T(8,128)S(1)}, u32[]{:S(2)}) copy-start(f32[256,1408]{1,0:T(8,128)S(1)} %fusion.238) | copy-start | bytes 4325380
  695.0 27.9 %collective-permute-start.1 = (f32[9888]{0:T(1024)S(1)}, f32[9888]{0:T(1024)}, u32[]{:S(2)}, u32[]{:S(2)}) collective-permute-start(f32[9888]{0:T(1024)S(1)} %constant_dynamic-update-slice_fusion.1), channel_id=1, source_target_pairs={{0,1},{1,0},{2,3},{3,2},{4,5},{5,4},{6,7},{7,6},{8,9},{9,8},{10,11... | collective-permute-start | bytes 118664 | tf_op jit(solution)/shard_map/ppermute | solution.py:743
  720.7 43.8 %copy-start.78 = (bf16[88,1408]{1,0:T(8,128)(2,1)S(1)}, bf16[88,1408]{1,0:T(8,128)(2,1)}, u32[]{:S(2)}) copy-start(bf16[88,1408]{1,0:T(8,128)(2,1)} %param.27) | copy-start | bytes 743428
  722.9 55.8 %copy-start.108 = (bf16[2,1408]{1,0:T(2,128)(2,1)S(1)}, bf16[2,1408]{1,0:T(2,128)(2,1)}, u32[]{:S(2)}) copy-start(bf16[2,1408]{1,0:T(2,128)(2,1)} %param.20) | copy-start | bytes 16900
  722.9 56.4 %copy-start.117 = (f32[2,16]{1,0:T(2,128)S(1)}, f32[2,16]{1,0:T(2,128)}, u32[]{:S(2)}) copy-start(f32[2,16]{1,0:T(2,128)} %param.35) | copy-start | bytes 388
  722.9 56.7 %copy-start.74 = (bf16[88,1408]{1,0:T(8,128)(2,1)S(1)}, bf16[88,1408]{1,0:T(8,128)(2,1)}, u32[]{:S(2)}) copy-start(bf16[88,1408]{1,0:T(8,128)(2,1)} %param.30) | copy-start | bytes 743428
  722.9 84.3 %collective-permute-start.6 = (bf16[1408,2176]{1,0:T(8,128)(2,1)}, bf16[1408,2176]{1,0:T(8,128)(2,1)}, u32[]{:S(2)}, u32[]{:S(2)}) collective-permute-start(bf16[1408,2176]{1,0:T(8,128)(2,1)} %convolution_convert_fusion.1), channel_id=1, source_target_pairs={{0,1},{1,0},{2,3},{3,2},{4,5},{5,4},{6,7},{7,6},{8,9},{9,8},{10,11... | collective-permute-start | bytes 18382856 | tf_op jit(solution)/shard_map/ppermute | solution.py:743
  764.5 22.6 %copy-start.118 = (f32[2,16]{1,0:T(2,128)}, f32[2,16]{1,0:T(2,128)S(1)}, u32[]{:S(2)}) copy-start(f32[2,16]{1,0:T(2,128)S(1)} %reshape.664) | copy-start | bytes 388
  764.7 22.5 %copy-start.43 = (bf16[256,640]{1,0:T(8,128)(2,1)S(1)}, bf16[256,640]{1,0:T(8,128)(2,1)}, u32[]{:S(2)}) copy-start(bf16[256,640]{1,0:T(8,128)(2,1)} %copy-done.41) | copy-start | bytes 983044
  779.3 21.9 %collective-permute-start.7 = (bf16[1408,1408]{1,0:T(8,128)(2,1)}, bf16[1408,1408]{1,0:T(8,128)(2,1)}, u32[]{:S(2)}, u32[]{:S(2)}) collective-permute-start(bf16[1408,1408]{1,0:T(8,128)(2,1)} %convolution_convert_fusion.3), channel_id=1, source_target_pairs={{0,1},{1,0},{2,3},{3,2},{4,5},{5,4},{6,7},{7,6},{8,9},{9,8},{10,11... | collective-permute-start | bytes 11894792 | tf_op jit(solution)/shard_map/ppermute | solution.py:743
  780.3 16.3 %collective-permute-start.5 = (bf16[1024,1408]{1,0:T(8,128)(2,1)}, bf16[1024,1408]{1,0:T(8,128)(2,1)}, u32[]{:S(2)}, u32[]{:S(2)}) collective-permute-start(bf16[1024,1408]{1,0:T(8,128)(2,1)} %convolution_convert_fusion.5), channel_id=1, source_target_pairs={{0,1},{1,0},{2,3},{3,2},{4,5},{5,4},{6,7},{7,6},{8,9},{9,8},{10,11... | collective-permute-start | bytes 8650760 | tf_op jit(solution)/shard_map/ppermute | solution.py:743
  (118 other events, 437.7 us)

commit v3 on v2

--- a/solution.py
+++ b/solution.py
@@ -718,6 +718,732 @@
     plan.ready(down_w)
     for w in range(7):
         plan.finish(w)
+
+
+def gelu_slope(value):
+    bent = gelu_parts(value)
+    inner = 0.7978845608028654 * (1.0 + 3 * 0.044715 * value * value)
+    return 0.5 * (1.0 + bent) + 0.5 * value * (1.0 - bent * bent) * inner
+
+
+def norm_back(value, gain, grad):
+    center = value - jnp.mean(value, axis=-1, keepdims=True)
+    factor = lax.rsqrt(jnp.mean(center * center, axis=-1, keepdims=True) + norm_eps)
+    normed = center * factor
+    gain_grad = jnp.sum(grad * normed, axis=0, keepdims=True)
+    grad = grad * gain
+    first = jnp.mean(grad, axis=-1, keepdims=True)
+    second = jnp.mean(grad * normed, axis=-1, keepdims=True)
+    return factor * (grad - first - normed * second), gain_grad
+
+
+class TwinSum:
+    def __init__(self, there, sums, send, recv, local, out_buffer, in_buffer, sibling):
+        self.there, self.sums = there, sums
+        self.send, self.recv, self.local = send, recv, local
+        self.out_buffer, self.in_buffer, self.sibling = out_buffer, in_buffer, sibling
+
+    def away(self, w, index, place, source):
+        return pltpu.make_async_remote_copy(
+            src_ref=source,
+            dst_ref=place(self.there[w]),
+            send_sem=self.send.at[w, index],
+            recv_sem=self.recv.at[w, index],
+            device_id=self.sibling,
+            device_id_type=MESH,
+        )
+
+    def run(self, w, places, shape, other, own, between=None):
+        depth = self.out_buffer.shape[0]
+
+        def slot(buffer, index):
+            views = [pl.ds(0, n) for n in shape(index)]
+            return buffer.at[(index % depth, *views)]
+
+        for index, place in enumerate(places):
+            if index >= depth:
+                before = index - depth
+                self.away(w, before, places[before], slot(self.out_buffer, before)).wait_send()
+            target = slot(self.out_buffer, index)
+            target[...] = other(index).astype(bf16)
+            self.away(w, index, place, target).start()
+        for index in range(max(0, len(places) - depth), len(places)):
+            self.away(w, index, places[index], slot(self.out_buffer, index)).wait_send()
+        if between is not None:
+            between()
+
+        def fetch(index):
+            return pltpu.make_async_copy(
+                places[index](self.there[w]),
+                slot(self.in_buffer, index),
+                self.local.at[index % depth],
+            )
+
+        def store(index):
+            return pltpu.make_async_copy(
+                slot(self.out_buffer, index),
+                places[index](self.sums[w]),
+                self.local.at[depth + index % depth],
+            )
+
+        def begin(index):
+            self.away(w, index, places[index], slot(self.out_buffer, index)).wait_recv()
+            fetch(index).start()
+
+        begin(0)
+        for index in range(len(places)):
+            if index + 1 < len(places):
+                begin(index + 1)
+            value = own(index)
+            fetch(index).wait()
+            if index >= depth:
+                store(index - depth).wait()
+            target = slot(self.out_buffer, index)
+            target[...] = (value + slot(self.in_buffer, index)[...].astype(f32)).astype(bf16)
+            store(index).start()
+        for index in range(max(0, len(places) - depth), len(places)):
+            store(index).wait()
+
+
+def lane_places(height, width, size):
+    starts = [(start, min(size, width - start)) for start in range(0, width, size)]
+    places = [
+        lambda ref, start=start, extent=extent: ref.at[:, :, :, pl.ds(start, extent)]
+        for start, extent in starts
+    ]
+    return starts, places, lambda index: (4, 4, height, starts[index][1])
+
+
+def mlp_back_body(batch, *refs):
+    refs = list(refs)
+    take = refs.pop
+    out_grad, activated, upper, mlp_in, after_cross, order, gains = (take(0) for _ in range(7))
+    up_w, down_w = take(0), take(0)
+    block_out, cross_grad, gain_grad = (take(0) for _ in range(3))
+    sums = [take(0), take(0)]
+    there = [take(0), take(0)]
+    upper_grad, turned, total, down_buffer, up_buffer = (take(0) for _ in range(5))
+    out_down, in_down, out_up, in_up = (take(0) for _ in range(4))
+    semaphore, send, recv, local = refs
+    rows, width = after_cross.shape
+    size = rows // batch
+    block = activated.shape[1] // 16
+    half_width = out_grad.shape[2]
+    me = lax.axis_index("fsdp")
+    core = lax.axis_index("seq")
+    sibling = (me, 1 - core)
+    greet([sibling])
+
+    planes = [
+        lambda ref, k=k, q=q: ref.at[k, q] for k in range(4) for q in range(4)
+    ]
+    down = TwinSum(there, sums, send, recv, local, out_down, in_down, sibling)
+
+    def down_part(half):
+        def part(index):
+            return dot_left_t(activated[:, index * block : (index + 1) * block], out_grad[half])
+
+        return part
+
+    def down_back():
+        depth = down_buffer.shape[0]
+
+        def copy(index):
+            k, q = divmod(index, 4)
+            return pltpu.make_async_copy(
+                down_w.at[:, k, q], down_buffer.at[index % depth], semaphore.at[index % depth]
+            )
+
+        for index in range(depth - 1):
+            copy(index).start()
+        total[...] = jnp.zeros_like(total)
+        for index in range(16):
+            if index + depth - 1 < 16:
+                copy(index + depth - 1).start()
+            copy(index).wait()
+            first, second = down_buffer[index % depth, 0], down_buffer[index % depth, 1]
+            shard = jnp.bitwise_xor(me, index)
+            lanes = pl.ds(pl.multiple_of(shard * block, block), block)
+            grad = dot_right_t(out_grad[0], first) + dot_right_t(out_grad[1], second)
+            grad = (grad * gelu_slope(upper[:, lanes])).astype(bf16)
+            in_half = pl.multiple_of((shard % 8) * block, block)
+            upper_grad[shard // 8, :, pl.ds(in_half, block)] = grad
+            active = activated[:, index * block : (index + 1) * block]
+            total[0] += dot_plain(active, first)
+            total[1] += dot_plain(active, second)
+        cut = width - half_width
+        block_out[:, pl.ds(0, half_width)] = (
+            after_cross[:, pl.ds(0, half_width)] + total[0]
+        ).astype(bf16)
+        block_out[:, pl.ds(half_width, cut)] = (
+            after_cross[:, pl.ds(half_width, cut)] + total[1][:, :cut]
+        ).astype(bf16)
+
+    down.run(
+        0, planes, lambda index: (block, half_width), down_part(1 - core), down_part(core), down_back
+    )
+
+    turned[...] = jnp.transpose(mlp_in[...])
+    starts, places, shape = lane_places(width // 16, upper_grad.shape[2], out_up.shape[4])
+    up = TwinSum(there, sums, send, recv, local, out_up, in_up, sibling)
+
+    def up_part(half):
+        def part(index):
+            start, extent = starts[index]
+            value = dot_plain(turned[...], upper_grad[half, :, pl.ds(start, extent)])
+            return value.reshape(4, 4, width // 16, extent)
+
+        return part
+
+    def up_back():
+        tiles = tiles_of(upper_grad.shape[2], 512)
+
+        def body(index, tile):
+            half, start, extent = tiles[index]
+            value = dot_right_t(upper_grad[half, :, pl.ds(start, extent)], tile)
+            if index == 0:
+                cross_grad[...] = value
+            else:
+                cross_grad[...] += value
+
+        stream(up_w, tiles, up_buffer, semaphore, body)
+        gain_grad[...] = jnp.zeros_like(gain_grad)
+        for b in range(batch):
+            rows_b = pl.ds(b * size, size)
+            grad = exact_restore(order[...], cross_grad[rows_b, :])
+            value, gain_part = norm_back(after_cross[rows_b, :], gains[2:3, :], grad)
+            gain_grad[0:1, :] += gain_part
+            result = jnp.concatenate(
+                [out_grad[0, rows_b, :], out_grad[1, rows_b, : width - half_width]], axis=1
+            )
+            cross_grad[rows_b, :] = result.astype(f32) + value
+
+    up.run(1, places, shape, up_part(1 - core), up_part(core), up_back)
+
+
+class ScatterPlan:
+    def __init__(self, sums, out, half, passing, quarter, leaving, last, slots, totals, sems):
+        self.sums, self.out, self.half = sums, out, half
+        self.passing, self.quarter, self.leaving, self.last = passing, quarter, leaving, last
+        self.slots, self.totals = slots, totals
+        self.send, self.recv, self.load, self.store = sems
+        self.core, self.first_mask, self.second_mask, self.at, self.sibling = neighbours(4)
+        self.far_peers = [self.at(4 * k) for k in range(1, 4)]
+
+    def peers(self):
+        return [*self.far_peers, self.at(self.first_mask), self.at(self.second_mask), self.sibling]
+
+    def copy(self, w, slot, source, target, peer):
+        return pltpu.make_async_remote_copy(
+            src_ref=source,
+            dst_ref=target,
+            send_sem=self.send.at[w, slot],
+            recv_sem=self.recv.at[w, slot],
+            device_id=peer,
+            device_id_type=MESH,
+        )
+
+    def give(self, w, n):
+        q = 3 if n == 0 else self.second_mask
+        return self.copy(
+            w, n, self.sums[w].at[:, q], self.half[w].at[n], self.at(self.second_mask)
+        )
+
+    def hand(self, w):
+        return self.copy(w, 2, self.passing[w], self.quarter[w], self.at(self.first_mask))
+
+    def far(self, w, k):
+        return self.copy(
+            w, 2 + k, self.leaving[w].at[k - 1], self.last[w].at[k - 1], self.far_peers[k - 1]
+        )
+
+    def chunks(self, w):
+        height, width = self.out[w].shape[1:]
+        which = 0 if height <= self.slots[0].shape[1] else 1
+        size = self.slots[which].shape[2]
+        return which, height, [(s, min(size, width - s)) for s in range(0, width, size)]
+
+    def add(self, w, groups, finish):
+        which, height, chunks = self.chunks(w)
+        slots = self.slots[which]
+        for start, extent in chunks:
+            lanes = pl.ds(start, extent)
+            views = []
+            for planes in groups:
+                for plane in planes:
+                    at = len(views)
+                    view = slots.at[at, pl.ds(0, height), pl.ds(0, extent)]
+                    copy = pltpu.make_async_copy(plane.at[:, lanes], view, self.load.at[at])
+                    copy.start()
+                    views.append((view, copy))
+            at = 0
+            pending = []
+            for index, planes in enumerate(groups):
+                mine = views[at : at + len(planes)]
+                at += len(planes)
+                for _, copy in mine:
+                    copy.wait()
+                pending.extend(finish(index, lanes, extent, [view for view, _ in mine]))
+            for copy in pending:
+                copy.wait()
+
+    def added(self, views, extent, put):
+        step = 256 if extent % 256 == 0 else 128
+
+        @pl.loop(0, extent // step)
+        def _(i):
+            lanes = pl.ds(pl.multiple_of(i * step, step), step)
+            value = views[0][:, lanes].astype(f32)
+            for view in views[1:]:
+                value = value + view[:, lanes].astype(f32)
+            put(lanes, value)
+
+    def rounded(self, targets):
+        def finish(index, lanes, extent, views):
+            def put(at, value):
+                views[0][:, at] = value.astype(bf16)
+
+            self.added(views, extent, put)
+            copy = pltpu.make_async_copy(
+                views[0], targets[index].at[:, lanes], self.store.at[index]
+            )
+            copy.start()
+            return [copy]
+
+        return finish
+
+    def begin(self, w):
+        self.give(w, 0).start()
+        self.give(w, 1).start()
+
+    def middle(self, w):
+        self.give(w, 0).wait_recv()
+        mask = self.first_mask
+        groups = [[self.half[w].at[0, k], self.sums[w].at[k, mask]] for k in range(4)]
+        self.add(w, groups, self.rounded([self.passing[w].at[k] for k in range(4)]))
+        self.hand(w).start()
+
+    def leave(self, w):
+        self.give(w, 1).wait_recv()
+        self.hand(w).wait_recv()
+        groups = [
+            [self.half[w].at[1, k], self.sums[w].at[k, 0], self.quarter[w].at[k]]
+            for k in range(1, 4)
+        ]
+        self.add(w, groups, self.rounded([self.leaving[w].at[k] for k in range(3)]))
+        for k in range(1, 4):
+            self.far(w, k).start()
+
+    def close(self, w):
+        for k in range(1, 4):
+            self.far(w, k).wait_recv()
+        group = [self.half[w].at[1, 0], self.sums[w].at[0, 0], self.quarter[w].at[0]]
+        group += [self.last[w].at[k] for k in range(3)]
+        which, height, _ = self.chunks(w)
+        totals = self.totals[which]
+
+        def finish(index, lanes, extent, views):
+            total = totals.at[pl.ds(0, height), pl.ds(0, extent)]
+
+            def put(at, value):
+                total[:, at] = value
+
+            self.added(views, extent, put)
+            target = self.out[w].at[self.core, :, lanes]
+            here = pltpu.make_async_copy(total, target, self.store.at[0])
+            there = self.copy(w, 6 + (0 if lanes.start == 0 else 1), total, target, self.sibling)
+            here.start()
+            there.start()
+            here.wait()
+            there.wait_send()
+            there.wait_recv()
+            return []
+
+        self.add(w, [group], finish)
+
+    def finish(self, w):
+        self.give(w, 0).wait_send()
+        self.give(w, 1).wait_send()
+        self.hand(w).wait_send()
+        for k in range(1, 4):
+            self.far(w, k).wait_send()
+
+
+def rest_back_body(batch, scaling, *refs):
+    refs = list(refs)
+    take = refs.pop
+
+    def several(count):
+        return [take(0) for _ in range(count)]
+
+    cross_cat, attn_cat, cross_in, attn_in, text, after_self, hidden, normed = several(8)
+    gains, order, heads_ref = several(3)
+    tables = several(3)
+    valid = take(0)
+    skip_w, qkv_w, pair_w, query_w, keyval_w = several(5)
+    cross_keyval, cq_proj, ckey_mine, qkv, keyval_here, keyval_there, cross_grad = several(7)
+    summed = several(2)
+    text_grad, gain_grads, shift_grad, normed_grad = several(4)
+    out = several(7)
+    own_sums, there = several(5), several(5)
+    half, passing, quarter, leaving, last = (several(7) for _ in range(5))
+    grad, wide, factor, back = several(4)
+    query, mix_grad, total, keyval, proj, turned, halves = several(7)
+    buffer, out_buffer, in_buffer = several(3)
+    slots, totals = several(2), several(2)
+    landed = take(0)
+    semaphore, loads, twin_send, twin_recv, twin_local = several(5)
+    exchange_send, exchange_recv, send, recv, add_load, add_store = several(6)
+    rows, width = hidden.shape
+    size = rows // batch
+    block = width // 16
+    core = lax.axis_index("seq")
+    down, up, query_s, keyval_s, pair_s, qkv_s, skip_s = range(7)
+    plan = ScatterPlan(
+        summed + own_sums, out, half, passing, quarter, leaving, last, slots, totals,
+        (send, recv, add_load, add_store),
+    )
+    twin = TwinSum(
+        there, own_sums, twin_send, twin_recv, twin_local, out_buffer, in_buffer, plan.sibling
+    )
+    greet(plan.peers())
+    plan.begin(down)
+    plan.begin(up)
+
+    first_lanes, last_lanes = pl.ds(0, width), pl.ds(width, width)
+
+    def load(*pairs):
+        copies = [
+            pltpu.make_async_copy(source, target, loads.at[at])
+            for at, (source, target) in enumerate(pairs)
+        ]
+        for copy in copies:
+            copy.start()
+        for copy in copies:
+            copy.wait()
+
+    load(
+        (cross_grad, grad),
+        (cross_keyval, keyval),
+        (cq_proj, proj.at[:, first_lanes]),
+        (ckey_mine, proj.at[:, last_lanes]),
+    )
+    gain_grads[...] = jnp.zeros_like(gain_grads)
+    shift_grad[...] = jnp.zeros_like(shift_grad)
+
+    def each(body):
+        for b in range(batch):
+            body(b, pl.ds(b * size, size))
+
+    def back_through(weight, tiles, factor_of, target):
+        def body(index, tile):
+            value = dot_right_t(factor_of(*tiles[index]), tile)
+            if index == 0:
+                target[...] = value
+            else:
+                target[...] += value
+
+        stream(weight, tiles, buffer, semaphore, body)
+
+    def restored(target):
+        def part(b, rows_b):
+            target[rows_b, :] = dot_right_t(wide[rows_b, :].astype(bf16), order[...]).astype(bf16)
+
+        each(part)
+
+    def split_lanes(value, rows_b, start):
+        halves[0, rows_b, pl.ds(start, 768)] = value[:, :768]
+        halves[1, rows_b, pl.ds(start, width - 768)] = value[:, 768:]
+        halves[1, rows_b, pl.ds(start + width - 768, 2 * 768 - width)] = jnp.zeros(
+            (value.shape[0], 2 * 768 - width), bf16
+        )
+
+    def attention_back(sources, table_refs, masked, put):
+        back[...] = jnp.zeros_like(back)
+        total[...] = jnp.zeros_like(total)
+
+        def prepare(b, rows_b):
+            value, scale = head_norm(proj[rows_b, first_lanes], heads_ref)
+            wide[rows_b, :] = value
+            factor[rows_b, :] = scale
+            turned_value = turn(value, table_refs) if table_refs else value
+            query[rows_b, :] = turned_value.astype(bf16)
+
+        each(prepare)
+
+        @pl.loop(0, batch)
+        def _(b):
+            rows_b = pl.ds(pl.multiple_of(b * size, size), size)
+            for head in range(HEADS):
+                lanes, inside = window_of(head, width)
+                behind = shift_lanes(lanes, width)
+                queries = query[rows_b, lanes] * inside.astype(bf16)
+                keys = pair_rows(sources, b, size, lanes)
+                scores = dot_right_t(queries, keys) * scaling
+                if masked:
+                    scores = jnp.where(valid[pl.ds(b, 1), :] > 0.5, scores, masked_value)
+                probs, _ = softmax_of(scores)
+                grads = mix_grad[rows_b, lanes] * inside.astype(bf16)
+                prob_grad = dot_right_t(grads, pair_rows(sources, b, size, behind))
+                score_grad = softmax_back(probs, prob_grad).astype(bf16)
+                value_grad = dot_left_t(probs.astype(bf16), grads)
+                key_grad = dot_left_t(score_grad, queries) * scaling
+                back[rows_b, lanes] += dot_plain(score_grad, keys) * (inside * scaling)
+                for at in range(2):
+                    part = slice(at * size, (at + 1) * size)
+                    total[at, rows_b, lanes] += key_grad[part]
+                    total[at, rows_b, behind] += value_grad[part]
+
+        def finish(b, rows_b):
+            value = back[rows_b, :]
+            if table_refs:
+                value = turn_back(value, table_refs)
+            value = head_norm_back(value, wide[rows_b, :], factor[rows_b, :], heads_ref)
+            put(value.astype(bf16), rows_b)
+
+        each(finish)
+
+    def exchange(index):
+        return pltpu.make_async_remote_copy(
+            src_ref=keyval.at[pl.ds(0, rows), :],
+            dst_ref=landed.at[index],
+            send_sem=exchange_send.at[index],
+            recv_sem=exchange_recv.at[index],
+            device_id=plan.sibling,
+            device_id_type=MESH,
+        )
+
+    def keys_back(index, mine, table_refs, put):
+        def part(b, rows_b):
+            normed_keys, scale = head_norm(proj[rows_b, last_lanes], heads_ref)
+            value = total[mine, rows_b, first_lanes] + landed[index, rows_b, first_lanes].astype(f32)
+            if table_refs:
+                value = turn_back(value, table_refs)
+            key_grad = head_norm_back(value, normed_keys, scale, heads_ref).astype(bf16)
+            value = total[mine, rows_b, last_lanes] + landed[index, rows_b, last_lanes].astype(f32)
+            put(key_grad, value.astype(bf16), rows_b)
+
+        each(part)
+
+    def twin_product(w, extent, height, left, right):
+        starts, places, shape = lane_places(height, extent, out_buffer.shape[4])
+
+        def part(which):
+            def value(index):
+                start, lanes = starts[index]
+                product = dot_plain(left(which), right(which, start, lanes))
+                return product.reshape(4, 4, height, lanes)
+
+            return value
+
+        twin.run(w, places, shape, part(1 - core), part(core))
+
+    halves[1, :, first_lanes] = grad[...].astype(bf16)
+    pair_tiles = tiles_of(width, 384, (1,))
+    back_through(
+        pair_w, pair_tiles, lambda at, start, extent: halves[at, :, pl.ds(start, extent)], wide
+    )
+    restored(mix_grad)
+    attention_back([keyval], (), True, lambda value, rows_b: split_lanes(value, rows_b, width))
+    keyval[pl.ds(0, rows), :] = total[1 - core].astype(bf16)
+    exchange(0).start()
+    plan.middle(down)
+    query_tiles = tiles_of(768, 384)
+    back_through(
+        query_w,
+        query_tiles,
+        lambda at, start, extent: halves[at, :, pl.ds(width + start, extent)],
+        wide,
+    )
+
+    def self_part(b, rows_b):
+        value = exact_restore(order[...], wide[rows_b, :])
+        value, gain_part = norm_back(after_self[rows_b, :], gains[1:2, :], value)
+        gain_grads[1:2, :] += gain_part
+        value = grad[rows_b, :] + value
+        grad[rows_b, :] = value
+        halves[0, rows_b, first_lanes] = value.astype(bf16)
+
+    each(self_part)
+    pair_tiles_two = tiles_of(width, 384, (0,))
+    back_through(
+        pair_w, pair_tiles_two, lambda at, start, extent: halves[at, :, pl.ds(start, extent)], wide
+    )
+    restored(mix_grad)
+    turned[0] = jnp.transpose(attn_cat[...])
+    turned[1] = jnp.transpose(cross_cat[...])
+    twin_product(
+        2,
+        width,
+        block,
+        lambda at: turned[at],
+        lambda at, start, extent: halves[at, :, pl.ds(start, extent)],
+    )
+    plan.begin(pair_s)
+    turned[0] = jnp.transpose(cross_in[...])
+    twin_product(
+        0,
+        768,
+        block,
+        lambda at: turned[0],
+        lambda at, start, extent: halves[at, :, pl.ds(width + start, extent)],
+    )
+    plan.begin(query_s)
+    plan.middle(up)
+    plan.leave(down)
+
+    exchange(0).wait()
+
+    def text_part(key_grad, value_grad, rows_b):
+        halves[0, rows_b, first_lanes] = key_grad
+        halves[1, rows_b, first_lanes] = value_grad
+
+    keys_back(0, core, (), text_part)
+    text_width = text.shape[1]
+    turned[0, pl.ds(0, text_width), :] = jnp.transpose(text[...])
+    twin_product(
+        1,
+        width,
+        text_width // 16,
+        lambda at: turned[0, pl.ds(0, text_width), :],
+        lambda at, start, extent: halves[at, :, pl.ds(start, extent)],
+    )
+    plan.begin(keyval_s)
+    keyval_tiles = tiles_of(width, 384)
+    back_through(
+        keyval_w,
+        keyval_tiles,
+        lambda at, start, extent: halves[at, :, pl.ds(start, extent)],
+        text_grad,
+    )
+
+    load(
+        (qkv, proj),
+        (keyval_here, keyval.at[pl.ds(0, rows), :]),
+        (keyval_there, keyval.at[pl.ds(rows, rows), :]),
+    )
+
+    def query_part(value, rows_b):
+        halves[0, rows_b, first_lanes] = value
+
+    sources = [keyval.at[pl.ds(0, rows), :], keyval.at[pl.ds(rows, rows), :]]
+    attention_back(sources, tables, False, query_part)
+    keyval[pl.ds(0, rows), :] = total[1].astype(bf16)
+    exchange(1).start()
+    plan.leave(up)
+    plan.close(down)
+    plan.middle(pair_s)
+    plan.middle(query_s)
+    exchange(1).wait()
+
+    def key_part(key_grad, value_grad, rows_b):
+        halves[1, rows_b, first_lanes] = key_grad
+        split_lanes(value_grad, rows_b, width)
+
+    keys_back(1, 0, tables, key_part)
+    turned[0] = jnp.transpose(attn_in[...])
+    wide_half = halves.shape[2]
+    twin_product(
+        3,
+        wide_half,
+        block,
+        lambda at: turned[0],
+        lambda at, start, extent: halves[at, :, pl.ds(start, extent)],
+    )
+    plan.begin(qkv_s)
+    qkv_tiles = tiles_of(wide_half, 384)
+    back_through(
+        qkv_w, qkv_tiles, lambda at, start, extent: halves[at, :, pl.ds(start, extent)], wide
+    )
+
+    def hidden_part(b, rows_b):
+        value = exact_restore(order[...], wide[rows_b, :])
+        shift_grad[b : b + 1, :] = jnp.sum(value, axis=0, keepdims=True)
+        value, gain_part = norm_back(hidden[rows_b, :], gains[0:1, :], value)
+        gain_grads[0:1, :] += gain_part
+        halves[0, rows_b, first_lanes] = (grad[rows_b, :] + value).astype(bf16)
+
+    each(hidden_part)
+    plan.close(up)
+    plan.middle(keyval_s)
+    plan.leave(pair_s)
+    plan.leave(query_s)
+
+    for at in range(2):
+        for part in range(2):
+            turned[at, pl.ds(part * (width // 2), width // 2), :] = jnp.transpose(
+                normed[at, part]
+            )
+    twin_product(
+        4,
+        width,
+        block,
+        lambda at: turned[at],
+        lambda at, start, extent: halves[0, :, pl.ds(start, extent)],
+    )
+    plan.begin(skip_s)
+    plan.leave(keyval_s)
+    plan.middle(qkv_s)
+    skip_tiles = tiles_of(width, 384)
+
+    def skip_body(index, tile):
+        at, start, extent = skip_tiles[index]
+        value = dot_right_t(halves[0, :, pl.ds(start, extent)], tile)
+        lanes = pl.ds(at * width, width)
+        if start == 0:
+            total[0, :, lanes] = value
+        else:
+            total[0, :, lanes] += value
+
+    stream(skip_w, skip_tiles, buffer, semaphore, skip_body)
+    keep = pltpu.make_async_copy(total.at[0], normed_grad, loads.at[0])
+    keep.start()
+    plan.close(pair_s)
+    plan.close(query_s)
+    plan.close(keyval_s)
+    plan.leave(qkv_s)
+    plan.middle(skip_s)
+    plan.close(qkv_s)
+    plan.leave(skip_s)
+    plan.close(skip_s)
+    keep.wait()
+    for w in range(7):
+        plan.finish(w)
+
+
+def joined_back_body(batch, normed_grad, latent, skip, skip_gain, order_skip, joined, gain_grad):
+    width = latent.shape[1]
+    size = latent.shape[0] // batch
+    upper_half = lax.axis_index("fsdp") >= 8
+    gain_grad[...] = jnp.zeros_like(gain_grad)
+    for b in range(batch):
+        rows_b = pl.ds(b * size, size)
+        near, away = 0.0, 0.0
+        for at in range(2):
+            part = normed_grad[rows_b, at * width : (at + 1) * width]
+            near = near + exact_restore(order_skip[at], part[:, : width // 2])
+            away = away + exact_restore(order_skip[at], part[:, width // 2 :])
+        left = latent[rows_b, :].astype(f32)
+        right = skip[rows_b, :].astype(f32)
+        left_grad = jnp.where(upper_half, away, near)
+        right_grad = jnp.where(upper_half, near, away)
+
+        def mean(first, second):
+            total = jnp.sum(first, axis=1, keepdims=True) + jnp.sum(second, axis=1, keepdims=True)
+            return total / (2 * width)
+
+        middle = mean(left, right)
+        left, right = left - middle, right - middle
+        factor = lax.rsqrt(mean(left * left, right * right) + norm_eps)
+        left, right = left * factor, right * factor
+        gain_grad[0:1, :width] += jnp.sum(left_grad * left, axis=0, keepdims=True)
+        gain_grad[0:1, width:] += jnp.sum(right_grad * right, axis=0, keepdims=True)
+        left_grad = left_grad * skip_gain[:, :width]
+        right_grad = right_grad * skip_gain[:, width:]
+        first = mean(left_grad, right_grad)
+        second = mean(left_grad * left, right_grad * right)
+        joined[0, rows_b, :] = factor * (left_grad - first - left * second)
+        joined[1, rows_b, :] = factor * (right_grad - first - right * second)
 
 
 class Links:
@@ -1779,158 +2505,126 @@
             collective_id=7, has_side_effects=True, vmem_limit_bytes=62 * 2**20
         ),
     )(*given, *shards)
-    w_skip, w_qkv, w_pair, w_query, w_keyval, w_up, w_down = (
-        g.reshape(2, 16 * g.shape[3], g.shape[4]) for g in gathered
-    )
-
-    def cut_halves(value):
-        cut = (value.shape[1] // 2 + 127) // 128 * 128
-        second = value[:, cut:]
-        return value[:, :cut], jnp.pad(second, ((0, 0), (0, cut - second.shape[1])))
-
-    def product(halves, weight):
-        return dot_plain(halves[0], weight[0]) + dot_plain(halves[1], weight[1])
-
-    def product_back(halves, weight):
-        return dot_right_t(halves[0], weight[0]) + dot_right_t(halves[1], weight[1])
-
-    def sum_twins(*pairs):
-        (left, right), (left_two, right_two) = pairs
-        there = dot_left_t(links.pick(left_two, left), links.pick(right_two, right)).astype(bf16)
-        mine = dot_left_t(links.pick(left, left_two), links.pick(right, right_two))
-        value = (mine + links.sibling(there).astype(f32)).astype(bf16)
-        return value.reshape(4, 4, value.shape[0] // 16, value.shape[1])
-
-    def column_grad(value, halves):
-        return sum_twins((value, halves[0]), (value, halves[1]))
-
-    def restore(value):
-        return dot_right_t(value.astype(bf16), order).astype(bf16)
-
-    def blocks_moved(value):
-        size = value.shape[1] // 16
-        return jnp.concatenate(
-            [
-                lax.dynamic_slice_in_dim(value, jnp.bitwise_xor(me, at) * size, size, 1)
-                for at in range(16)
-            ],
-            axis=1,
-        )
-
     down_in = out_grad.reshape(rows, width)
-    result_grad = down_in.astype(f32)
-    down_halves = cut_halves(down_in)
-    put_down = column_grad(activated, down_halves)
-    result = [dot_plain(activated, w_down[0]), dot_plain(activated, w_down[1])]
-    result = jnp.concatenate([result[0], result[1][:, : width - result[0].shape[1]]], axis=1)
-    block_out = (after_cross + result).astype(bf16)
-    act_grad = blocks_moved(product_back(down_halves, w_down))
-    upper_grad = jax.vjp(gelu_tanh, upper)[1](act_grad)[0].astype(bf16)
-    upper_halves = cut_halves(upper_grad)
-    put_up = column_grad(mlp_in, upper_halves)
-    mlp_in_grad = exact_restore(order, product_back(upper_halves, w_up))
-    cross_part, gain_third = jax.vjp(gained_norm, after_cross, gains[2])[1](mlp_in_grad)
-    cross_grad = result_grad + cross_part
-    cross_bf = cross_grad.astype(bf16)
-    cmix_grad = restore(dot_right_t(cross_bf, w_pair[1]))
-    back_scratch = [
-        pltpu.VMEM((rows, width), f32),
-        pltpu.VMEM((rows, width), f32),
-        pltpu.VMEM((rows, width), bf16),
-        pltpu.VMEM((rows, width), f32),
-        pltpu.VMEM((2, rows, 2 * width), f32),
-    ]
-    back_outs = [flat_low, shaped(rows, 2 * width), double_low]
-    heads_block = (head_at, None)
-    cq_grad, ckeyval_mine, ckeyval_theirs = plain_call(
-        functools.partial(attention_back_body, batch, True, False, 1, scaling),
-        back_outs,
-        [(cq_proj, None), (cmix_grad, None), heads_block, (cross_keyval_all, None)],
-        back_scratch,
-        text_lengths,
-    )
-    cq_halves = cut_halves(cq_grad)
-    put_query = column_grad(cross_in, cq_halves)
-    cross_in_grad = exact_restore(order, product_back(cq_halves, w_query))
-    self_part, gain_second = jax.vjp(gained_norm, after_self, gains[1])[1](cross_in_grad)
-    self_grad = cross_grad + self_part
+    cut = shards[6].shape[1]
+    out_halves = jnp.stack(
+        [down_in[:, :cut], jnp.pad(down_in[:, cut:], ((0, 0), (0, 2 * cut - width)))]
+    )
+    up_shape, down_shape = shards[5].shape, shards[6].shape
+    whole = [shaped(4, 4, *shape, dtype=bf16) for shape in (down_shape, up_shape)]
+    tile = 384
+    block_out, cross_grad, gain_third, *rest = pl.pallas_call(
+        functools.partial(mlp_back_body, batch),
+        out_shape=[flat_low, flat, shaped(8, width), *whole, *whole],
+        in_specs=[IN_VMEM] * 7 + [ANYWHERE] * 2,
+        out_specs=[IN_VMEM] * 3 + [ANYWHERE] * 4,
+        scratch_shapes=[
+            pltpu.VMEM((2, rows, inner // 2), bf16),
+            pltpu.VMEM((width, rows), bf16),
+            pltpu.VMEM((2, rows, cut), f32),
+            pltpu.VMEM((3, 2, *down_shape), bf16),
+            pltpu.VMEM((3, 4, 4, block, 512), bf16),
+            pltpu.VMEM((2, *down_shape), bf16),
+            pltpu.VMEM((2, *down_shape), bf16),
+            pltpu.VMEM((2, 4, 4, block, tile), bf16),
+            pltpu.VMEM((2, 4, 4, block, tile), bf16),
+            pltpu.SemaphoreType.DMA((3,)),
+            pltpu.SemaphoreType.DMA((2, 16)),
+            pltpu.SemaphoreType.DMA((2, 16)),
+            pltpu.SemaphoreType.DMA((4,)),
+        ],
+        compiler_params=pltpu.CompilerParams(
+            collective_id=8, has_side_effects=True, vmem_limit_bytes=60 * 2**20
+        ),
+    )(out_halves, activated, upper, mlp_in, after_cross, order, gains, gathered[5], gathered[6])
+    sums_down, sums_up = rest[0], rest[1]
 
     text_half = text_rows // 2
-    (keyval_grad,) = plain_call(
-        functools.partial(keys_back_body, batch, False),
-        [double_low],
-        [
-            (ckey_mine, None),
-            (ckeyval_mine, None),
-            (links.sibling(ckeyval_theirs), None),
-            heads_block,
-        ],
-    )
     text_mine = lax.dynamic_slice_in_dim(
         text_ordered.reshape(batch, text_rows, text_width), core * text_half, text_half, 1
     ).reshape(-1, text_width)
-    keyval_halves = cut_halves(keyval_grad)
-    put_keyval = column_grad(text_mine, keyval_halves)
-    grad_text = exact_restore(order_text, product_back(keyval_halves, w_keyval))
-    grad_text = grad_text.reshape(batch, text_half, text_width)
-
-    self_bf = self_grad.astype(bf16)
-    put_pair = sum_twins((attn_cat, self_bf), (cross_cat, cross_bf))
-    mix_grad = restore(dot_right_t(self_bf, w_pair[0]))
-    query_grad, here, there = plain_call(
-        functools.partial(attention_back_body, batch, False, True, 2, scaling),
-        back_outs,
-        [
-            (qkv_proj, (0, width)),
-            (mix_grad, None),
-            heads_block,
-            *tables,
-            (keyval_here, None),
-            (keyval_there, None),
+    parts = [shards[at].shape for at in (6, 5, 3, 4, 2, 1, 0)]
+    moved = [
+        *[shaped(2, *shape) for shape in parts],
+        *[shaped(4, 4, *shape, dtype=bf16) for shape in parts[2:]],
+        *[shaped(4, 4, *shape, dtype=bf16) for shape in parts[2:]],
+        *[shaped(2, 4, *shape, dtype=bf16) for shape in parts],
+        *[shaped(4, *shape, dtype=bf16) for shape in parts],
+        *[shaped(4, *shape, dtype=bf16) for shape in parts],
+        *[shaped(3, *shape, dtype=bf16) for shape in parts],
+        *[shaped(3, *shape, dtype=bf16) for shape in parts],
+    ]
+    placed = [
+        cross_cat, attn_cat, cross_in, attn_in, text_mine, after_self, hidden, normed,
+        gains, order, head_at, *table_arrays, valid,
+    ]
+    apart = [
+        *gathered[:5],
+        cross_keyval_all, cq_proj, ckey_mine, qkv_proj, keyval_here, keyval_there, cross_grad,
+        sums_down, sums_up,
+    ]
+    small_outs = [shaped(rows, text_width), shaped(8, width), shaped(8, width)]
+    text_grad, gain_grads, shift_grad, normed_grad, *rest = pl.pallas_call(
+        functools.partial(rest_back_body, batch, scaling),
+        out_shape=[*small_outs, shaped(rows, 2 * width), *moved],
+        in_specs=[IN_VMEM] * len(placed) + [ANYWHERE] * len(apart),
+        out_specs=[IN_VMEM] * 3 + [ANYWHERE] * (1 + len(moved)),
+        scratch_shapes=[
+            *[pltpu.VMEM((rows, width), f32)] * 4,
+            pltpu.VMEM((rows, width), bf16),
+            pltpu.VMEM((rows, width), bf16),
+            pltpu.VMEM((2, rows, 2 * width), f32),
+            pltpu.VMEM((2 * rows, 2 * width), bf16),
+            pltpu.VMEM((rows, 2 * width), f32),
+            pltpu.VMEM((2, width, rows), bf16),
+            pltpu.VMEM((2, rows, shards[1].shape[1]), bf16),
+            pltpu.VMEM((3, 4, 4, block, tile), bf16),
+            pltpu.VMEM((2, 4, 4, block, tile), bf16),
+            pltpu.VMEM((2, 4, 4, block, tile), bf16),
+            pltpu.VMEM((9, block, 1536), bf16),
+            pltpu.VMEM((9, down_shape[0], tile), bf16),
+            pltpu.VMEM((block, 1536), f32),
+            pltpu.VMEM((down_shape[0], tile), f32),
+            pltpu.VMEM((2, rows, 2 * width), bf16),
+            pltpu.SemaphoreType.DMA((3,)),
+            pltpu.SemaphoreType.DMA((4,)),
+            pltpu.SemaphoreType.DMA((5, 8)),
+            pltpu.SemaphoreType.DMA((5, 8)),
+            pltpu.SemaphoreType.DMA((4,)),
+            pltpu.SemaphoreType.DMA((2,)),
+            pltpu.SemaphoreType.DMA((2,)),
+            pltpu.SemaphoreType.DMA((7, 8)),
+            pltpu.SemaphoreType.DMA((7, 8)),
+            pltpu.SemaphoreType.DMA((9,)),
+            pltpu.SemaphoreType.DMA((4,)),
         ],
-        back_scratch,
-    )
-    (key_value_grad,) = plain_call(
-        functools.partial(keys_back_body, batch, True),
-        [double_low],
-        [(qkv_proj, (1, width)), (here, None), (links.sibling(there), None), heads_block, *tables],
-    )
-    qkv_grad = qkv_halves(jnp.concatenate([query_grad, key_value_grad], axis=1))
-    put_qkv = column_grad(attn_in, qkv_grad)
-    attn_in_grad = exact_restore(order, product_back(qkv_grad, w_qkv))
-
-    def shifted(values, gain, moved):
-        wide = jnp.broadcast_to(moved[:, None, :], (batch, tokens, width)).reshape(rows, width)
-        return layer_norm(values) * gain + wide
-
-    hidden_part, gain_first, shift_grad = jax.vjp(shifted, hidden, gains[0], shift)[1](
-        attn_in_grad
-    )
-    hidden_grad = self_grad + hidden_part
-    hidden_bf = hidden_grad.astype(bf16)
-    normed_halves = [jnp.concatenate([normed[c, 0], normed[c, 1]], axis=1) for c in range(2)]
-    put_skip = sum_twins((normed_halves[0], hidden_bf), (normed_halves[1], hidden_bf))
-    near_grad, away_grad = 0.0, 0.0
-    for at in range(2):
-        part = dot_right_t(hidden_bf, w_skip[at])
-        near_grad = near_grad + exact_restore(order_skip[at], part[:, : width // 2])
-        away_grad = away_grad + exact_restore(order_skip[at], part[:, width // 2 :])
-    normed_grad = jnp.concatenate(
-        [jnp.where(me < 8, near_grad, away_grad), jnp.where(me < 8, away_grad, near_grad)], axis=1
-    )
-    joined = jnp.concatenate(
-        [latent.reshape(rows, width), skip_input.reshape(rows, width)], axis=1
-    ).astype(f32)
-    joined_grad, skip_gain_grad = jax.vjp(gained_norm, joined, skip_gain_all)[1](normed_grad)
-    grads_down, grads_up = scatter([put_down, put_up], 4, 8)
-    grads = scatter([put_pair, put_query, put_keyval, put_qkv, put_skip], 4, 4)
-    grad_down = jnp.concatenate([grads_down[0], grads_down[1]], axis=1)[:, :width]
-    grad_up = jnp.concatenate([grads_up[0], grads_up[1]], axis=1)
-    grad_self_out, grad_cross_out = grads[0][0], grads[0][1]
-    grad_cross_query = jnp.concatenate([grads[1][0], grads[1][1]], axis=1)[:, :width]
-    grad_keyval = jnp.concatenate([grads[2][0], grads[2][1]], axis=1)
-    grad_qkv = qkv_whole(grads[3][0], grads[3][1])
-    grad_skip_linear = grads[4].reshape(skip_linear.shape)
+        compiler_params=pltpu.CompilerParams(
+            collective_id=9, has_side_effects=True, vmem_limit_bytes=62 * 2**20
+        ),
+    )(*placed, *apart)
+    grads = rest[:7]
+    joined_grad, skip_gain_grad = pl.pallas_call(
+        functools.partial(joined_back_body, batch),
+        out_shape=[shaped(2, rows, width), shaped(8, 2 * width)],
+        in_specs=[IN_VMEM] * 5,
+        out_specs=[IN_VMEM] * 2,
+        compiler_params=pltpu.CompilerParams(vmem_limit_bytes=60 * 2**20),
+    )(normed_grad, latent.reshape(rows, width), skip_input.reshape(rows, width), skip_gain_all[None, :], order_skip)
+    skip_gain_grad = skip_gain_grad[0]
+    gain_first, gain_second, gain_third = gain_grads[0], gain_grads[1], gain_third[0]
+    shift_grad = shift_grad[:batch]
+    grad_text = exact_restore(order_text, text_grad).reshape(batch, text_half, text_width)
+
+    def wide_of(part):
+        return jnp.concatenate([part[0], part[1]], axis=1)
+
+    grad_down = wide_of(grads[0])[:, :width]
+    grad_up = wide_of(grads[1])
+    grad_cross_query = wide_of(grads[2])[:, :width]
+    grad_keyval = wide_of(grads[3])
+    grad_self_out, grad_cross_out = grads[4][0], grads[4][1]
+    grad_qkv = qkv_whole(grads[5][0], grads[5][1])
+    grad_skip_linear = grads[6].reshape(skip_linear.shape)
 
     gains_grad = jnp.stack([gain_first, gain_second, gain_third])
     gains_grad = gains_grad.reshape(3, count, third).transpose(1, 0, 2).reshape(count, 3 * third)
@@ -1971,8 +2665,8 @@
     ).astype(bf16)
     return (
         block_out.reshape(batch, tokens, width),
-        joined_grad[:, :width].reshape(batch, tokens, width),
-        joined_grad[:, width:].reshape(batch, tokens, width),
+        joined_grad[0].reshape(batch, tokens, width),
+        joined_grad[1].reshape(batch, tokens, width),
         grad_cond,
         grad_text,
         grad_skip_gain,

time: 1250 us -> 1010 us (0.81)
  matrix products: 160 us -> 6.83 us
  local copies, waits for them, and re-layouts: 96.7 us -> 32.1 us
  other arithmetic: 65.4 us -> 32.5 us
  Pallas kernels: 907 us -> 926 us
    dot_general x15 -> x1, matrix products: 74.6 us -> 1.1 us  [dot_left_t(): lax.dot_general(left, right, (((0,), (0,)), ((), ())), preferred_element_...]
    dot_general x31 -> x3, matrix products: 74.3 us -> 3.19 us  [dot_right_t(): lax.dot_general(left, right, (((1,), (1,)), ((), ())), preferred_element_...]
    slice x11 -> x6, local copies, waits for them, and re-layouts: 50.6 us -> 6.06 us  [the longest x1 1.76 us: local_sixteen(): joined_grad[1].reshape(batch, tokens, width)]
    pallas_call x6 -> x3, Pallas kernels: 459 us -> 498 us  [the longest x1 385 us: local_sixteen(): pl.pallas_call(functools.partial(rest_back_body, batch, scaling), out_sha...]
    pallas_call x4, Pallas kernels: 67.4 us -> 47.5 us  [trade(): pl.pallas_call(functools.partial(trade_body, count, same), out_shape=jax....]
    reduce_sum x14 -> x0, other arithmetic: 16.1 us -> none  [the longest x8 9.49 us: layer_norm(): center = values - jnp.mean(values, axis=-1, keepdims=True)]
    unnamed x296 -> x68, local copies, waits for them, and re-layouts: 24.6 us -> 11.7 us
  transfers between devices with their start and end apart: 10 -> 1, of which waited for: 0 -> 0; matrix products, arithmetic and copies ran while one was open for 17% -> 1% of each run, Pallas kernels for 25% -> 0%
where the time goes in v3:
time: 1010 us; the launch traced here: 999 us
  Pallas kernels  926 us (92%)
  other arithmetic  32.5 us (3%)
  local copies, waits for them, and re-layouts  32.1 us (3%)
    pallas_call x1, Pallas kernels, local_sixteen(): pl.pallas_call(functools.partial(rest_back_body, batch, scaling), out_sha...  385 us
    pallas_call x1, Pallas kernels, local_sixteen(): pl.pallas_call(functools.partial(forward_body, batch, scaling), out_shape...  380 us
    pallas_call x1, Pallas kernels, local_sixteen(): pl.pallas_call(functools.partial(mlp_back_body, batch), out_shape=[flat_l...  96.2 us
    pallas_call x4, Pallas kernels, trade(): pl.pallas_call(functools.partial(trade_body, count, same), out_shape=jax....  47.5 us
  transfers between devices with their start and end apart: 1, of which 0 were waited for; matrix products, arithmetic and copies ran while one was open for 1% of the time, Pallas kernels for 0%

profile of v3, /device:TPU:0, one launch (start us, length us, event | category | flops | bytes accessed | tf_op | source)
XLA Modules:
  0.0 999.2 jit_solution(2389658402580679208)
XLA Ops:
  4.3 12.0 %shard_map.329 = bf16[16,32,128]{2,1,0:T(8,128)(2,1)} custom-call(bf16[32,128]{1,0:T(8,128)(2,1)} %pad_bitcast_fusion.2.source), custom_call_target="tpu_custom_call" | custom-call | tf_op jit(solution)/shard_map/pallas_call | solution.py:95
  16.3 1.0 copy.54
  17.5 1.2 fusion.57
  22.5 10.7 %shard_map.330 = f32[16,24,128]{2,1,0:T(8,128)} custom-call(f32[16,24,128]{2,1,0:T(8,128)} %bitcast.93), custom_call_target="tpu_custom_call" | custom-call | tf_op jit(solution)/shard_map/pallas_call | solution.py:95
  33.2 1.0 reduce_sum.18
  36.2 1.0 slice.246
  37.2 1.0 fusion.11.refs_7_.refs_10_
  38.2 1.9 slice_bitcast_fusion.8
  43.6 3.6 fusion.refs_5_.refs_9_
  47.2 2.3 fusion.7
  49.6 3.0 add_convert_fusion.refs_6_.order_skip
  54.3 4.0 negate_select_fusion
  58.3 380.5 %shard_map.331 = (bf16[2,4,4,88,1408]{4,3,2,1,0:T(8,128)(2,1)}, bf16[2,4,4,88,2176]{4,3,2,1,0:T(8,128)(2,1)}, bf16[2,4,4,88,1408]{4,3,2,1,0:T(8,128)(2,1)}, bf16...) custom-call(bf16[256,1408]{1,0:T(8,128)(2,1)} %bitcast.83, ...), custom_call_target="tpu_custom_call" | custom-call | tf_op jit(solution)/shard_map/pallas_call | solution.py:2488
  441.4 96.2 %shard_map.332 = (bf16[256,1408]{1,0:T(8,128)(2,1)}, f32[256,1408]{1,0:T(8,128)}, f32[8,1408]{1,0:T(8,128)}, bf16[4,4,384,768]{3,2,1,0:T(8,128)(2,1)}, bf16[4,4,...) custom-call(bf16[2,256,768]{2,1,0:T(8,128)(2,1)} %pad_maximum_fusion.3.refs_0_, ...), custom_call_target="tpu_custom_call" | custom-call | tf_op jit(solution)/shard_map/pallas_call | solution.py:2516
  539.3 385.0 %shard_map.333 = (f32[256,1024]{1,0:T(8,128)}, f32[8,1408]{1,0:T(8,128)}, f32[8,1408]{1,0:T(8,128)}, f32[256,2816]{1,0:T(8,128)}, f32[2,384,768]{2,1,0:T(8,128)}...) custom-call(bf16[256,1408]{1,0:T(8,128)(2,1)} %get-tuple-element.71., ...), custom_call_target="tpu_custom_call" | custom-call | tf_op jit(solution)/shard_map/pallas_call | solution.py:2567
  924.3 16.5 %shard_map.334 = (f32[2,256,1408]{2,1,0:T(8,128)}, f32[8,2816]{1,0:T(8,128)}) custom-call(f32[256,2816]{1,0:T(8,128)} %get-tuple-element.92.normed_grad, bf16[256,1408]{1,0:T(8,128)(2,1)} %bitcast.84, bf16[256,1408]{1,0:T(8,128)(2,1)} %bitcast.86, f32[1,2816]{1,0:T(1,128)} %reshape.464.refs_2_.skip_gain, bf16[2,1408,704]{2,1,0:T(8,128)(2,1)} %add_convert_fusion.refs_6_.order_skip), custom_call_target="tpu_custom_call" | custom-call | tf_op jit(solution)/shard_map/pallas_call | solution.py:2606
  944.5 1.7 copy-done.3
  946.2 1.8 fusion.56
  948.1 1.1 copy-done.15
  949.2 1.0 slice_bitcast_fusion.6
  950.2 1.0 fusion.1
  951.2 2.0 fusion.8
  953.4 1.5 copy-done.5
  956.0 1.5 pad_maximum_fusion.1
  957.4 1.5 pad_maximum_fusion
  958.9 1.2 pad_maximum_fusion.2
  961.6 15.3 %shard_map.335 = f32[16,24,128]{2,1,0:T(8,128)} custom-call(f32[24,128]{1,0:T(8,128)} %fusion.21.source), custom_call_target="tpu_custom_call" | custom-call | tf_op jit(solution)/shard_map/pallas_call | solution.py:95
  976.9 1.0 copy.53
  979.1 9.5 shard_map.336
  990.1 1.1 fusion.45
  994.7 1.0 multiply_convert_fusion
  996.6 2.2 copy.64
  (176 shorter events, 32.5 us)
Async XLA Ops:
  0.7 46.6 %copy-start = (bf16[2,256,1024]{2,1,0:T(8,128)(2,1)S(1)}, bf16[2,256,1024]{2,1,0:T(8,128)(2,1)}, u32[]{:S(2)}) copy-start(bf16[2,256,1024]{2,1,0:T(8,128)(2,1)} %param.21) | copy-start | bytes 3145732
  0.7 18.0 %copy-start.27 = (s32[2]{0:T(128)S(1)}, s32[2]{0:T(128)}, u32[]{:S(2)}) copy-start(s32[2]{0:T(128)} %param.22) | copy-start | bytes 28
  0.7 20.7 %copy-start.16 = (bf16[88,1408]{1,0:T(8,128)(2,1)S(1)}, bf16[88,1408]{1,0:T(8,128)(2,1)}, u32[]{:S(2)}) copy-start(bf16[88,1408]{1,0:T(8,128)(2,1)} %param.27) | copy-start | bytes 743428
  17.5 17.3 %copy-start.13 = (bf16[88,1408]{1,0:T(8,128)(2,1)S(1)}, bf16[88,1408]{1,0:T(8,128)(2,1)}, u32[]{:S(2)}) copy-start(bf16[88,1408]{1,0:T(8,128)(2,1)} %param.30) | copy-start | bytes 743428
  17.5 17.3 %slice-start.3 = ((bf16[88,1408]{1,0:T(8,128)(2,1)}), bf16[88,640]{1,0:T(8,128)(2,1)S(1)}, s32[]{:S(2)}) async-start(bf16[88,1408]{1,0:T(8,128)(2,1)} %param.30), calls=%async_computation.3 | async-start | bytes 225280 | tf_op jit(solution)/shard_map/slice | solution.py:2383
  17.5 18.0 %copy-start.10 = (bf16[64,2816]{1,0:T(8,128)(2,1)S(1)}, bf16[64,2816]{1,0:T(8,128)(2,1)}, u32[]{:S(2)}) copy-start(bf16[64,2816]{1,0:T(8,128)(2,1)} %param.31) | copy-start | bytes 1081348
  34.8 5.3 copy-start.7
  34.8 5.3 slice-start.2
  38.2 2.8 copy-start.12
  49.5 3.0 copy-start.21
  49.5 3.0 copy-start.22
  49.5 3.0 copy-start.23
  49.6 3.9 slice-start
  49.6 3.9 slice-start.1
  58.3 382.2 %copy-start.8 = (bf16[1,256,768]{2,1,0:T(8,128)(2,1)S(1)}, bf16[1,256,768]{2,1,0:T(8,128)(2,1)}, u32[]{:S(2)}) copy-start(bf16[1,256,768]{2,1,0:T(8,128)(2,1)} %get-tuple-element.131) | copy-start | bytes 1179652
  441.4 97.0 %copy-start.4 = (bf16[1024,512]{0,1:T(8,128)(2,1)S(1)}, bf16[1024,512]{0,1:T(8,128)(2,1)}, u32[]{:S(2)}) copy-start(bf16[1024,512]{0,1:T(8,128)(2,1)} %fusion.7) | copy-start | bytes 3145732
  924.3 20.0 %copy-start.9 = (f32[2,88,2176]{2,1,0:T(8,128)S(1)}, f32[2,88,2176]{2,1,0:T(8,128)}, u32[]{:S(2)}) copy-start(f32[2,88,2176]{2,1,0:T(8,128)} %get-tuple-element.102) | copy-start | bytes 4595716
  943.9 17.1 %collective-permute-start = (f32[9888]{0:T(1024)S(1)}, f32[9888]{0:T(1024)S(1)}, u32[]{:S(2)}, u32[]{:S(2)}) collective-permute-start(f32[9888]{0:T(1024)S(1)} %constant_dynamic-update-slice_fusion), channel_id=1, source_target_pairs={{0,1},{1,0},{2,3},{3,2},{4,5},{5,4},{6,7},{7,6},{8,9},{9,8},{10,11... | collective-permute-start | bytes 118664 | tf_op jit(solution)/shard_map/ppermute | solution.py:1469
  944.4 1.8 copy-start.3
  946.2 1.8 copy-start.20
  946.2 1.8 copy-start.19
  948.0 2.2 copy-start.28
  951.2 2.0 copy-start.6
  958.9 19.1 %copy-start.17 = (bf16[88,1408]{1,0:T(8,128)(2,1)S(1)}, bf16[88,1408]{1,0:T(8,128)(2,1)}, u32[]{:S(2)}) copy-start(bf16[88,1408]{1,0:T(8,128)(2,1)} %param.27) | copy-start | bytes 743428
  960.1 31.2 %copy-start.25 = (f32[2,16]{1,0:T(2,128)S(1)}, f32[2,16]{1,0:T(2,128)}, u32[]{:S(2)}) copy-start(f32[2,16]{1,0:T(2,128)} %param.35) | copy-start | bytes 388
  960.1 31.5 %copy-start.14 = (bf16[88,1408]{1,0:T(8,128)(2,1)S(1)}, bf16[88,1408]{1,0:T(8,128)(2,1)}, u32[]{:S(2)}) copy-start(bf16[88,1408]{1,0:T(8,128)(2,1)} %param.30) | copy-start | bytes 743428
  960.1 32.5 %copy-start.24 = (bf16[2,1408]{1,0:T(2,128)(2,1)S(1)}, bf16[2,1408]{1,0:T(2,128)(2,1)}, u32[]{:S(2)}) copy-start(bf16[2,1408]{1,0:T(2,128)(2,1)} %param.20) | copy-start | bytes 16900
  960.1 33.8 %copy-start.11 = (bf16[64,2816]{1,0:T(8,128)(2,1)S(1)}, bf16[64,2816]{1,0:T(8,128)(2,1)}, u32[]{:S(2)}) copy-start(bf16[64,2816]{1,0:T(8,128)(2,1)} %param.31) | copy-start | bytes 1081348
  961.0 33.8 %copy-start.2 = (bf16[88,4224]{1,0:T(8,128)(2,1)S(1)}, bf16[88,4224]{1,0:T(8,128)(2,1)}, u32[]{:S(2)}) copy-start(bf16[88,4224]{1,0:T(8,128)(2,1)} %param.28) | copy-start | bytes 2230276
  978.2 17.5 %copy-start.18 = (bf16[256,1408]{1,0:T(8,128)(2,1)S(1)}, bf16[256,1408]{1,0:T(8,128)(2,1)}, u32[]{:S(2)}) copy-start(bf16[256,1408]{1,0:T(8,128)(2,1)} %get-tuple-element.70) | copy-start | bytes 2162692
  991.3 5.3 copy-start.26
  994.7 4.1 copy-start.1
  (2 other events, 2.9 us)

commit v4 on v3

--- a/solution.py
+++ b/solution.py
@@ -362,8 +362,8 @@
 
 
 class GatherPlan:
-    def __init__(self, mine, out, send, recv, local):
-        self.mine, self.out = mine, out
+    def __init__(self, pieces, send, recv, local):
+        self.pieces = pieces
         self.send, self.recv, self.local = send, recv, local
         self.core, self.first_mask, self.second_mask, self.at, self.sibling = neighbours(4)
         self.far_peers = [self.at(4 * k) for k in range(1, 4)]
@@ -381,18 +381,27 @@
             device_id_type=MESH,
         )
 
+    def mine(self, w):
+        shard, _, lanes = self.pieces[w]
+        return shard.at[:, lanes]
+
     def block(self, w, q):
-        return self.out[w].at[self.core, :, q]
+        _, out, lanes = self.pieces[w]
+        return out.at[self.core, :, q, :, lanes]
+
+    def plane(self, w, k, q):
+        _, out, lanes = self.pieces[w]
+        return out.at[self.core, k, q, :, lanes]
+
+    def layer(self, w, k):
+        _, out, lanes = self.pieces[w]
+        return out.at[self.core, k, :, :, lanes]
 
     def far(self, w, k):
-        return self.copy(
-            w, k - 1, self.mine[w], self.out[w].at[self.core, k, 0], self.far_peers[k - 1]
-        )
+        return self.copy(w, k - 1, self.mine(w), self.plane(w, k, 0), self.far_peers[k - 1])
 
     def keep(self, w):
-        return pltpu.make_async_copy(
-            self.mine[w], self.out[w].at[self.core, 0, 0], self.local.at[w]
-        )
+        return pltpu.make_async_copy(self.mine(w), self.plane(w, 0, 0), self.local.at[w])
 
     def first(self, w):
         mask = self.first_mask
@@ -410,6 +419,62 @@
     def twin(self, w, n):
         q = (0, self.first_mask, self.second_mask, 3)[n]
         return self.copy(w, 6 + n, self.block(w, q), self.block(w, q), self.sibling)
+
+
+    def low_first(self, w):
+        mask = self.first_mask
+        return self.copy(w, 3, self.mine(w), self.plane(w, 0, mask), self.at(mask))
+
+    def low_second(self, w):
+        mask = self.second_mask
+        return self.copy(w, 4, self.mine(w), self.plane(w, 0, mask), self.at(mask))
+
+    def low_both(self, w):
+        mask = self.second_mask
+        return self.copy(
+            w, 5, self.plane(w, 0, self.first_mask), self.plane(w, 0, 3), self.at(mask)
+        )
+
+    def low_far(self, w, k):
+        return self.copy(w, k - 1, self.layer(w, 0), self.layer(w, k), self.far_peers[k - 1])
+
+    def low_twin(self, w, k):
+        return self.copy(w, 6 + k, self.layer(w, k), self.layer(w, k), self.sibling)
+
+    def low_begin(self, w):
+        self.keep(w).start()
+        self.low_first(w).start()
+        self.low_second(w).start()
+
+    def low_cross(self, w):
+        self.low_first(w).wait_recv()
+        self.low_both(w).start()
+        self.low_second(w).wait_recv()
+
+    def low_spread(self, w):
+        self.keep(w).wait()
+        self.low_both(w).wait_recv()
+        for k in range(1, 4):
+            self.low_far(w, k).start()
+        self.low_twin(w, 0).start()
+
+    def low_close(self, w):
+        for k in range(1, 4):
+            self.low_far(w, k).wait_recv()
+            self.low_twin(w, k).start()
+
+    def low_finish(self, w):
+        self.low_first(w).wait_send()
+        self.low_second(w).wait_send()
+        self.low_both(w).wait_send()
+        for k in range(1, 4):
+            self.low_far(w, k).wait_send()
+        for k in range(4):
+            self.low_twin(w, k).wait_send()
+
+    def low_ready(self, w):
+        for k in range(4):
+            self.low_twin(w, k).wait_recv()
 
     def begin(self, w):
         self.keep(w).start()
@@ -480,27 +545,51 @@
 def forward_body(batch, scaling, *refs):
     refs = list(refs)
     take = refs.pop
-    latent, skip, skip_gain, gains, shift = (take(0) for _ in range(5))
-    order, order_skip, heads_ref = (take(0) for _ in range(3))
-    tables = [take(0) for _ in range(3)]
-    text, valid = take(0), take(0)
+    latent, skip, skip_gain, gains, shift, out_grad, valid = (take(0) for _ in range(7))
+    loaded = [take(0) for _ in range(7)]
     mine = [take(0) for _ in range(7)]
     out = [take(0) for _ in range(7)]
-    normed, hidden, attn_in, qkv, keyval_here, keyval_there = (take(0) for _ in range(6))
-    attn_cat, after_self, cross_in, cq_proj, ckey_mine, cross_keyval = (take(0) for _ in range(6))
-    cross_cat, after_cross, mlp_in, upper, activated = (take(0) for _ in range(5))
-    self_peak, cross_peak = take(0), take(0)
-    wide, narrow, buffer, semaphore, send, recv, local, twin_send, twin_recv = refs
+    saved_out = [take(0) for _ in range(19)]
+    sums_down, there_down = take(0), take(0)
+    saved = [take(0) for _ in range(19)]
+    order, order_skip, heads_ref, *tables, text = placed = [take(0) for _ in range(7)]
+    wide, narrow, buffer, out_down, in_down, semaphore, send, recv, local = (
+        take(0) for _ in range(9)
+    )
+    twin_send, twin_recv, sum_send, sum_recv, sum_local, load_sem, save_sem = refs
+    normed, hidden, attn_in, qkv, keyval_here, keyval_there = saved[:6]
+    attn_cat, after_self, cross_in, cq_proj, ckey_mine, cross_keyval = saved[6:12]
+    cross_cat, after_cross, mlp_in, upper, activated, self_peak, cross_peak = saved[12:]
     rows, width = hidden.shape
     size = rows // batch
     me = lax.axis_index("fsdp")
     core = lax.axis_index("seq")
-    plan = GatherPlan(mine, out, send, recv, local)
-    skip_w, qkv_w, pair_w, query_w, keyval_w, up_w, down_w = range(7)
+    pieces = [(mine[w], out[w], pl.ds(0, mine[w].shape[1])) for w in range(6)]
+    cut = mine[6].shape[1] // 2
+    pieces += [(mine[6], out[6], pl.ds(at * cut, cut)) for at in range(2)]
+    plan = GatherPlan(pieces, send, recv, local)
+    skip_w, qkv_w, pair_w, query_w, keyval_w, up_w, down_w, last_w = range(8)
 
     greet(plan.peers())
-    for w in range(7):
-        plan.begin(w)
+    plan.low_begin(last_w)
+    plan.begin(skip_w)
+    plan.begin(qkv_w)
+    loads = [
+        pltpu.make_async_copy(source, target, load_sem.at[at])
+        for at, (source, target) in enumerate(zip(loaded, placed))
+    ]
+    saves = [
+        pltpu.make_async_copy(source, target, save_sem.at[at])
+        for at, (source, target) in enumerate(zip(saved, saved_out))
+    ]
+    for copy in loads:
+        copy.start()
+    for copy in loads:
+        copy.wait()
+
+    def save(*places):
+        for at in places:
+            saves[at].start()
 
     def each(body):
         for b in range(batch):
@@ -532,11 +621,13 @@
             normed[half, 1, rows_b, :] = dot_plain(away, order_skip[half]).astype(bf16)
 
     each(normed_part)
+    save(0)
+    plan.low_cross(last_w)
     plan.spread(skip_w)
+    plan.begin(pair_w)
+    plan.cross(skip_w)
     plan.spread(qkv_w)
-    plan.cross(skip_w)
-    plan.spread(pair_w)
-    plan.cross(qkv_w)
+    plan.begin(query_w)
     plan.close(skip_w)
     plan.ready(skip_w)
 
@@ -553,14 +644,19 @@
             hidden[:, lanes] += value
 
     stream(out[skip_w], skip_tiles, buffer, semaphore, skip_product)
+    save(1)
 
     def attn_in_part(b, rows_b):
         value = layer_norm(hidden[rows_b, :]) * gains[0:1, :] + shift[b : b + 1, :]
         attn_in[rows_b, :] = reorder(value.astype(bf16))
 
     each(attn_in_part)
+    save(2)
+    plan.cross(qkv_w)
+    plan.spread(pair_w)
+    plan.begin(keyval_w)
     plan.spread(query_w)
-    plan.cross(pair_w)
+    plan.begin(up_w)
     plan.close(qkv_w)
     plan.ready(qkv_w)
 
@@ -586,6 +682,7 @@
         keyval_here[rows_b, pl.ds(0, width)] = turn(value, tables).astype(bf16)
 
     each(key_part)
+    save(3, 4)
     exchange = pltpu.make_async_remote_copy(
         src_ref=keyval_here,
         dst_ref=keyval_there,
@@ -601,10 +698,12 @@
         narrow[rows_b, :] = turn(value, tables).astype(bf16)
 
     each(query_part)
+    plan.cross(pair_w)
     plan.spread(keyval_w)
-    plan.cross(query_w)
+    plan.begin(down_w)
     plan.close(pair_w)
     exchange.wait()
+    save(5)
 
     def attend(sources, peak, target, masked):
         peak[...] = jnp.full_like(peak, masked_value)
@@ -630,6 +729,10 @@
         target[...] = reorder(wide[...].astype(bf16))
 
     attend([keyval_here, keyval_there], self_peak, attn_cat, False)
+    save(6, 17)
+    plan.cross(query_w)
+    plan.spread(up_w)
+    plan.low_spread(last_w)
     plan.ready(pair_w)
     pair_tiles = tiles_of(width, 512)
 
@@ -642,14 +745,14 @@
 
     pair_body = out_product(attn_cat, hidden, after_self)
     stream(out[pair_w], tiles_of(width, 512, (0,)), buffer, semaphore, pair_body)
+    save(7)
 
     def cross_in_part(b, rows_b):
         value = layer_norm(after_self[rows_b, :]) * gains[1:2, :]
         cross_in[rows_b, :] = reorder(value.astype(bf16))
 
     each(cross_in_part)
-    plan.spread(up_w)
-    plan.cross(keyval_w)
+    save(8)
     plan.close(query_w)
     plan.ready(query_w)
     query_tiles = tiles_of(out[query_w].shape[4], 512)
@@ -661,11 +764,13 @@
         cq_proj[:, pl.ds(place, extent)] = dot_plain(cross_in[...], tile)[:, :extent]
 
     stream(out[query_w], query_tiles, buffer, semaphore, query_product)
+    save(9)
 
     def cross_query_part(b, rows_b):
         narrow[rows_b, :] = head_norm(cq_proj[rows_b, :], heads_ref)[0].astype(bf16)
 
     each(cross_query_part)
+    plan.cross(keyval_w)
     plan.spread(down_w)
     plan.close(keyval_w)
     plan.ready(keyval_w)
@@ -692,15 +797,19 @@
             pl.ds(pl.multiple_of(core * size, size), size), pl.ds(b * width, width)
         ]
     attend([cross_keyval], cross_peak, cross_cat, True)
+    save(10, 11, 12, 18)
     pair_body = out_product(cross_cat, after_self, after_cross)
     stream(out[pair_w], tiles_of(width, 512, (1,)), buffer, semaphore, pair_body)
+    save(13)
 
     def mlp_in_part(b, rows_b):
         value = layer_norm(after_cross[rows_b, :]) * gains[2:3, :]
         mlp_in[rows_b, :] = reorder(value.astype(bf16))
 
     each(mlp_in_part)
+    save(14)
     plan.cross(up_w)
+    plan.cross(down_w)
     plan.close(up_w)
     plan.ready(up_w)
     block = activated.shape[1] // 16
@@ -713,11 +822,29 @@
         activated[:, pl.ds(pl.multiple_of(slot * block, block), block)] = gelu_of(value).astype(bf16)
 
     stream(out[up_w], up_tiles, buffer, semaphore, up_product)
-    plan.cross(down_w)
+    save(15, 16)
+    def down_part(half):
+        def part(index):
+            return dot_left_t(activated[:, index * block : (index + 1) * block], out_grad[half])
+
+        return part
+
+    planes = [lambda ref, k=k, q=q: ref.at[k, q] for k in range(4) for q in range(4)]
+    down_sum = TwinSum(
+        [there_down], [sums_down], sum_send, sum_recv, sum_local, out_down, in_down, plan.sibling
+    )
+    down_sum.run(
+        0, planes, lambda index: mine[6].shape, down_part(1 - core), down_part(core)
+    )
     plan.close(down_w)
+    plan.low_close(last_w)
     plan.ready(down_w)
+    plan.low_ready(last_w)
     for w in range(7):
         plan.finish(w)
+    plan.low_finish(last_w)
+    for copy in saves:
+        copy.wait()
 
 
 def gelu_slope(value):
@@ -818,32 +945,25 @@
     refs = list(refs)
     take = refs.pop
     out_grad, activated, upper, mlp_in, after_cross, order, gains = (take(0) for _ in range(7))
-    up_w, down_w = take(0), take(0)
+    up_w, down_w, sums_down = (take(0) for _ in range(3))
     block_out, cross_grad, gain_grad = (take(0) for _ in range(3))
-    sums = [take(0), take(0)]
-    there = [take(0), take(0)]
+    sums_up, there_up, half_down = (take(0) for _ in range(3))
     upper_grad, turned, total, down_buffer, up_buffer = (take(0) for _ in range(5))
-    out_down, in_down, out_up, in_up = (take(0) for _ in range(4))
-    semaphore, send, recv, local = refs
+    out_up, in_up = take(0), take(0)
+    semaphore, send, recv, local, give_send, give_recv = refs
     rows, width = after_cross.shape
     size = rows // batch
     block = activated.shape[1] // 16
     half_width = out_grad.shape[2]
     me = lax.axis_index("fsdp")
     core = lax.axis_index("seq")
-    sibling = (me, 1 - core)
-    greet([sibling])
-
-    planes = [
-        lambda ref, k=k, q=q: ref.at[k, q] for k in range(4) for q in range(4)
-    ]
-    down = TwinSum(there, sums, send, recv, local, out_down, in_down, sibling)
-
-    def down_part(half):
-        def part(index):
-            return dot_left_t(activated[:, index * block : (index + 1) * block], out_grad[half])
-
-        return part
+    plan = ScatterPlan(
+        [sums_down], None, [half_down], None, None, None, None, None, None,
+        (give_send, give_recv, None, None),
+    )
+    sibling = plan.sibling
+    greet([plan.at(plan.second_mask), sibling])
+    plan.begin(0)
 
     def down_back():
         depth = down_buffer.shape[0]
@@ -879,13 +999,11 @@
             after_cross[:, pl.ds(half_width, cut)] + total[1][:, :cut]
         ).astype(bf16)
 
-    down.run(
-        0, planes, lambda index: (block, half_width), down_part(1 - core), down_part(core), down_back
-    )
+    down_back()
 
     turned[...] = jnp.transpose(mlp_in[...])
     starts, places, shape = lane_places(width // 16, upper_grad.shape[2], out_up.shape[4])
-    up = TwinSum(there, sums, send, recv, local, out_up, in_up, sibling)
+    up = TwinSum([there_up], [sums_up], send, recv, local, out_up, in_up, sibling)
 
     def up_part(half):
         def part(index):
@@ -910,7 +1028,7 @@
         gain_grad[...] = jnp.zeros_like(gain_grad)
         for b in range(batch):
             rows_b = pl.ds(b * size, size)
-            grad = exact_restore(order[...], cross_grad[rows_b, :])
+            grad = restore_order(order[...], cross_grad[rows_b, :])
             value, gain_part = norm_back(after_cross[rows_b, :], gains[2:3, :], grad)
             gain_grad[0:1, :] += gain_part
             result = jnp.concatenate(
@@ -918,11 +1036,17 @@
             )
             cross_grad[rows_b, :] = result.astype(f32) + value
 
-    up.run(1, places, shape, up_part(1 - core), up_part(core), up_back)
+    up.run(0, places, shape, up_part(1 - core), up_part(core), up_back)
+    for n in range(2):
+        plan.give(0, n).wait_send()
+        plan.give(0, n).wait_recv()
 
 
 class ScatterPlan:
-    def __init__(self, sums, out, half, passing, quarter, leaving, last, slots, totals, sems):
+    def __init__(
+        self, sums, out, half, passing, quarter, leaving, last, slots, totals, sems, given=()
+    ):
+        self.given = given
         self.sums, self.out, self.half = sums, out, half
         self.passing, self.quarter, self.leaving, self.last = passing, quarter, leaving, last
         self.slots, self.totals = slots, totals
@@ -957,80 +1081,108 @@
             w, 2 + k, self.leaving[w].at[k - 1], self.last[w].at[k - 1], self.far_peers[k - 1]
         )
 
-    def chunks(self, w):
-        height, width = self.out[w].shape[1:]
-        which = 0 if height <= self.slots[0].shape[1] else 1
-        size = self.slots[which].shape[2]
-        return which, height, [(s, min(size, width - s)) for s in range(0, width, size)]
-
-    def add(self, w, groups, finish):
-        which, height, chunks = self.chunks(w)
+    def add(self, w, groups, finish, settle):
+        height, width = self.sums[w].shape[2:]
+        which = 0 if height <= self.slots[0].shape[2] else 1
         slots = self.slots[which]
-        for start, extent in chunks:
-            lanes = pl.ds(start, extent)
-            views = []
+        size = slots.shape[3]
+        chunks = [(start, min(size, width - start)) for start in range(0, width, size)]
+
+        def loads(chunk):
+            start, extent = chunks[chunk]
+            bank = chunk % 2
+            copies, views = [], []
             for planes in groups:
                 for plane in planes:
-                    at = len(views)
-                    view = slots.at[at, pl.ds(0, height), pl.ds(0, extent)]
-                    copy = pltpu.make_async_copy(plane.at[:, lanes], view, self.load.at[at])
+                    at = len(copies)
+                    view = slots.at[bank, at, pl.ds(0, height), pl.ds(0, extent)]
+                    views.append(view)
+                    copies.append(
+                        pltpu.make_async_copy(
+                            plane.at[:, pl.ds(start, extent)], view, self.load.at[bank, at]
+                        )
+                    )
+            return copies, views
+
+        def lanes_of_chunk(chunk):
+            start, extent = chunks[chunk]
+            return pl.ds(start, extent), extent
+
+        for copy in loads(0)[0]:
+            copy.start()
+        for chunk in range(len(chunks)):
+            bank = chunk % 2
+            if chunk >= 1:
+                settle(1 - bank, chunk - 1, *lanes_of_chunk(chunk - 1))
+            if chunk + 1 < len(chunks):
+                for copy in loads(chunk + 1)[0]:
                     copy.start()
-                    views.append((view, copy))
+            copies, views = loads(chunk)
             at = 0
-            pending = []
             for index, planes in enumerate(groups):
-                mine = views[at : at + len(planes)]
+                for copy in copies[at : at + len(planes)]:
+                    copy.wait()
+                finish(bank, chunk, index, *lanes_of_chunk(chunk), views[at : at + len(planes)])
                 at += len(planes)
-                for _, copy in mine:
-                    copy.wait()
-                pending.extend(finish(index, lanes, extent, [view for view, _ in mine]))
-            for copy in pending:
-                copy.wait()
-
-    def added(self, views, extent, put):
+        last = len(chunks) - 1
+        settle(last % 2, last, *lanes_of_chunk(last))
+
+    def added(self, views, extent, kind, put):
         step = 256 if extent % 256 == 0 else 128
 
         @pl.loop(0, extent // step)
         def _(i):
             lanes = pl.ds(pl.multiple_of(i * step, step), step)
-            value = views[0][:, lanes].astype(f32)
+            value = views[0][:, lanes].astype(kind)
             for view in views[1:]:
-                value = value + view[:, lanes].astype(f32)
+                value = value + view[:, lanes].astype(kind)
             put(lanes, value)
 
-    def rounded(self, targets):
-        def finish(index, lanes, extent, views):
+    def rounded(self, w, groups, targets):
+        height = self.sums[w].shape[2]
+        which = 0 if height <= self.slots[0].shape[2] else 1
+        starts = [sum(len(planes) for planes in groups[:at]) for at in range(len(groups))]
+
+        def store(bank, index, lanes, extent):
+            view = self.slots[which].at[bank, starts[index], pl.ds(0, height), pl.ds(0, extent)]
+            return pltpu.make_async_copy(
+                view, targets[index].at[:, lanes], self.store.at[bank, index]
+            )
+
+        def finish(bank, chunk, index, lanes, extent, views):
             def put(at, value):
                 views[0][:, at] = value.astype(bf16)
 
-            self.added(views, extent, put)
-            copy = pltpu.make_async_copy(
-                views[0], targets[index].at[:, lanes], self.store.at[index]
-            )
-            copy.start()
-            return [copy]
-
-        return finish
+            self.added(views, extent, bf16 if len(views) == 2 else f32, put)
+            store(bank, index, lanes, extent).start()
+
+        def settle(bank, chunk, lanes, extent):
+            for index in range(len(groups)):
+                store(bank, index, lanes, extent).wait()
+
+        self.add(w, groups, finish, settle)
 
     def begin(self, w):
         self.give(w, 0).start()
         self.give(w, 1).start()
 
     def middle(self, w):
-        self.give(w, 0).wait_recv()
+        if w not in self.given:
+            self.give(w, 0).wait_recv()
         mask = self.first_mask
         groups = [[self.half[w].at[0, k], self.sums[w].at[k, mask]] for k in range(4)]
-        self.add(w, groups, self.rounded([self.passing[w].at[k] for k in range(4)]))
+        self.rounded(w, groups, [self.passing[w].at[k] for k in range(4)])
         self.hand(w).start()
 
     def leave(self, w):
-        self.give(w, 1).wait_recv()
+        if w not in self.given:
+            self.give(w, 1).wait_recv()
         self.hand(w).wait_recv()
         groups = [
             [self.half[w].at[1, k], self.sums[w].at[k, 0], self.quarter[w].at[k]]
             for k in range(1, 4)
         ]
-        self.add(w, groups, self.rounded([self.leaving[w].at[k] for k in range(3)]))
+        self.rounded(w, groups, [self.leaving[w].at[k] for k in range(3)])
         for k in range(1, 4):
             self.far(w, k).start()
 
@@ -1039,31 +1191,37 @@
             self.far(w, k).wait_recv()
         group = [self.half[w].at[1, 0], self.sums[w].at[0, 0], self.quarter[w].at[0]]
         group += [self.last[w].at[k] for k in range(3)]
-        which, height, _ = self.chunks(w)
-        totals = self.totals[which]
-
-        def finish(index, lanes, extent, views):
-            total = totals.at[pl.ds(0, height), pl.ds(0, extent)]
+        height = self.sums[w].shape[2]
+        which = 0 if height <= self.slots[0].shape[2] else 1
+
+        def moves(bank, chunk, lanes, extent):
+            total = self.totals[which].at[bank, pl.ds(0, height), pl.ds(0, extent)]
+            target = self.out[w].at[self.core, :, lanes]
+            here = pltpu.make_async_copy(total, target, self.store.at[bank, 0])
+            return total, here, self.copy(w, 6 + chunk, total, target, self.sibling)
+
+        def finish(bank, chunk, index, lanes, extent, views):
+            total, here, there = moves(bank, chunk, lanes, extent)
 
             def put(at, value):
                 total[:, at] = value
 
-            self.added(views, extent, put)
-            target = self.out[w].at[self.core, :, lanes]
-            here = pltpu.make_async_copy(total, target, self.store.at[0])
-            there = self.copy(w, 6 + (0 if lanes.start == 0 else 1), total, target, self.sibling)
+            self.added(views, extent, f32, put)
             here.start()
             there.start()
+
+        def settle(bank, chunk, lanes, extent):
+            _, here, there = moves(bank, chunk, lanes, extent)
             here.wait()
             there.wait_send()
             there.wait_recv()
-            return []
-
-        self.add(w, [group], finish)
+
+        self.add(w, [group], finish, settle)
 
     def finish(self, w):
-        self.give(w, 0).wait_send()
-        self.give(w, 1).wait_send()
+        if w not in self.given:
+            self.give(w, 0).wait_send()
+            self.give(w, 1).wait_send()
         self.hand(w).wait_send()
         for k in range(1, 4):
             self.far(w, k).wait_send()
@@ -1076,19 +1234,21 @@
     def several(count):
         return [take(0) for _ in range(count)]
 
-    cross_cat, attn_cat, cross_in, attn_in, text, after_self, hidden, normed = several(8)
-    gains, order, heads_ref = several(3)
-    tables = several(3)
-    valid = take(0)
+    gains, valid = several(2)
+    loaded = several(13)
     skip_w, qkv_w, pair_w, query_w, keyval_w = several(5)
     cross_keyval, cq_proj, ckey_mine, qkv, keyval_here, keyval_there, cross_grad = several(7)
-    summed = several(2)
+    summed, half_down = several(2), take(0)
     text_grad, gain_grads, shift_grad, normed_grad = several(4)
     out = several(7)
     own_sums, there = several(5), several(5)
-    half, passing, quarter, leaving, last = (several(7) for _ in range(5))
+    half = [half_down, *several(6)]
+    passing, quarter, leaving, last = (several(7) for _ in range(4))
     grad, wide, factor, back = several(4)
     query, mix_grad, total, keyval, proj, turned, halves = several(7)
+    placed = several(13)
+    cross_cat, attn_cat, cross_in, attn_in, text, after_self, hidden, normed = placed[:8]
+    order, heads_ref, *tables = placed[8:]
     buffer, out_buffer, in_buffer = several(3)
     slots, totals = several(2), several(2)
     landed = take(0)
@@ -1101,13 +1261,12 @@
     down, up, query_s, keyval_s, pair_s, qkv_s, skip_s = range(7)
     plan = ScatterPlan(
         summed + own_sums, out, half, passing, quarter, leaving, last, slots, totals,
-        (send, recv, add_load, add_store),
+        (send, recv, add_load, add_store), (0,),
     )
     twin = TwinSum(
         there, own_sums, twin_send, twin_recv, twin_local, out_buffer, in_buffer, plan.sibling
     )
     greet(plan.peers())
-    plan.begin(down)
     plan.begin(up)
 
     first_lanes, last_lanes = pl.ds(0, width), pl.ds(width, width)
@@ -1127,7 +1286,9 @@
         (cross_keyval, keyval),
         (cq_proj, proj.at[:, first_lanes]),
         (ckey_mine, proj.at[:, last_lanes]),
-    )
+        *zip(loaded, placed),
+    )
+    plan.middle(down)
     gain_grads[...] = jnp.zeros_like(gain_grads)
     shift_grad[...] = jnp.zeros_like(shift_grad)
 
@@ -1247,7 +1408,7 @@
     attention_back([keyval], (), True, lambda value, rows_b: split_lanes(value, rows_b, width))
     keyval[pl.ds(0, rows), :] = total[1 - core].astype(bf16)
     exchange(0).start()
-    plan.middle(down)
+    plan.leave(down)
     query_tiles = tiles_of(768, 384)
     back_through(
         query_w,
@@ -1257,7 +1418,7 @@
     )
 
     def self_part(b, rows_b):
-        value = exact_restore(order[...], wide[rows_b, :])
+        value = restore_order(order[...], wide[rows_b, :])
         value, gain_part = norm_back(after_self[rows_b, :], gains[1:2, :], value)
         gain_grads[1:2, :] += gain_part
         value = grad[rows_b, :] + value
@@ -1290,32 +1451,13 @@
     )
     plan.begin(query_s)
     plan.middle(up)
-    plan.leave(down)
-
     exchange(0).wait()
 
     def text_part(key_grad, value_grad, rows_b):
-        halves[0, rows_b, first_lanes] = key_grad
-        halves[1, rows_b, first_lanes] = value_grad
+        landed[0, rows_b, first_lanes] = key_grad
+        landed[0, rows_b, last_lanes] = value_grad
 
     keys_back(0, core, (), text_part)
-    text_width = text.shape[1]
-    turned[0, pl.ds(0, text_width), :] = jnp.transpose(text[...])
-    twin_product(
-        1,
-        width,
-        text_width // 16,
-        lambda at: turned[0, pl.ds(0, text_width), :],
-        lambda at, start, extent: halves[at, :, pl.ds(start, extent)],
-    )
-    plan.begin(keyval_s)
-    keyval_tiles = tiles_of(width, 384)
-    back_through(
-        keyval_w,
-        keyval_tiles,
-        lambda at, start, extent: halves[at, :, pl.ds(start, extent)],
-        text_grad,
-    )
 
     load(
         (qkv, proj),
@@ -1330,8 +1472,6 @@
     attention_back(sources, tables, False, query_part)
     keyval[pl.ds(0, rows), :] = total[1].astype(bf16)
     exchange(1).start()
-    plan.leave(up)
-    plan.close(down)
     plan.middle(pair_s)
     plan.middle(query_s)
     exchange(1).wait()
@@ -1357,17 +1497,14 @@
     )
 
     def hidden_part(b, rows_b):
-        value = exact_restore(order[...], wide[rows_b, :])
+        value = restore_order(order[...], wide[rows_b, :])
         shift_grad[b : b + 1, :] = jnp.sum(value, axis=0, keepdims=True)
         value, gain_part = norm_back(hidden[rows_b, :], gains[0:1, :], value)
         gain_grads[0:1, :] += gain_part
         halves[0, rows_b, first_lanes] = (grad[rows_b, :] + value).astype(bf16)
 
     each(hidden_part)
-    plan.close(up)
-    plan.middle(keyval_s)
-    plan.leave(pair_s)
-    plan.leave(query_s)
+    plan.leave(up)
 
     for at in range(2):
         for part in range(2):
@@ -1382,8 +1519,28 @@
         lambda at, start, extent: halves[0, :, pl.ds(start, extent)],
     )
     plan.begin(skip_s)
-    plan.leave(keyval_s)
+    plan.leave(pair_s)
+    plan.leave(query_s)
+
+    text_width = text.shape[1]
+    turned[0, pl.ds(0, text_width), :] = jnp.transpose(text[...])
+    twin_product(
+        1,
+        width,
+        text_width // 16,
+        lambda at: turned[0, pl.ds(0, text_width), :],
+        lambda at, start, extent: landed[0, :, pl.ds(at * width + start, extent)]
+        if isinstance(at, int)
+        else landed[0, :, pl.ds(pl.multiple_of(at * width + start, 128), extent)],
+    )
+    plan.begin(keyval_s)
     plan.middle(qkv_s)
+    back_through(
+        keyval_w,
+        tiles_of(width, 384),
+        lambda at, start, extent: landed[0, :, pl.ds(at * width + start, extent)],
+        text_grad,
+    )
     skip_tiles = tiles_of(width, 384)
 
     def skip_body(index, tile):
@@ -1398,14 +1555,18 @@
     stream(skip_w, skip_tiles, buffer, semaphore, skip_body)
     keep = pltpu.make_async_copy(total.at[0], normed_grad, loads.at[0])
     keep.start()
+    plan.close(down)
+    plan.middle(skip_s)
+    plan.leave(qkv_s)
+    plan.middle(keyval_s)
+    plan.close(up)
+    plan.leave(skip_s)
+    plan.leave(keyval_s)
     plan.close(pair_s)
     plan.close(query_s)
+    plan.close(qkv_s)
+    plan.close(skip_s)
     plan.close(keyval_s)
-    plan.leave(qkv_s)
-    plan.middle(skip_s)
-    plan.close(qkv_s)
-    plan.leave(skip_s)
-    plan.close(skip_s)
     keep.wait()
     for w in range(7):
         plan.finish(w)
@@ -1421,8 +1582,8 @@
         near, away = 0.0, 0.0
         for at in range(2):
             part = normed_grad[rows_b, at * width : (at + 1) * width]
-            near = near + exact_restore(order_skip[at], part[:, : width // 2])
-            away = away + exact_restore(order_skip[at], part[:, width // 2 :])
+            near = near + restore_order(order_skip[at], part[:, : width // 2])
+            away = away + restore_order(order_skip[at], part[:, width // 2 :])
         left = latent[rows_b, :].astype(f32)
         right = skip[rows_b, :].astype(f32)
         left_grad = jnp.where(upper_half, away, near)
@@ -1803,7 +1964,7 @@
 def softmax_of(scores):
     largest = jnp.max(scores, axis=1, keepdims=True)
     raised = jnp.exp(scores - largest)
-    return raised / jnp.sum(raised, axis=1, keepdims=True), largest
+    return raised * (1.0 / jnp.sum(raised, axis=1, keepdims=True)), largest
 
 
 def attention_body(batch, masked, turned, sources, scaling, *refs):
@@ -1937,6 +2098,10 @@
     spare = -value.shape[-1] % size
     value = jnp.pad(value, [(0, 0)] * (value.ndim - 1) + [(0, spare)])
     return value.reshape(*value.shape[:-1], -1, 128)
+
+
+def restore_order(matrix, value):
+    return dot_right_t(value.astype(bf16), matrix)
 
 
 def exact_restore(matrix, value):
@@ -2349,15 +2514,16 @@
     count = links.count
 
     positions = core * tokens + jnp.arange(tokens)
-    feature = jnp.arange(width) % HD
+    feature = jnp.arange(HD)
     freqs = 10000.0 ** (-(feature % (HD // 4)).astype(f32) / (HD // 4))
     place = jnp.where(
         feature[None, :] < HD // 2, (positions // GRID_W)[:, None], (positions % GRID_W)[:, None]
     )
     angles = place.astype(f32) * freqs[None, :]
     former = (feature % (HD // 2) < HD // 4)[None, :]
-    cosine = jnp.cos(angles)
-    sine = jnp.where(former, -jnp.sin(angles), jnp.sin(angles))
+    cosine = jnp.tile(jnp.cos(angles), (1, HEADS))
+    sine = jnp.tile(jnp.where(former, -jnp.sin(angles), jnp.sin(angles)), (1, HEADS))
+    former = jnp.tile(former, (1, HEADS))
     tables = [(cosine, None), (sine, None), (former.astype(f32), None)]
     head_at = jnp.arange(width)[:, None] // HD == jnp.arange(128)[None, :]
     head_at = (head_at.astype(bf16), None)
@@ -2427,6 +2593,15 @@
     def shaped(*shape, dtype=f32):
         return jax.ShapeDtypeStruct(shape, dtype)
 
+    down_in = out_grad.reshape(rows, width)
+    cut = shards[6].shape[1]
+    out_halves = jnp.stack(
+        [down_in[:, :cut], jnp.pad(down_in[:, cut:], ((0, 0), (0, 2 * cut - width)))]
+    )
+    up_shape, down_shape = shards[5].shape, shards[6].shape
+    whole_down, whole_up = [shaped(4, 4, *shape, dtype=bf16) for shape in (down_shape, up_shape)]
+    tile = 384
+
     flat, flat_low = shaped(rows, width), shaped(rows, width, dtype=bf16)
     double_low = shaped(rows, 2 * width, dtype=bf16)
     inner = mlp_down.shape[0] * 16
@@ -2436,13 +2611,13 @@
         skip_gain_all[None, :],
         gains,
         shift,
-        order,
-        order_skip,
-        head_at,
-        *table_arrays,
-        text_ordered,
+        out_halves,
         valid,
     ]
+    loaded = [order, order_skip, head_at, *table_arrays, text_ordered]
+
+    def like(array):
+        return pltpu.VMEM(array.shape, array.dtype)
     saved = [
         shaped(2, 2, rows, width // 2, dtype=bf16),
         flat,
@@ -2485,59 +2660,72 @@
         activated,
         self_peak,
         cross_peak,
+        sums_down,
+        _,
     ) = pl.pallas_call(
         functools.partial(forward_body, batch, scaling),
-        out_shape=[shaped(2, 4, 4, *shard.shape, dtype=bf16) for shard in shards] + saved,
-        in_specs=[IN_VMEM] * len(given) + [ANYWHERE] * 7,
-        out_specs=[ANYWHERE] * 7 + [IN_VMEM] * len(saved),
+        out_shape=[
+            *[shaped(2, 4, 4, *shard.shape, dtype=bf16) for shard in shards],
+            *saved,
+            whole_down,
+            whole_down,
+        ],
+        in_specs=[IN_VMEM] * len(given) + [ANYWHERE] * 14,
+        out_specs=[ANYWHERE] * (9 + len(saved)),
         scratch_shapes=[
+            *[like(array) for array in saved],
+            *[like(array) for array in loaded],
             pltpu.VMEM((rows, width), f32),
             pltpu.VMEM((rows, width), bf16),
             pltpu.VMEM((3, 4, 4, block, 512), bf16),
+            pltpu.VMEM((2, *down_shape), bf16),
+            pltpu.VMEM((2, *down_shape), bf16),
             pltpu.SemaphoreType.DMA((3,)),
-            pltpu.SemaphoreType.DMA((7, 10)),
-            pltpu.SemaphoreType.DMA((7, 10)),
-            pltpu.SemaphoreType.DMA((7,)),
+            pltpu.SemaphoreType.DMA((8, 10)),
+            pltpu.SemaphoreType.DMA((8, 10)),
+            pltpu.SemaphoreType.DMA((8,)),
             pltpu.SemaphoreType.DMA,
             pltpu.SemaphoreType.DMA,
+            pltpu.SemaphoreType.DMA((1, 16)),
+            pltpu.SemaphoreType.DMA((1, 16)),
+            pltpu.SemaphoreType.DMA((4,)),
+            pltpu.SemaphoreType.DMA((7,)),
+            pltpu.SemaphoreType.DMA((19,)),
         ],
         compiler_params=pltpu.CompilerParams(
             collective_id=7, has_side_effects=True, vmem_limit_bytes=62 * 2**20
         ),
-    )(*given, *shards)
-    down_in = out_grad.reshape(rows, width)
-    cut = shards[6].shape[1]
-    out_halves = jnp.stack(
-        [down_in[:, :cut], jnp.pad(down_in[:, cut:], ((0, 0), (0, 2 * cut - width)))]
-    )
-    up_shape, down_shape = shards[5].shape, shards[6].shape
-    whole = [shaped(4, 4, *shape, dtype=bf16) for shape in (down_shape, up_shape)]
-    tile = 384
-    block_out, cross_grad, gain_third, *rest = pl.pallas_call(
+    )(*given, *loaded, *shards)
+    block_out, cross_grad, gain_third, sums_up, _, half_down = pl.pallas_call(
         functools.partial(mlp_back_body, batch),
-        out_shape=[flat_low, flat, shaped(8, width), *whole, *whole],
-        in_specs=[IN_VMEM] * 7 + [ANYWHERE] * 2,
-        out_specs=[IN_VMEM] * 3 + [ANYWHERE] * 4,
+        out_shape=[
+            flat_low, flat, shaped(8, width), whole_up, whole_up,
+            shaped(2, 4, *down_shape, dtype=bf16),
+        ],
+        in_specs=[IN_VMEM] * 7 + [ANYWHERE] * 3,
+        out_specs=[IN_VMEM] * 3 + [ANYWHERE] * 3,
         scratch_shapes=[
             pltpu.VMEM((2, rows, inner // 2), bf16),
             pltpu.VMEM((width, rows), bf16),
             pltpu.VMEM((2, rows, cut), f32),
             pltpu.VMEM((3, 2, *down_shape), bf16),
             pltpu.VMEM((3, 4, 4, block, 512), bf16),
-            pltpu.VMEM((2, *down_shape), bf16),
-            pltpu.VMEM((2, *down_shape), bf16),
             pltpu.VMEM((2, 4, 4, block, tile), bf16),
             pltpu.VMEM((2, 4, 4, block, tile), bf16),
             pltpu.SemaphoreType.DMA((3,)),
-            pltpu.SemaphoreType.DMA((2, 16)),
-            pltpu.SemaphoreType.DMA((2, 16)),
+            pltpu.SemaphoreType.DMA((1, 16)),
+            pltpu.SemaphoreType.DMA((1, 16)),
             pltpu.SemaphoreType.DMA((4,)),
+            pltpu.SemaphoreType.DMA((1, 8)),
+            pltpu.SemaphoreType.DMA((1, 8)),
         ],
         compiler_params=pltpu.CompilerParams(
             collective_id=8, has_side_effects=True, vmem_limit_bytes=60 * 2**20
         ),
-    )(out_halves, activated, upper, mlp_in, after_cross, order, gains, gathered[5], gathered[6])
-    sums_down, sums_up = rest[0], rest[1]
+    )(
+        out_halves, activated, upper, mlp_in, after_cross, order, gains,
+        gathered[5], gathered[6], sums_down,
+    )
 
     text_half = text_rows // 2
     text_mine = lax.dynamic_slice_in_dim(
@@ -2548,20 +2736,22 @@
         *[shaped(2, *shape) for shape in parts],
         *[shaped(4, 4, *shape, dtype=bf16) for shape in parts[2:]],
         *[shaped(4, 4, *shape, dtype=bf16) for shape in parts[2:]],
-        *[shaped(2, 4, *shape, dtype=bf16) for shape in parts],
+        *[shaped(2, 4, *shape, dtype=bf16) for shape in parts[1:]],
         *[shaped(4, *shape, dtype=bf16) for shape in parts],
         *[shaped(4, *shape, dtype=bf16) for shape in parts],
         *[shaped(3, *shape, dtype=bf16) for shape in parts],
         *[shaped(3, *shape, dtype=bf16) for shape in parts],
     ]
-    placed = [
+    placed = [gains, valid]
+    loaded = [
         cross_cat, attn_cat, cross_in, attn_in, text_mine, after_self, hidden, normed,
-        gains, order, head_at, *table_arrays, valid,
+        order, head_at, *table_arrays,
     ]
     apart = [
+        *loaded,
         *gathered[:5],
         cross_keyval_all, cq_proj, ckey_mine, qkv_proj, keyval_here, keyval_there, cross_grad,
-        sums_down, sums_up,
+        sums_down, sums_up, half_down,
     ]
     small_outs = [shaped(rows, text_width), shaped(8, width), shaped(8, width)]
     text_grad, gain_grads, shift_grad, normed_grad, *rest = pl.pallas_call(
@@ -2578,25 +2768,26 @@
             pltpu.VMEM((rows, 2 * width), f32),
             pltpu.VMEM((2, width, rows), bf16),
             pltpu.VMEM((2, rows, shards[1].shape[1]), bf16),
+            *[like(array) for array in loaded],
             pltpu.VMEM((3, 4, 4, block, tile), bf16),
             pltpu.VMEM((2, 4, 4, block, tile), bf16),
             pltpu.VMEM((2, 4, 4, block, tile), bf16),
-            pltpu.VMEM((9, block, 1536), bf16),
-            pltpu.VMEM((9, down_shape[0], tile), bf16),
-            pltpu.VMEM((block, 1536), f32),
-            pltpu.VMEM((down_shape[0], tile), f32),
+            pltpu.VMEM((2, 9, block, 768), bf16),
+            pltpu.VMEM((2, 9, down_shape[0], 128), bf16),
+            pltpu.VMEM((2, block, 768), f32),
+            pltpu.VMEM((2, down_shape[0], 128), f32),
             pltpu.VMEM((2, rows, 2 * width), bf16),
             pltpu.SemaphoreType.DMA((3,)),
-            pltpu.SemaphoreType.DMA((4,)),
+            pltpu.SemaphoreType.DMA((17,)),
             pltpu.SemaphoreType.DMA((5, 8)),
             pltpu.SemaphoreType.DMA((5, 8)),
             pltpu.SemaphoreType.DMA((4,)),
             pltpu.SemaphoreType.DMA((2,)),
             pltpu.SemaphoreType.DMA((2,)),
-            pltpu.SemaphoreType.DMA((7, 8)),
-            pltpu.SemaphoreType.DMA((7, 8)),
-            pltpu.SemaphoreType.DMA((9,)),
-            pltpu.SemaphoreType.DMA((4,)),
+            pltpu.SemaphoreType.DMA((7, 12)),
+            pltpu.SemaphoreType.DMA((7, 12)),
+            pltpu.SemaphoreType.DMA((2, 9)),
+            pltpu.SemaphoreType.DMA((2, 4)),
         ],
         compiler_params=pltpu.CompilerParams(
             collective_id=9, has_side_effects=True, vmem_limit_bytes=62 * 2**20
@@ -2613,7 +2804,7 @@
     skip_gain_grad = skip_gain_grad[0]
     gain_first, gain_second, gain_third = gain_grads[0], gain_grads[1], gain_third[0]
     shift_grad = shift_grad[:batch]
-    grad_text = exact_restore(order_text, text_grad).reshape(batch, text_half, text_width)
+    grad_text = restore_order(order_text, text_grad).reshape(batch, text_half, text_width)
 
     def wide_of(part):
         return jnp.concatenate([part[0], part[1]], axis=1)

time: 1010 us -> 923 us (0.914)
  Pallas kernels: 926 us -> 837 us
    pallas_call x1, Pallas kernels: 385 us -> 354 us  [local_sixteen(): pl.pallas_call(functools.partial(rest_back_body, batch, scaling), out_sha...]
    pallas_call x1, Pallas kernels: 96.2 us -> 65.3 us  [local_sixteen(): pl.pallas_call(functools.partial(mlp_back_body, batch), out_shape=[flat_l...]
    pallas_call x1, Pallas kernels: 380 us -> 362 us  [local_sixteen(): pl.pallas_call(functools.partial(forward_body, batch, scaling), out_shape...]
where the time goes in v4:
time: 923 us; the launch traced here: 910 us
  Pallas kernels  837 us (91%)
  local copies, waits for them, and re-layouts  35.9 us (4%)
  other arithmetic  28.1 us (3%)
    pallas_call x1, Pallas kernels, local_sixteen(): pl.pallas_call(functools.partial(forward_body, batch, scaling), out_shape...  362 us
    pallas_call x1, Pallas kernels, local_sixteen(): pl.pallas_call(functools.partial(rest_back_body, batch, scaling), out_sha...  354 us
    pallas_call x1, Pallas kernels, local_sixteen(): pl.pallas_call(functools.partial(mlp_back_body, batch), out_shape=[flat_l...  65.3 us
    pallas_call x4, Pallas kernels, trade(): pl.pallas_call(functools.partial(trade_body, count, same), out_shape=jax....  44.8 us
  transfers between devices with their start and end apart: 1, of which 0 were waited for; matrix products, arithmetic and copies ran while one was open for 1% of the time, Pallas kernels for 0%

profile of v4, /device:TPU:0, one launch (start us, length us, event | category | flops | bytes accessed | tf_op | source)
XLA Modules:
  0.0 910.0 jit_solution(15436970119696363356)
XLA Ops:
  3.8 12.0 %shard_map.329 = bf16[16,32,128]{2,1,0:T(8,128)(2,1)} custom-call(bf16[32,128]{1,0:T(8,128)(2,1)} %pad_bitcast_fusion.2.source), custom_call_target="tpu_custom_call" | custom-call | tf_op jit(solution)/shard_map/pallas_call | solution.py:95
  15.8 1.0 copy.58
  17.0 1.9 fusion.40
  24.0 10.8 %shard_map.330 = f32[16,24,128]{2,1,0:T(8,128)} custom-call(f32[16,24,128]{2,1,0:T(8,128)} %bitcast.97), custom_call_target="tpu_custom_call" | custom-call | tf_op jit(solution)/shard_map/pallas_call | solution.py:95
  34.7 1.0 reduce_sum.18
  37.7 1.0 slice.246
  38.7 1.0 fusion.7.refs_9_.refs_11_
  39.7 1.1 slice_bitcast_fusion.8
  43.0 1.1 copy.42.refs_11_.refs_13_
  44.1 1.1 copy.41.refs_10_.refs_12_
  47.0 3.6 fusion.refs_7_.refs_5_.refs_10_
  51.6 2.3 fusion.5
  54.0 3.0 add_convert_fusion.refs_8_.order_skip
  58.7 361.8 %shard_map.331 = (bf16[2,4,4,88,1408]{4,3,2,1,0:T(8,128)(2,1)}, bf16[2,4,4,88,2176]{4,3,2,1,0:T(8,128)(2,1)}, bf16[2,4,4,88,1408]{4,3,2,1,0:T(8,128)(2,1)}, bf16...) custom-call(bf16[256,1408]{1,0:T(8,128)(2,1)} %bitcast.85, ...), custom_call_target="tpu_custom_call" | custom-call | tf_op jit(solution)/shard_map/pallas_call | solution.py:2665
  422.3 65.3 %shard_map.332 = (bf16[256,1408]{1,0:T(8,128)(2,1)}, f32[256,1408]{1,0:T(8,128)}, f32[8,1408]{1,0:T(8,128)}, bf16[4,4,88,3072]{3,2,1,0:T(8,128)(2,1)}, bf16[4,4,...) custom-call(bf16[2,256,768]{2,1,0:T(8,128)(2,1)} %pad_maximum_fusion.3.refs_5_.refs_0_, ...), custom_call_target="tpu_custom_call" | custom-call | tf_op jit(solution)/shard_map/pallas_call | solution.py:2699
  489.2 354.1 %shard_map.333 = (f32[256,1024]{1,0:T(8,128)}, f32[8,1408]{1,0:T(8,128)}, f32[8,1408]{1,0:T(8,128)}, f32[256,2816]{1,0:T(8,128)}, f32[2,384,768]{2,1,0:T(8,128)}...) custom-call(f32[3,1408]{1,0:T(4,128)} %reshape.583.refs_3_.refs_6_.r, ...), custom_call_target="tpu_custom_call" | custom-call | tf_op jit(solution)/shard_map/pallas_call | solution.py:2757
  843.3 11.5 %shard_map.334 = (f32[2,256,1408]{2,1,0:T(8,128)}, f32[8,2816]{1,0:T(8,128)}) custom-call(f32[256,2816]{1,0:T(8,128)} %get-tuple-element.94.normed_grad, bf16[256,1408]{1,0:T(8,128)(2,1)} %bitcast.86, bf16[256,1408]{1,0:T(8,128)(2,1)} %bitcast.88, f32[1,2816]{1,0:T(1,128)} %reshape.582.refs_2_.skip_gain, bf16[2,1408,704]{2,1,0:T(8,128)(2,1)} %add_convert_fusion.refs_8_.order_skip), custom_call_target="tpu_custom_call" | custom-call | tf_op jit(solution)/shard_map/pallas_call | solution.py:2797
  858.4 1.7 copy-done.3
  860.0 1.8 fusion.39
  861.9 1.1 copy-done.12
  863.0 1.0 slice_bitcast_fusion.6
  864.0 2.0 fusion.1
  866.1 1.5 copy-done.5
  868.7 1.5 pad_maximum_fusion.1
  870.2 1.5 pad_maximum_fusion
  871.7 1.2 pad_maximum_fusion.2
  874.4 12.6 %shard_map.335 = f32[16,24,128]{2,1,0:T(8,128)} custom-call(f32[24,128]{1,0:T(8,128)} %fusion.13.source), custom_call_target="tpu_custom_call" | custom-call | tf_op jit(solution)/shard_map/pallas_call | solution.py:95
  887.0 1.0 copy.57
  889.1 9.4 %shard_map.336 = f32[16,8,128]{2,1,0:T(8,128)} custom-call(f32[16,8,128]{2,1,0:T(8,128)} %bitcast.108), custom_call_target="tpu_custom_call" | custom-call | tf_op jit(solution)/shard_map/pallas_call | solution.py:95
  900.2 1.8 fusion.23
  905.5 1.0 multiply_convert_fusion
  907.3 2.2 copy.68
  (185 shorter events, 33.4 us)
Async XLA Ops:
  0.7 50.9 %copy-start = (bf16[2,256,1024]{2,1,0:T(8,128)(2,1)S(1)}, bf16[2,256,1024]{2,1,0:T(8,128)(2,1)}, u32[]{:S(2)}) copy-start(bf16[2,256,1024]{2,1,0:T(8,128)(2,1)} %param.21) | copy-start | bytes 3145732
  0.7 18.2 %copy-start.29 = (s32[2]{0:T(128)S(1)}, s32[2]{0:T(128)}, u32[]{:S(2)}) copy-start(s32[2]{0:T(128)} %param.22) | copy-start | bytes 28
  0.7 22.2 %copy-start.13 = (bf16[88,1408]{1,0:T(8,128)(2,1)S(1)}, bf16[88,1408]{1,0:T(8,128)(2,1)}, u32[]{:S(2)}) copy-start(bf16[88,1408]{1,0:T(8,128)(2,1)} %param.27) | copy-start | bytes 743428
  16.9 19.4 %copy-start.11 = (bf16[88,1408]{1,0:T(8,128)(2,1)S(1)}, bf16[88,1408]{1,0:T(8,128)(2,1)}, u32[]{:S(2)}) copy-start(bf16[88,1408]{1,0:T(8,128)(2,1)} %param.30) | copy-start | bytes 743428
  16.9 19.4 %slice-start.3 = ((bf16[88,1408]{1,0:T(8,128)(2,1)}), bf16[88,640]{1,0:T(8,128)(2,1)S(1)}, s32[]{:S(2)}) async-start(bf16[88,1408]{1,0:T(8,128)(2,1)} %param.30), calls=%async_computation.3 | async-start | bytes 225280 | tf_op jit(solution)/shard_map/slice | solution.py:2549
  16.9 20.1 %copy-start.9 = (bf16[64,2816]{1,0:T(8,128)(2,1)S(1)}, bf16[64,2816]{1,0:T(8,128)(2,1)}, u32[]{:S(2)}) copy-start(bf16[64,2816]{1,0:T(8,128)(2,1)} %param.31) | copy-start | bytes 1081348
  36.3 4.5 copy-start.7
  36.3 4.5 slice-start.2
  39.7 2.1 copy-start.10
  47.0 4.6 copy-start.26
  53.9 3.1 copy-start.20
  53.9 3.1 copy-start.21
  53.9 3.1 copy-start.22
  53.9 4.0 slice-start
  53.9 4.0 slice-start.1
  53.9 3.9 copy-start.15
  53.9 3.9 copy-start.16
  422.3 66.1 %copy-start.4 = (bf16[1024,512]{0,1:T(8,128)(2,1)S(1)}, bf16[1024,512]{0,1:T(8,128)(2,1)}, u32[]{:S(2)}) copy-start(bf16[1024,512]{0,1:T(8,128)(2,1)} %fusion.5) | copy-start | bytes 3145732
  843.3 14.5 %copy-start.24 = (f32[9888]{0:T(1024)S(1)}, f32[9888]{0:T(1024)}, u32[]{:S(2)}) copy-start(f32[9888]{0:T(1024)} %custom-call) | copy-start | bytes 118660
  843.3 14.8 %copy-start.8 = (f32[2,88,2176]{2,1,0:T(8,128)S(1)}, f32[2,88,2176]{2,1,0:T(8,128)}, u32[]{:S(2)}) copy-start(f32[2,88,2176]{2,1,0:T(8,128)} %get-tuple-element.104) | copy-start | bytes 4595716
  857.9 15.8 %collective-permute-start = (f32[9888]{0:T(1024)S(1)}, f32[9888]{0:T(1024)S(1)}, u32[]{:S(2)}, u32[]{:S(2)}) collective-permute-start(f32[9888]{0:T(1024)S(1)} %constant_dynamic-update-slice_fusion), channel_id=1, source_target_pairs={{0,1},{1,0},{2,3},{3,2},{4,5},{5,4},{6,7},{7,6},{8,9},{9,8},{10,11... | collective-permute-start | bytes 118664 | tf_op jit(solution)/shard_map/ppermute | solution.py:1630
  858.2 1.8 copy-start.3
  860.0 1.8 copy-start.18
  861.8 2.2 copy-start.30
  864.0 2.0 copy-start.6
  871.7 16.4 %copy-start.14 = (bf16[88,1408]{1,0:T(8,128)(2,1)S(1)}, bf16[88,1408]{1,0:T(8,128)(2,1)}, u32[]{:S(2)}) copy-start(bf16[88,1408]{1,0:T(8,128)(2,1)} %param.27) | copy-start | bytes 743428
  872.9 29.2 %copy-start.27 = (f32[2,16]{1,0:T(2,128)S(1)}, f32[2,16]{1,0:T(2,128)}, u32[]{:S(2)}) copy-start(f32[2,16]{1,0:T(2,128)} %param.35) | copy-start | bytes 388
  872.9 30.5 %copy-start.25 = (bf16[2,1408]{1,0:T(2,128)(2,1)S(1)}, bf16[2,1408]{1,0:T(2,128)(2,1)}, u32[]{:S(2)}) copy-start(bf16[2,1408]{1,0:T(2,128)(2,1)} %param.20) | copy-start | bytes 16900
  873.7 31.7 %copy-start.2 = (bf16[88,4224]{1,0:T(8,128)(2,1)S(1)}, bf16[88,4224]{1,0:T(8,128)(2,1)}, u32[]{:S(2)}) copy-start(bf16[88,4224]{1,0:T(8,128)(2,1)} %param.28) | copy-start | bytes 2230276
  888.3 18.2 %copy-start.17 = (bf16[256,1408]{1,0:T(8,128)(2,1)S(1)}, bf16[256,1408]{1,0:T(8,128)(2,1)}, u32[]{:S(2)}) copy-start(bf16[256,1408]{1,0:T(8,128)(2,1)} %get-tuple-element.72) | copy-start | bytes 2162692
  902.1 5.3 copy-start.28
  905.5 4.1 copy-start.1
  (4 other events, 5.4 us)

commit v5 on v4

--- a/solution.py
+++ b/solution.py
@@ -702,6 +702,9 @@
     plan.spread(keyval_w)
     plan.begin(down_w)
     plan.close(pair_w)
+    plan.cross(query_w)
+    plan.spread(up_w)
+    plan.low_spread(last_w)
     exchange.wait()
     save(5)
 
@@ -730,9 +733,6 @@
 
     attend([keyval_here, keyval_there], self_peak, attn_cat, False)
     save(6, 17)
-    plan.cross(query_w)
-    plan.spread(up_w)
-    plan.low_spread(last_w)
     plan.ready(pair_w)
     pair_tiles = tiles_of(width, 512)
 
@@ -1408,7 +1408,7 @@
     attention_back([keyval], (), True, lambda value, rows_b: split_lanes(value, rows_b, width))
     keyval[pl.ds(0, rows), :] = total[1 - core].astype(bf16)
     exchange(0).start()
-    plan.leave(down)
+    plan.middle(up)
     query_tiles = tiles_of(768, 384)
     back_through(
         query_w,
@@ -1441,6 +1441,7 @@
         lambda at, start, extent: halves[at, :, pl.ds(start, extent)],
     )
     plan.begin(pair_s)
+    plan.leave(down)
     turned[0] = jnp.transpose(cross_in[...])
     twin_product(
         0,
@@ -1450,7 +1451,7 @@
         lambda at, start, extent: halves[at, :, pl.ds(width + start, extent)],
     )
     plan.begin(query_s)
-    plan.middle(up)
+    plan.leave(up)
     exchange(0).wait()
 
     def text_part(key_grad, value_grad, rows_b):
@@ -1458,6 +1459,7 @@
         landed[0, rows_b, last_lanes] = value_grad
 
     keys_back(0, core, (), text_part)
+    plan.middle(pair_s)
 
     load(
         (qkv, proj),
@@ -1472,8 +1474,8 @@
     attention_back(sources, tables, False, query_part)
     keyval[pl.ds(0, rows), :] = total[1].astype(bf16)
     exchange(1).start()
-    plan.middle(pair_s)
     plan.middle(query_s)
+    plan.leave(pair_s)
     exchange(1).wait()
 
     def key_part(key_grad, value_grad, rows_b):
@@ -1504,7 +1506,7 @@
         halves[0, rows_b, first_lanes] = (grad[rows_b, :] + value).astype(bf16)
 
     each(hidden_part)
-    plan.leave(up)
+    plan.leave(query_s)
 
     for at in range(2):
         for part in range(2):
@@ -1519,8 +1521,6 @@
         lambda at, start, extent: halves[0, :, pl.ds(start, extent)],
     )
     plan.begin(skip_s)
-    plan.leave(pair_s)
-    plan.leave(query_s)
 
     text_width = text.shape[1]
     turned[0, pl.ds(0, text_width), :] = jnp.transpose(text[...])
@@ -1555,12 +1555,12 @@
     stream(skip_w, skip_tiles, buffer, semaphore, skip_body)
     keep = pltpu.make_async_copy(total.at[0], normed_grad, loads.at[0])
     keep.start()
-    plan.close(down)
     plan.middle(skip_s)
     plan.leave(qkv_s)
     plan.middle(keyval_s)
+    plan.close(down)
+    plan.leave(skip_s)
     plan.close(up)
-    plan.leave(skip_s)
     plan.leave(keyval_s)
     plan.close(pair_s)
     plan.close(query_s)

time: 923 us -> 910 us (0.986)
  Pallas kernels: 837 us -> 825 us
where the time goes in v5:
time: 910 us; the launch traced here: 897 us
  Pallas kernels  825 us (91%)
  local copies, waits for them, and re-layouts  35.9 us (4%)
  other arithmetic  28.1 us (3%)
    pallas_call x1, Pallas kernels, local_sixteen(): pl.pallas_call(functools.partial(forward_body, batch, scaling), out_shape...  355 us
    pallas_call x1, Pallas kernels, local_sixteen(): pl.pallas_call(functools.partial(rest_back_body, batch, scaling), out_sha...  351 us
    pallas_call x1, Pallas kernels, local_sixteen(): pl.pallas_call(functools.partial(mlp_back_body, batch), out_shape=[flat_l...  62.1 us
    pallas_call x4, Pallas kernels, trade(): pl.pallas_call(functools.partial(trade_body, count, same), out_shape=jax....  44.6 us
  transfers between devices with their start and end apart: 1, of which 0 were waited for; matrix products, arithmetic and copies ran while one was open for 1% of the time, Pallas kernels for 0%

profile of v5, /device:TPU:0, one launch (start us, length us, event | category | flops | bytes accessed | tf_op | source)
XLA Modules:
  0.0 897.1 jit_solution(16930696236939194816)
XLA Ops:
  3.8 12.0 %shard_map.329 = bf16[16,32,128]{2,1,0:T(8,128)(2,1)} custom-call(bf16[32,128]{1,0:T(8,128)(2,1)} %pad_bitcast_fusion.2.source), custom_call_target="tpu_custom_call" | custom-call | tf_op jit(solution)/shard_map/pallas_call | solution.py:95
  15.8 1.0 copy.58
  17.0 1.9 fusion.40
  24.0 10.8 %shard_map.330 = f32[16,24,128]{2,1,0:T(8,128)} custom-call(f32[16,24,128]{2,1,0:T(8,128)} %bitcast.97), custom_call_target="tpu_custom_call" | custom-call | tf_op jit(solution)/shard_map/pallas_call | solution.py:95
  34.7 1.0 reduce_sum.18
  37.7 1.0 slice.246
  38.7 1.0 fusion.7.refs_9_.refs_11_
  39.7 1.1 slice_bitcast_fusion.8
  43.0 1.1 copy.42.refs_11_.refs_13_
  44.1 1.1 copy.41.refs_10_.refs_12_
  47.0 3.6 fusion.refs_7_.refs_5_.refs_10_
  51.6 2.3 fusion.5
  54.0 3.0 add_convert_fusion.refs_8_.order_skip
  58.7 355.3 %shard_map.331 = (bf16[2,4,4,88,1408]{4,3,2,1,0:T(8,128)(2,1)}, bf16[2,4,4,88,2176]{4,3,2,1,0:T(8,128)(2,1)}, bf16[2,4,4,88,1408]{4,3,2,1,0:T(8,128)(2,1)}, bf16...) custom-call(bf16[256,1408]{1,0:T(8,128)(2,1)} %bitcast.85, ...), custom_call_target="tpu_custom_call" | custom-call | tf_op jit(solution)/shard_map/pallas_call | solution.py:2665
  415.8 62.1 %shard_map.332 = (bf16[256,1408]{1,0:T(8,128)(2,1)}, f32[256,1408]{1,0:T(8,128)}, f32[8,1408]{1,0:T(8,128)}, bf16[4,4,88,3072]{3,2,1,0:T(8,128)(2,1)}, bf16[4,4,...) custom-call(bf16[2,256,768]{2,1,0:T(8,128)(2,1)} %pad_maximum_fusion.3.refs_5_.refs_0_, ...), custom_call_target="tpu_custom_call" | custom-call | tf_op jit(solution)/shard_map/pallas_call | solution.py:2699
  479.5 351.1 %shard_map.333 = (f32[256,1024]{1,0:T(8,128)}, f32[8,1408]{1,0:T(8,128)}, f32[8,1408]{1,0:T(8,128)}, f32[256,2816]{1,0:T(8,128)}, f32[2,384,768]{2,1,0:T(8,128)}...) custom-call(f32[3,1408]{1,0:T(4,128)} %reshape.583.refs_3_.refs_6_.r, ...), custom_call_target="tpu_custom_call" | custom-call | tf_op jit(solution)/shard_map/pallas_call | solution.py:2757
  830.6 11.5 %shard_map.334 = (f32[2,256,1408]{2,1,0:T(8,128)}, f32[8,2816]{1,0:T(8,128)}) custom-call(f32[256,2816]{1,0:T(8,128)} %get-tuple-element.94.normed_grad, bf16[256,1408]{1,0:T(8,128)(2,1)} %bitcast.86, bf16[256,1408]{1,0:T(8,128)(2,1)} %bitcast.88, f32[1,2816]{1,0:T(1,128)} %reshape.582.refs_2_.skip_gain, bf16[2,1408,704]{2,1,0:T(8,128)(2,1)} %add_convert_fusion.refs_8_.order_skip), custom_call_target="tpu_custom_call" | custom-call | tf_op jit(solution)/shard_map/pallas_call | solution.py:2797
  845.6 1.7 copy-done.3
  847.3 1.8 fusion.39
  849.2 1.1 copy-done.12
  850.3 1.0 slice_bitcast_fusion.6
  851.3 2.0 fusion.1
  853.4 1.5 copy-done.5
  856.0 1.5 pad_maximum_fusion.1
  857.5 1.5 pad_maximum_fusion
  859.0 1.2 pad_maximum_fusion.2
  861.6 12.4 %shard_map.335 = f32[16,24,128]{2,1,0:T(8,128)} custom-call(f32[24,128]{1,0:T(8,128)} %fusion.13.source), custom_call_target="tpu_custom_call" | custom-call | tf_op jit(solution)/shard_map/pallas_call | solution.py:95
  874.1 1.0 copy.57
  876.3 9.4 %shard_map.336 = f32[16,8,128]{2,1,0:T(8,128)} custom-call(f32[16,8,128]{2,1,0:T(8,128)} %bitcast.108), custom_call_target="tpu_custom_call" | custom-call | tf_op jit(solution)/shard_map/pallas_call | solution.py:95
  887.3 1.8 fusion.23
  892.6 1.0 multiply_convert_fusion
  894.5 2.2 copy.68
  (185 shorter events, 33.4 us)
Async XLA Ops:
  0.7 50.9 %copy-start = (bf16[2,256,1024]{2,1,0:T(8,128)(2,1)S(1)}, bf16[2,256,1024]{2,1,0:T(8,128)(2,1)}, u32[]{:S(2)}) copy-start(bf16[2,256,1024]{2,1,0:T(8,128)(2,1)} %param.21) | copy-start | bytes 3145732
  0.7 18.2 %copy-start.29 = (s32[2]{0:T(128)S(1)}, s32[2]{0:T(128)}, u32[]{:S(2)}) copy-start(s32[2]{0:T(128)} %param.22) | copy-start | bytes 28
  0.7 22.2 %copy-start.13 = (bf16[88,1408]{1,0:T(8,128)(2,1)S(1)}, bf16[88,1408]{1,0:T(8,128)(2,1)}, u32[]{:S(2)}) copy-start(bf16[88,1408]{1,0:T(8,128)(2,1)} %param.27) | copy-start | bytes 743428
  16.9 19.4 %copy-start.11 = (bf16[88,1408]{1,0:T(8,128)(2,1)S(1)}, bf16[88,1408]{1,0:T(8,128)(2,1)}, u32[]{:S(2)}) copy-start(bf16[88,1408]{1,0:T(8,128)(2,1)} %param.30) | copy-start | bytes 743428
  16.9 19.4 %slice-start.3 = ((bf16[88,1408]{1,0:T(8,128)(2,1)}), bf16[88,640]{1,0:T(8,128)(2,1)S(1)}, s32[]{:S(2)}) async-start(bf16[88,1408]{1,0:T(8,128)(2,1)} %param.30), calls=%async_computation.3 | async-start | bytes 225280 | tf_op jit(solution)/shard_map/slice | solution.py:2549
  16.9 20.1 %copy-start.9 = (bf16[64,2816]{1,0:T(8,128)(2,1)S(1)}, bf16[64,2816]{1,0:T(8,128)(2,1)}, u32[]{:S(2)}) copy-start(bf16[64,2816]{1,0:T(8,128)(2,1)} %param.31) | copy-start | bytes 1081348
  36.3 4.5 copy-start.7
  36.3 4.5 slice-start.2
  39.7 2.1 copy-start.10
  47.0 4.6 copy-start.26
  53.9 3.1 copy-start.20
  53.9 3.1 copy-start.21
  53.9 3.1 copy-start.22
  53.9 4.0 slice-start
  53.9 4.0 slice-start.1
  53.9 3.9 copy-start.15
  53.9 3.9 copy-start.16
  415.8 62.9 %copy-start.4 = (bf16[1024,512]{0,1:T(8,128)(2,1)S(1)}, bf16[1024,512]{0,1:T(8,128)(2,1)}, u32[]{:S(2)}) copy-start(bf16[1024,512]{0,1:T(8,128)(2,1)} %fusion.5) | copy-start | bytes 3145732
  830.6 14.5 %copy-start.24 = (f32[9888]{0:T(1024)S(1)}, f32[9888]{0:T(1024)}, u32[]{:S(2)}) copy-start(f32[9888]{0:T(1024)} %custom-call) | copy-start | bytes 118660
  830.6 14.8 %copy-start.8 = (f32[2,88,2176]{2,1,0:T(8,128)S(1)}, f32[2,88,2176]{2,1,0:T(8,128)}, u32[]{:S(2)}) copy-start(f32[2,88,2176]{2,1,0:T(8,128)} %get-tuple-element.104) | copy-start | bytes 4595716
  845.2 15.8 %collective-permute-start = (f32[9888]{0:T(1024)S(1)}, f32[9888]{0:T(1024)S(1)}, u32[]{:S(2)}, u32[]{:S(2)}) collective-permute-start(f32[9888]{0:T(1024)S(1)} %constant_dynamic-update-slice_fusion), channel_id=1, source_target_pairs={{0,1},{1,0},{2,3},{3,2},{4,5},{5,4},{6,7},{7,6},{8,9},{9,8},{10,11... | collective-permute-start | bytes 118664 | tf_op jit(solution)/shard_map/ppermute | solution.py:1630
  845.5 1.8 copy-start.3
  847.3 1.8 copy-start.18
  849.1 2.2 copy-start.30
  851.3 2.0 copy-start.6
  859.0 16.3 %copy-start.14 = (bf16[88,1408]{1,0:T(8,128)(2,1)S(1)}, bf16[88,1408]{1,0:T(8,128)(2,1)}, u32[]{:S(2)}) copy-start(bf16[88,1408]{1,0:T(8,128)(2,1)} %param.27) | copy-start | bytes 743428
  860.2 29.0 %copy-start.27 = (f32[2,16]{1,0:T(2,128)S(1)}, f32[2,16]{1,0:T(2,128)}, u32[]{:S(2)}) copy-start(f32[2,16]{1,0:T(2,128)} %param.35) | copy-start | bytes 388
  860.2 30.3 %copy-start.25 = (bf16[2,1408]{1,0:T(2,128)(2,1)S(1)}, bf16[2,1408]{1,0:T(2,128)(2,1)}, u32[]{:S(2)}) copy-start(bf16[2,1408]{1,0:T(2,128)(2,1)} %param.20) | copy-start | bytes 16900
  861.0 31.6 %copy-start.2 = (bf16[88,4224]{1,0:T(8,128)(2,1)S(1)}, bf16[88,4224]{1,0:T(8,128)(2,1)}, u32[]{:S(2)}) copy-start(bf16[88,4224]{1,0:T(8,128)(2,1)} %param.28) | copy-start | bytes 2230276
  875.4 18.2 %copy-start.17 = (bf16[256,1408]{1,0:T(8,128)(2,1)S(1)}, bf16[256,1408]{1,0:T(8,128)(2,1)}, u32[]{:S(2)}) copy-start(bf16[256,1408]{1,0:T(8,128)(2,1)} %get-tuple-element.72) | copy-start | bytes 2162692
  889.2 5.3 copy-start.28
  892.6 4.1 copy-start.1
  (4 other events, 5.4 us)
